TPU v7x, 32 devices: a whole 2x2x4 slice. The times are simulated.
32 devices in a mesh: section: 4 (over y, core), dp: 8 (over z, x).
Axes of the slice: x: 2, y: 2, z: 4, core: 2. Of those that a mesh axis runs over, the one named last changes fastest.
Arguments:
- tokens_in: bfloat16 [16, 1024, 768], P('dp', 'section'), may hold values from -6 to 6
- seg_starts: int32 [16, 6], P('dp'), may hold values from 0 to 1023, as said below
- pad_mask: int32 [16, 1024], P('dp'), may hold values from 0 to 1, as said below
- w_qkv: bfloat16 [4, 768, 2304], P('section'), may hold values from -0.21875 to 0.21875
- b_qv: float32 [4, 1536], P('section'), may hold values from -3 to 3
- w_attn_out: bfloat16 [4, 768, 768], P('section'), may hold values from -0.875 to 0.875
- b_attn_out: float32 [4, 768], P('section'), may hold values from -3 to 3
- ln_gain: float32 [4, 2, 768], P('section'), may hold values from 0.5 to 1.5
- ln_bias: float32 [4, 2, 768], P('section'), may hold values from -2 to 2
- w_up: bfloat16 [4, 768, 3072], P('section'), may hold values from -0.21875 to 0.21875
- b_up: float32 [4, 3072], P('section'), may hold values from -3 to 3
- w_down: bfloat16 [4, 3072, 768], P('section'), may hold values from -0.109375 to 0.109375
- b_down: float32 [4, 768], P('section'), may hold values from -3 to 3
- w_proj: bfloat16 [768, 128], P(None, 'section'), may hold values from -0.21875 to 0.21875
- cotangent: bfloat16 [16, 1024, 128], P('dp', None, 'section'), may hold values from -6 to 6
Outputs:
- embedded: bfloat16 [16, 1024, 128], P('dp', None, 'section')
- grad_in: float32 [16, 1024, 768], P('dp', 'section')
- grad_w_qkv: float32 [4, 768, 2304], P('section', 'dp')
- grad_b_qv: float32 [4, 1536], P('section', 'dp')
- grad_w_attn_out: float32 [4, 768, 768], P('section', 'dp')
- grad_b_attn_out: float32 [4, 768], P('section', 'dp')
- grad_ln_gain: float32 [4, 2, 768], P('section', None, 'dp')
- grad_ln_bias: float32 [4, 2, 768], P('section', None, 'dp')
- grad_w_up: float32 [4, 768, 3072], P('section', 'dp')
- grad_b_up: float32 [4, 3072], P('section', 'dp')
- grad_w_down: float32 [4, 3072, 768], P('section', 'dp')
- grad_b_down: float32 [4, 768], P('section', 'dp')
- grad_w_proj: float32 [768, 128], P('dp', 'section')
Inputs may be any that keep to these rules, and one draw needn't show every extreme that they name: `seg_starts`: in each row the 6 starts rise strictly and the first is 0. `pad_mask`: in each row the zeros form a tail of at most 256 positions.
All inputs are finite; a program needn't handle non-finite values.
Results may differ from a plain program's by a relative error of at most 0.025.
Values may be sent and summed in bfloat16 or wider, within the bound.
No kernel may reach another device: no remote copies, remote signals or barrier semaphores. Data moves between devices by JAX's collectives and lax.ppermute only.
A program may use at most 512 MiB of HBM per device.

v0:
```python
from functools import partial
import math

import jax
import jax.numpy as jnp
from jax import lax
from jax.sharding import PartitionSpec as P

HEADS = 12
HEAD = 64
DIM = 128


EPS_NORM = 1e-05
EPS_PROJ = 1e-06
NEG_FILL = -1e30


def passed_along(value, axis, steps):
    count = lax.axis_size(axis)
    leading, last = (max(0, -steps), min(count, count - steps))
    return lax.ppermute(value, axis, [(source, source + steps) for source in range(leading, last)])


def spread_2(value, axis, root):
    mine = lax.axis_index(axis) == root
    return lax.psum(jnp.where(mine, value, jnp.zeros_like(value)), axis)


def norm_rows(values, gain_row, shift_by):
    centred = values - jnp.mean(values, axis=-1, keepdims=True)
    spread = jnp.mean(centred * centred, axis=-1, keepdims=True)
    return centred * lax.rsqrt(spread + EPS_NORM) * gain_row + shift_by


def row_allowed(starts, real_flags):
    places = jnp.arange(real_flags.shape[0], dtype=jnp.int32)
    segment = jnp.sum((starts[None, :] <= places[:, None]).astype(jnp.int32), axis=1)
    same_segment = segment[:, None] == segment[None, :]
    usable = (real_flags[None, :] == 1) | (places[:, None] == places[None, :])
    return same_segment & usable


def matmul(left_rows, right_rows):
    return jnp.dot(left_rows, right_rows, preferred_element_type=jnp.float32)


def contract_rows(left_rows, right_rows):
    return lax.dot_general(
        left_rows, right_rows, (((0,), (0,)), ((), ())), preferred_element_type=jnp.float32
    )


def contract_cols(left_rows, right_rows):
    return lax.dot_general(
        left_rows, right_rows, (((1,), (1,)), ((), ())), preferred_element_type=jnp.float32
    )


def empty_piece(length, feat_width, ff_width):
    block_rows = min(512, length)
    first_rows = jnp.zeros((length, feat_width), jnp.bfloat16)
    kept_parts = (
        first_rows,
        jnp.zeros((length, 3 * feat_width), jnp.bfloat16),
        jnp.zeros((length, feat_width), jnp.bfloat16),
        jnp.zeros((length // block_rows, HEADS, block_rows), jnp.float32),
        jnp.zeros((length, feat_width), jnp.float32),
        jnp.zeros((length, ff_width), jnp.float32),
        jnp.zeros((length, feat_width), jnp.float32),
    )
    return (jnp.zeros((length, feat_width), jnp.bfloat16), kept_parts)


def attend_forward(queries, key_rows, value_rows, allowed):
    length = queries.shape[0]
    block_rows = min(512, length)
    score_scale = HEAD ** (-0.5)
    keys_split = key_rows.reshape(length, HEADS, HEAD)
    values_split = value_rows.reshape(length, HEADS, HEAD)

    def one_block(block_piece):
        query_part, mask_part = block_piece
        scores = (
            jnp.einsum("qhd,khd->hqk", query_part, keys_split, preferred_element_type=jnp.float32)
            * score_scale
        )
        scores = jnp.where(mask_part[None], scores, NEG_FILL)
        row_top = jnp.max(scores, axis=-1, keepdims=True)
        expo_scores = jnp.exp(scores - row_top)
        row_total = jnp.sum(expo_scores, axis=-1, keepdims=True)
        soft_probs = (expo_scores / row_total).astype(jnp.bfloat16)
        context = jnp.einsum(
            "hqk,khd->qhd", soft_probs, values_split, preferred_element_type=jnp.float32
        )
        return (context, row_top[..., 0] + jnp.log(row_total[..., 0]))

    context, logsum = lax.map(
        one_block,
        (
            queries.reshape(length // block_rows, block_rows, HEADS, HEAD),
            allowed.reshape(length // block_rows, block_rows, length),
        ),
    )
    return (context.reshape(length, HEADS * HEAD).astype(jnp.bfloat16), logsum)


def attend_backward(queries, key_rows, value_rows, logsum, grad_context, allowed):
    length = queries.shape[0]
    block_rows = min(512, length)
    block_count = length // block_rows
    score_scale = HEAD ** (-0.5)
    keys_split = key_rows.reshape(length, HEADS, HEAD)
    values_split = value_rows.reshape(length, HEADS, HEAD)

    def one_block(carried, block_piece):
        grad_keys, grad_values = carried
        query_part, mask_part, logsum_part, grad_part = block_piece
        scores = (
            jnp.einsum("qhd,khd->hqk", query_part, keys_split, preferred_element_type=jnp.float32)
            * score_scale
        )
        scores = jnp.where(mask_part[None], scores, NEG_FILL)
        soft_probs = jnp.exp(scores - logsum_part[..., None])
        grad_probs = jnp.einsum(
            "qhd,khd->hqk", grad_part, values_split, preferred_element_type=jnp.float32
        )
        inner_sum = jnp.sum(soft_probs * grad_probs, axis=-1, keepdims=True)
        grad_scores = (soft_probs * (grad_probs - inner_sum)).astype(jnp.bfloat16)
        grad_query = (
            jnp.einsum("hqk,khd->qhd", grad_scores, keys_split, preferred_element_type=jnp.float32)
            * score_scale
        )
        grad_keys = (
            grad_keys
            + jnp.einsum(
                "hqk,qhd->khd", grad_scores, query_part, preferred_element_type=jnp.float32
            )
            * score_scale
        )
        grad_values = grad_values + jnp.einsum(
            "hqk,qhd->khd",
            soft_probs.astype(jnp.bfloat16),
            grad_part,
            preferred_element_type=jnp.float32,
        )
        return ((grad_keys, grad_values), grad_query)

    empty_heads = jnp.zeros((length, HEADS, HEAD), jnp.float32)
    pieces = (
        queries.reshape(block_count, block_rows, HEADS, HEAD),
        allowed.reshape(block_count, block_rows, length),
        logsum,
        grad_context.reshape(block_count, block_rows, HEADS, HEAD),
    )
    (grad_keys, grad_values), grad_query = lax.scan(one_block, (empty_heads, empty_heads), pieces)
    return (
        grad_query.reshape(length, HEADS * HEAD),
        grad_keys.reshape(length, HEADS * HEAD),
        grad_values.reshape(length, HEADS * HEAD),
    )


def layer_forward(source, weights, allowed):
    w_qkv, b_qv, w_out, b_out, norm_gains, shifts, w_up, b_up, w_down, b_down = weights
    feat_width = source.shape[-1]
    mixed_rows = matmul(source, w_qkv)
    queries = (mixed_rows[:, :feat_width] + b_qv[:feat_width]).astype(jnp.bfloat16)
    key_rows = mixed_rows[:, feat_width : 2 * feat_width].astype(jnp.bfloat16)
    value_rows = (mixed_rows[:, 2 * feat_width :] + b_qv[feat_width:]).astype(jnp.bfloat16)
    context, logsum = attend_forward(queries, key_rows, value_rows, allowed)
    summed = source.astype(jnp.float32) + matmul(context, w_out) + b_out
    hidden = norm_rows(summed, norm_gains[0], shifts[0])
    raised = matmul(hidden.astype(jnp.bfloat16), w_up) + b_up
    lowered = matmul(jax.nn.gelu(raised, approximate=False).astype(jnp.bfloat16), w_down) + b_down
    joined = hidden + lowered
    result = norm_rows(joined, norm_gains[1], shifts[1])
    packed = jnp.concatenate([queries, key_rows, value_rows], axis=1)
    return (result, (packed, context, logsum, summed, raised, joined))


def layer_backward(source, weights, kept_parts, grad_out, allowed):
    w_qkv, b_qv, w_out, b_out, norm_gains, shifts, w_up, b_up, w_down, b_down = weights
    packed, context, logsum, summed, raised, joined = kept_parts
    feat_width = source.shape[-1]
    _, pull_last = jax.vjp(norm_rows, joined, norm_gains[1], shifts[1])
    grad_joined, gain_last, shift_last = pull_last(grad_out)
    grad_lowered = grad_joined.astype(jnp.bfloat16)
    activated, pull_gelu = jax.vjp(partial(jax.nn.gelu, approximate=False), raised)
    activated = activated.astype(jnp.bfloat16)
    grad_w_down = contract_rows(activated, grad_lowered)
    grad_b_down = jnp.sum(grad_lowered.astype(jnp.float32), axis=0)
    grad_raised = pull_gelu(contract_cols(grad_lowered, w_down))[0].astype(jnp.bfloat16)
    hidden, pull_first = jax.vjp(norm_rows, summed, norm_gains[0], shifts[0])
    grad_w_up = contract_rows(hidden.astype(jnp.bfloat16), grad_raised)
    grad_b_up = jnp.sum(grad_raised.astype(jnp.float32), axis=0)
    grad_hidden = grad_joined + contract_cols(grad_raised, w_up)
    grad_summed, gain_first, shift_first = pull_first(grad_hidden)
    grad_attn = grad_summed.astype(jnp.bfloat16)
    grad_w_out = contract_rows(context, grad_attn)
    grad_b_out = jnp.sum(grad_attn.astype(jnp.float32), axis=0)
    grad_context = contract_cols(grad_attn, w_out).astype(jnp.bfloat16)
    queries = packed[:, :feat_width]
    key_rows = packed[:, feat_width : 2 * feat_width]
    value_rows = packed[:, 2 * feat_width :]
    grad_query, grad_keys, grad_values = attend_backward(
        queries, key_rows, value_rows, logsum, grad_context, allowed
    )
    grad_packed = jnp.concatenate([grad_query, grad_keys, grad_values], axis=1).astype(jnp.bfloat16)
    grad_w_qkv = contract_rows(source, grad_packed)
    grad_b_qv = jnp.concatenate(
        [
            jnp.sum(grad_packed[:, :feat_width].astype(jnp.float32), axis=0),
            jnp.sum(grad_packed[:, 2 * feat_width :].astype(jnp.float32), axis=0),
        ]
    )
    grad_source = grad_summed + contract_cols(grad_packed, w_qkv)
    grads = (
        grad_w_qkv,
        grad_b_qv,
        grad_w_out,
        grad_b_out,
        jnp.stack([gain_first, gain_last]),
        jnp.stack([shift_first, shift_last]),
        grad_w_up,
        grad_b_up,
        grad_w_down,
        grad_b_down,
    )
    return (grad_source, grads)


def body(
    tokens_in,
    seg_starts,
    pad_mask,
    w_qkv,
    b_qv,
    w_attn_out,
    b_attn_out,
    ln_gain,
    ln_bias,
    w_up,
    b_up,
    w_down,
    b_down,
    w_proj,
    cotangent,
):
    weights = (
        w_qkv[0],
        b_qv[0],
        w_attn_out[0],
        b_attn_out[0],
        ln_gain[0],
        ln_bias[0],
        w_up[0],
        b_up[0],
        w_down[0],
        b_down[0],
    )
    section_count = lax.axis_size("section")
    section_at = lax.axis_index("section")
    micro_count = tokens_in.shape[0]
    gathered = lax.all_gather(tokens_in, "section", axis=1, tiled=True)
    length = gathered.shape[1]
    feat_width = gathered.shape[2]
    ff_width = w_up.shape[2]
    tick_count = micro_count + section_count - 1

    def forward_piece(source, allowed):
        result, kept_parts = layer_forward(source, weights, allowed)
        return (result.astype(jnp.bfloat16), (source,) + kept_parts)

    blank_piece = empty_piece(length, feat_width, ff_width)
    saved_rows = jax.tree.map(
        lambda member: jnp.zeros((micro_count,) + member.shape, member.dtype), blank_piece[1]
    )
    finals = jnp.zeros((micro_count, length, feat_width), jnp.bfloat16)

    def forward_tick(tick_at, carried):
        in_rows, saved_now, finals_now = carried
        micro_at = tick_at - section_at
        is_live = (micro_at >= 0) & (micro_at < micro_count)
        slot_at = jnp.clip(micro_at, 0, micro_count - 1)
        source = jnp.where(
            section_at == 0, lax.dynamic_index_in_dim(gathered, slot_at, 0, keepdims=False), in_rows
        )
        allowed = row_allowed(seg_starts[slot_at], pad_mask[slot_at])
        outgoing, kept_parts = lax.cond(
            is_live,
            lambda operand: forward_piece(source, allowed),
            lambda operand: empty_piece(length, feat_width, ff_width),
            0,
        )
        saved_now = jax.tree.map(
            lambda buffer, fresh_part: lax.dynamic_update_index_in_dim(
                buffer, jnp.where(is_live, fresh_part, buffer[slot_at]), slot_at, 0
            ),
            saved_now,
            kept_parts,
        )
        at_last = is_live & (section_at == section_count - 1)
        finals_now = lax.dynamic_update_index_in_dim(
            finals_now, jnp.where(at_last, outgoing, finals_now[slot_at]), slot_at, 0
        )
        in_rows = passed_along(outgoing, "section", 1)
        return (in_rows, saved_now, finals_now)

    start_rows = jnp.zeros((length, feat_width), jnp.bfloat16)
    _, saved_rows, finals = lax.fori_loop(
        0, tick_count, forward_tick, (start_rows, saved_rows, finals)
    )
    factor = math.sqrt(DIM)
    dim_share = cotangent.shape[2]
    last_rows = spread_2(finals, "section", section_count - 1).reshape(
        micro_count * length, feat_width
    )
    columns = matmul(last_rows, w_proj)
    target = cotangent.reshape(micro_count * length, dim_share).astype(jnp.float32)
    square_part, cross_part = lax.psum(
        (jnp.sum(columns * columns, axis=1), jnp.sum(columns * target, axis=1)), "section"
    )
    inverse = lax.rsqrt(square_part + EPS_PROJ)[:, None]
    embedded = (factor * columns * inverse).astype(jnp.bfloat16).reshape(cotangent.shape)
    grad_columns = (
        factor * (target * inverse - columns * cross_part[:, None] * inverse**3)
    ).astype(jnp.bfloat16)
    grad_proj = contract_rows(last_rows, grad_columns)
    grad_last = (
        lax.psum(contract_cols(grad_columns, w_proj).astype(jnp.bfloat16), "section")
        .astype(jnp.float32)
        .reshape(micro_count, length, feat_width)
    )

    def backward_piece(stored, incoming, allowed):
        rest_parts = stored[1:]
        return layer_backward(stored[0], weights, rest_parts, incoming, allowed)

    zero_grads = tuple((jnp.zeros(member.shape, jnp.float32) for member in weights))
    totals = zero_grads

    def backward_tick(tick_at, carried):
        in_rows, totals_now, grad_rows = carried
        micro_at = tick_at - (section_count - 1 - section_at)
        is_live = (micro_at >= 0) & (micro_at < micro_count)
        slot_at = jnp.clip(micro_at, 0, micro_count - 1)
        from_head = lax.dynamic_index_in_dim(grad_last, slot_at, 0, keepdims=False)
        incoming = jnp.where(
            section_at == section_count - 1, from_head, in_rows.astype(jnp.float32)
        )
        stored = jax.tree.map(
            lambda buffer: lax.dynamic_index_in_dim(buffer, slot_at, 0, keepdims=False), saved_rows
        )
        allowed = row_allowed(seg_starts[slot_at], pad_mask[slot_at])
        grad_source, grads = lax.cond(
            is_live,
            lambda operand: backward_piece(stored, incoming, allowed),
            lambda operand: (jnp.zeros((length, feat_width), jnp.float32), zero_grads),
            0,
        )
        totals_now = tuple((before + added for before, added in zip(totals_now, grads)))
        at_first = is_live & (section_at == 0)
        grad_rows = lax.dynamic_update_index_in_dim(
            grad_rows, jnp.where(at_first, grad_source, grad_rows[slot_at]), slot_at, 0
        )
        in_rows = passed_along(grad_source.astype(jnp.bfloat16), "section", -1)
        return (in_rows, totals_now, grad_rows)

    start_grads = jnp.zeros((micro_count, length, feat_width), jnp.float32)
    _, totals, grad_rows = lax.fori_loop(
        0, tick_count, backward_tick, (start_rows, totals, start_grads)
    )
    shards = (
        lax.psum_scatter(totals[0][None], "dp", scatter_dimension=1, tiled=True),
        lax.psum_scatter(totals[1][None], "dp", scatter_dimension=1, tiled=True),
        lax.psum_scatter(totals[2][None], "dp", scatter_dimension=1, tiled=True),
        lax.psum_scatter(totals[3][None], "dp", scatter_dimension=1, tiled=True),
        lax.psum_scatter(totals[4][None], "dp", scatter_dimension=2, tiled=True),
        lax.psum_scatter(totals[5][None], "dp", scatter_dimension=2, tiled=True),
        lax.psum_scatter(totals[6][None], "dp", scatter_dimension=1, tiled=True),
        lax.psum_scatter(totals[7][None], "dp", scatter_dimension=1, tiled=True),
        lax.psum_scatter(totals[8][None], "dp", scatter_dimension=1, tiled=True),
        lax.psum_scatter(totals[9][None], "dp", scatter_dimension=1, tiled=True),
        lax.psum_scatter(grad_proj, "dp", scatter_dimension=0, tiled=True),
    )
    grad_input = lax.psum_scatter(
        grad_rows.astype(jnp.bfloat16), "section", scatter_dimension=1, tiled=True
    ).astype(jnp.float32)
    return (
        embedded,
        grad_input,
        shards[0],
        shards[1],
        shards[2],
        shards[3],
        shards[4],
        shards[5],
        shards[6],
        shards[7],
        shards[8],
        shards[9],
        shards[10],
    )


def solution(mesh):
    in_specs = (
        P("dp", "section", None),
        P("dp", None),
        P("dp", None),
        P("section", None, None),
        P("section", None),
        P("section", None, None),
        P("section", None),
        P("section", None, None),
        P("section", None, None),
        P("section", None, None),
        P("section", None),
        P("section", None, None),
        P("section", None),
        P(None, "section"),
        P("dp", None, "section"),
    )
    out_specs = (
        P("dp", None, "section"),
        P("dp", "section", None),
        P("section", "dp", None),
        P("section", "dp"),
        P("section", "dp", None),
        P("section", "dp"),
        P("section", None, "dp"),
        P("section", None, "dp"),
        P("section", "dp", None),
        P("section", "dp"),
        P("section", "dp", None),
        P("section", "dp"),
        P("dp", "section"),
    )
    return jax.shard_map(body, mesh=mesh, in_specs=in_specs, out_specs=out_specs, check_vma=False)
```

profile of v0, /device:TPU:13, one launch (start us, length us, event | category | flops | bytes accessed | tf_op | source)
XLA Modules:
  0.0 4107.4 jit_solution(3543887551145537343)
XLA Ops:
  10.3 29.4 all-gather.2.cloned.1.call-done
  69.9 1139.0 %while.113 = (s32[]{:T(128)}, bf16[1024,768]{0,1:T(8,128)(2,1)}, bf16[2,1024,768]{2,1,0:T(8,128)(2,1)}, bf16[2,1024,2304]{1,2,0:T(8,128)(2,1)}, bf16[2,1024,768]...) while((s32[]{:T(128)}, bf16[1024,768]{0,1:T(8,128)(2,1)}, ...), condition=%wide.region_12.13_spmd, body=%wide.region_0.12_spmd.sunk | while | flops 16442222592 | bytes 767307648 | solution.py:311
  75.8 25.6 conditional.5
  453.1 182.8 %collective-permute-done.1 = bf16[1024,768]{0,1:T(8,128)(2,1)} collective-permute-done((bf16[1024,768]{0,1:T(8,128)(2,1)}, bf16[1024,768]{0,1:T(8,128)(2,1)}, u32[]{:S(2)}, u32[]{:S(2)}) %collective-permute-start.1) | collective-permute-done | bytes 1572896 | tf_op jit(solution)/shard_map/while/body/eval_jaxpr/ppermute | solution.py:22
  641.5 172.4 %conditional.5 = (bf16[1024,768]{0,1:T(8,128)(2,1)}, bf16[1024,768]{0,1:T(8,128)(2,1)}, bf16[1024,2304]{1,0:T(8,128)(2,1)}, bf16[1024,768]{0,1:T(8,128)(2,1)}, f...) conditional(s32[]{:T(128)} %convert_element_type.257, ...), branch_computations={%region_1.1_spmd, %region_2.11_spmd} | conditional | flops 16432760832 | bytes 400721120 | solution.py:290
  673.7 71.0 %while.111 = (s32[]{:T(128)}, bf16[2,512,12,64]{1,3,2,0:T(8,128)(2,1)}, f32[2,12,512]{2,1,0:T(8,128)S(1)}, pred[2,512,1024]{2,1,0:T(8,128)(4,1)}, bf16[2,512,12,...) while((s32[]{:T(128)}, ...), condition=%wide.region_7.6_spmd, body=%wide.region_4.5_spmd.sunk | while | flops 1686104064 | bytes 190800528 | solution.py:98
  768.1 37.2 fusion.143
  926.3 172.4 %conditional.5 = (bf16[1024,768]{0,1:T(8,128)(2,1)}, bf16[1024,768]{0,1:T(8,128)(2,1)}, bf16[1024,2304]{1,0:T(8,128)(2,1)}, bf16[1024,768]{0,1:T(8,128)(2,1)}, f...) conditional(s32[]{:T(128)} %convert_element_type.257, ...), branch_computations={%region_1.1_spmd, %region_2.11_spmd} | conditional | flops 16432760832 | bytes 400721120 | solution.py:290
  958.5 71.0 %while.111 = (s32[]{:T(128)}, bf16[2,512,12,64]{1,3,2,0:T(8,128)(2,1)}, f32[2,12,512]{2,1,0:T(8,128)S(1)}, pred[2,512,1024]{2,1,0:T(8,128)(4,1)}, bf16[2,512,12,...) while((s32[]{:T(128)}, ...), condition=%wide.region_7.6_spmd, body=%wide.region_4.5_spmd.sunk | while | flops 1686104064 | bytes 190800528 | solution.py:98
  1052.9 37.2 fusion.143
  1212.8 68.2 %all-reduce.4.cloned.1.call-done = bf16[2048,768]{1,0:T(8,128)(2,1)} async-done(((bf16[2048,768]{1,0:T(8,128)(2,1)}), bf16[2048,768]{1,0:T(8,128)(2,1)}) %all-reduce.4.cloned.1.call-update) | async-done | bytes 3145744 | tf_op jit(solution)/shard_map/psum | solution.py:27
  1301.2 65.6 %all-reduce.6.cloned.1.call-done = bf16[2,1024,768]{2,1,0:T(8,128)(2,1)} async-done(((bf16[2,1024,768]{2,1,0:T(8,128)(2,1)}), bf16[2,1024,768]{2,1,0:T(8,128)(2,1)}) %all-reduce.6.cloned.1.call-update) | async-done | bytes 3145744 | tf_op jit(solution)/shard_map/psum | solution.py:331
  1373.0 1494.5 %while.114 = (s32[]{:T(128)}, bf16[1024,768]{1,0:T(8,128)(2,1)}, f32[768,2304]{1,0:T(8,128)}, f32[1536]{0:T(1024)}, f32[768,768]{1,0:T(8,128)}, /*index=5*/f32[7...) while((s32[]{:T(128)}, bf16[1024,768]{1,0:T(8,128)(2,1)}, ...), condition=%wide.region_43.44_spmd.clone, body=%wide.region_19.43_spmd.clone.sunk | while | flops 33471242240 | bytes 939819776 | solution.py:371
  1379.3 321.7 %conditional.6 = (bf16[1024,768]{1,0:T(8,128)(2,1)}, f32[768,2304]{1,0:T(8,128)}, f32[1536]{0:T(1024)S(1)}, f32[768,768]{1,0:T(8,128)}, f32[768]{0:T(1024)}, /*i...) conditional(s32[]{:T(128)} %convert_element_type.259, ...), branch_computations={%region_20.20_spmd, %region_21.42_spmd} | conditional | flops 33456269312 | bytes 800403072 | solution.py:356
  1397.0 26.9 fusion.91
  1476.6 172.6 %while.112 = (s32[]{:T(128)}, f32[1024,12,64]{0,2,1:T(8,128)S(1)}, f32[1024,12,64]{0,2,1:T(8,128)}, bf16[2,512,12,64]{1,3,2,0:T(8,128)(2,1)}, bf16[2,512,12,64]{...) while((s32[]{:T(128)}, f32[1024,12,64]{0,2,1:T(8,128)S(1)}, ...), condition=%wide.region_33.32_spmd.clone, body=%wide.region_31.31_spmd.clone.sunk | while | flops 4125222912 | bytes 217754288 | solution.py:156
  1742.1 321.5 %conditional.6 = (bf16[1024,768]{1,0:T(8,128)(2,1)}, f32[768,2304]{1,0:T(8,128)}, f32[1536]{0:T(1024)S(1)}, f32[768,768]{1,0:T(8,128)}, f32[768]{0:T(1024)}, /*i...) conditional(s32[]{:T(128)} %convert_element_type.259, ...), branch_computations={%region_20.20_spmd, %region_21.42_spmd} | conditional | flops 33456269312 | bytes 800403072 | solution.py:356
  1759.7 26.9 fusion.91
  1839.2 172.6 %while.112 = (s32[]{:T(128)}, f32[1024,12,64]{0,2,1:T(8,128)S(1)}, f32[1024,12,64]{0,2,1:T(8,128)}, bf16[2,512,12,64]{1,3,2,0:T(8,128)(2,1)}, bf16[2,512,12,64]{...) while((s32[]{:T(128)}, f32[1024,12,64]{0,2,1:T(8,128)S(1)}, ...), condition=%wide.region_33.32_spmd.clone, body=%wide.region_31.31_spmd.clone.sunk | while | flops 4125222912 | bytes 217754288 | solution.py:156
  2129.2 277.9 %collective-permute-start = (bf16[1024,768]{1,0:T(8,128)(2,1)}, bf16[1024,768]{1,0:T(8,128)(2,1)S(1)}, u32[]{:S(2)}, u32[]{:S(2)}) collective-permute-start(bf16[1024,768]{1,0:T(8,128)(2,1)} %get-tuple-element.2798), channel_id=1, source_target_pairs={{8,0},{16,8},{24,16},{9,1},{17,9},{25,17},{10,2},{18,10},{26,18},{... | collective-permute-start | bytes 4718600 | tf_op jit(solution)/shard_map/while/body/eval_jaxpr/ppermute | solution.py:22
  2541.7 282.1 %collective-permute-start = (bf16[1024,768]{1,0:T(8,128)(2,1)}, bf16[1024,768]{1,0:T(8,128)(2,1)S(1)}, u32[]{:S(2)}, u32[]{:S(2)}) collective-permute-start(bf16[1024,768]{1,0:T(8,128)(2,1)} %get-tuple-element.2798), channel_id=1, source_target_pairs={{8,0},{16,8},{24,16},{9,1},{17,9},{25,17},{10,2},{18,10},{26,18},{... | collective-permute-start | bytes 4718600 | tf_op jit(solution)/shard_map/while/body/eval_jaxpr/ppermute | solution.py:22
  2883.6 312.8 %reduce-scatter.47.cloned.1.call-done = f32[96,1]{1,0:T(8,128)} async-done(((f32[768,1]{1,0:T(8,128)}), f32[96,1]{1,0:T(8,128)}) %reduce-scatter.47.cloned.1.call-update) | async-done | bytes 400
  3197.8 62.2 %reduce-scatter.39.cloned.1.call-done = f32[96,1]{1,0:T(8,128)} async-done(((f32[768,1]{1,0:T(8,128)}), f32[96,1]{1,0:T(8,128)}) %reduce-scatter.39.cloned.1.call-update) | async-done | bytes 400
  3261.4 63.6 %reduce-scatter.37.cloned.1.call-done = f32[192,1]{1,0:T(8,128)} async-done(((f32[1536,1]{1,0:T(8,128)}), f32[192,1]{1,0:T(8,128)}) %reduce-scatter.37.cloned.1.call-update) | async-done | bytes 784
  3326.5 62.3 %reduce-scatter.43.cloned.1.call-done = f32[96,2]{1,0:T(8,128)} async-done(((f32[768,2]{1,0:T(8,128)}), f32[96,2]{1,0:T(8,128)}) %reduce-scatter.43.cloned.1.call-update) | async-done | bytes 784
  3390.3 62.7 %reduce-scatter.41.cloned.1.call-done = f32[96,2]{1,0:T(8,128)} async-done(((f32[768,2]{1,0:T(8,128)}), f32[96,2]{1,0:T(8,128)}) %reduce-scatter.41.cloned.1.call-update) | async-done | bytes 784
  3454.4 67.3 %reduce-scatter.45.cloned.1.call-done = f32[384,1]{1,0:T(8,128)} async-done(((f32[3072,1]{1,0:T(8,128)}), f32[384,1]{1,0:T(8,128)}) %reduce-scatter.45.cloned.1.call-update) | async-done | bytes 1552
  3523.3 38.6 reduce-scatter.27.cloned.1.call-done
  3564.2 70.1 %reduce-scatter.31.cloned.1.call-done = f32[1,96,768]{2,1,0:T(8,128)} async-done(((f32[1,768,768]{2,1,0:T(8,128)}), f32[1,96,768]{2,1,0:T(8,128)}) %reduce-scatter.31.cloned.1.call-update) | async-done | bytes 294928 | tf_op jit(solution)/shard_map/reduce_scatter | solution.py:377
  3634.3 133.6 %reduce-scatter.29.cloned.1.call-done = f32[1,96,2304]{2,1,0:T(8,128)} async-done(((f32[1,768,2304]{2,1,0:T(8,128)}), f32[1,96,2304]{2,1,0:T(8,128)}) %reduce-scatter.29.cloned.1.call-update) | async-done | bytes 884752 | tf_op jit(solution)/shard_map/reduce_scatter | solution.py:375
  3767.9 166.2 %reduce-scatter.33.cloned.1.call-done = f32[1,96,3072]{2,1,0:T(8,128)} async-done(((f32[1,768,3072]{2,1,0:T(8,128)}), f32[1,96,3072]{2,1,0:T(8,128)}) %reduce-scatter.33.cloned.1.call-update) | async-done | bytes 1179664 | tf_op jit(solution)/shard_map/reduce_scatter | solution.py:381
  3934.1 166.6 %reduce-scatter.35.cloned.1.call-done = f32[1,384,768]{2,1,0:T(8,128)} async-done(((f32[1,3072,768]{2,1,0:T(8,128)}), f32[1,384,768]{2,1,0:T(8,128)}) %reduce-scatter.35.cloned.1.call-update) | async-done | bytes 1179664 | tf_op jit(solution)/shard_map/reduce_scatter | solution.py:383
  (1160 shorter events, 1911.9 us)
Async XLA Ops:
  7.2 1273.8 %copy-start = (bf16[768,32]{0,1:T(8,128)(2,1)S(1)}, bf16[768,32]{0,1:T(8,128)(2,1)}, u32[]{:S(2)}) copy-start(bf16[768,32]{0,1:T(8,128)(2,1)} %param.40) | copy-start | bytes 147460
  7.2 32.5 all-gather.2.cloned.1.call-start
  9.6 1271.4 %all-reduce.4.cloned.1.call-start = ((), (), s32[]{:S(2)}) async-start(), calls=%async_computation.13 | async-start | bytes 6291456 | tf_op jit(solution)/shard_map/psum | solution.py:27
  101.4 96.0 %collective-permute-start.1 = (bf16[1024,768]{0,1:T(8,128)(2,1)}, bf16[1024,768]{0,1:T(8,128)(2,1)}, u32[]{:S(2)}, u32[]{:S(2)}) collective-permute-start(bf16[1024,768]{0,1:T(8,128)(2,1)} %get-tuple-element.2754), channel_id=1, source_target_pairs={{0,8},{8,16},{16,24},{1,9},{9,17},{17,25},{2,10},{10,18},{18,26},{... | collective-permute-start | bytes 4718600 | tf_op jit(solution)/shard_map/while/body/eval_jaxpr/ppermute | solution.py:22
  229.2 96.0 %collective-permute-start.1 = (bf16[1024,768]{0,1:T(8,128)(2,1)}, bf16[1024,768]{0,1:T(8,128)(2,1)}, u32[]{:S(2)}, u32[]{:S(2)}) collective-permute-start(bf16[1024,768]{0,1:T(8,128)(2,1)} %get-tuple-element.2754), channel_id=1, source_target_pairs={{0,8},{8,16},{16,24},{1,9},{9,17},{17,25},{2,10},{10,18},{18,26},{... | collective-permute-start | bytes 4718600 | tf_op jit(solution)/shard_map/while/body/eval_jaxpr/ppermute | solution.py:22
  357.0 278.8 %collective-permute-start.1 = (bf16[1024,768]{0,1:T(8,128)(2,1)}, bf16[1024,768]{0,1:T(8,128)(2,1)}, u32[]{:S(2)}, u32[]{:S(2)}) collective-permute-start(bf16[1024,768]{0,1:T(8,128)(2,1)} %get-tuple-element.2754), channel_id=1, source_target_pairs={{0,8},{8,16},{16,24},{1,9},{9,17},{17,25},{2,10},{10,18},{18,26},{... | collective-permute-start | bytes 4718600 | tf_op jit(solution)/shard_map/while/body/eval_jaxpr/ppermute | solution.py:22
  438.7 197.2 %copy-start.65 = (f32[1536]{0:T(1024)S(1)}, f32[1536]{0:T(1024)}, u32[]{:S(2)}) copy-start(f32[1536]{0:T(1024)} %copy-done.64) | copy-start | bytes 18436 | tf_op jit(solution)/shard_map/while
  813.9 106.5 %collective-permute-start.1 = (bf16[1024,768]{0,1:T(8,128)(2,1)}, bf16[1024,768]{0,1:T(8,128)(2,1)}, u32[]{:S(2)}, u32[]{:S(2)}) collective-permute-start(bf16[1024,768]{0,1:T(8,128)(2,1)} %get-tuple-element.2754), channel_id=1, source_target_pairs={{0,8},{8,16},{16,24},{1,9},{9,17},{17,25},{2,10},{10,18},{18,26},{... | collective-permute-start | bytes 4718600 | tf_op jit(solution)/shard_map/while/body/eval_jaxpr/ppermute | solution.py:22
  1098.7 106.4 %collective-permute-start.1 = (bf16[1024,768]{0,1:T(8,128)(2,1)}, bf16[1024,768]{0,1:T(8,128)(2,1)}, u32[]{:S(2)}, u32[]{:S(2)}) collective-permute-start(bf16[1024,768]{0,1:T(8,128)(2,1)} %get-tuple-element.2754), channel_id=1, source_target_pairs={{0,8},{8,16},{16,24},{1,9},{9,17},{17,25},{2,10},{10,18},{18,26},{... | collective-permute-start | bytes 4718600 | tf_op jit(solution)/shard_map/while/body/eval_jaxpr/ppermute | solution.py:22
  1212.7 154.1 %all-reduce.6.cloned.1.call-start = ((), (), s32[]{:S(2)}) async-start(), calls=%async_computation.14 | async-start | bytes 6291456 | tf_op jit(solution)/shard_map/psum | solution.py:331
  1297.0 1585.1 %reduce-scatter.49.cloned.1.call-start = ((), (), s32[]{:S(2)}) async-start(), calls=%async_computation.26 | async-start | bytes 442368
  1301.1 71.9 %copy-start.40 = (f32[2,2,12,512]{3,2,1,0:T(8,128)S(1)}, f32[2,2,12,512]{3,2,1,0:T(8,128)}, u32[]{:S(2)}) copy-start(f32[2,2,12,512]{3,2,1,0:T(8,128)} %get-tuple-element.3044) | copy-start | bytes 294916
  1301.1 71.9 %copy-start.45 = (f32[2,768]{1,0:T(2,128)S(1)}, f32[2,768]{1,0:T(2,128)}, u32[]{:S(2)}) copy-start(f32[2,768]{1,0:T(2,128)} %get-tuple-element.3175) | copy-start | bytes 18436
  1301.1 1895.3 %reduce-scatter.47.cloned.1.call-start = ((), (), s32[]{:S(2)}) async-start(), calls=%async_computation.25 | async-start | bytes 442368
  1381.5 71.5 %copy-start.42 = (f32[1024]{0:T(1024)}, f32[1024]{0:T(1024)S(1)}, u32[]{:S(2)}) copy-start(f32[1024]{0:T(1024)S(1)} %broadcast_multiply_fusion.2) | copy-start | bytes 12292 | tf_op jit(solution)/shard_map/while/body/eval_jaxpr/cond
  1701.0 33.7 collective-permute-start
  1744.4 71.2 %copy-start.42 = (f32[1024]{0:T(1024)}, f32[1024]{0:T(1024)S(1)}, u32[]{:S(2)}) copy-start(f32[1024]{0:T(1024)S(1)} %broadcast_multiply_fusion.2) | copy-start | bytes 12292 | tf_op jit(solution)/shard_map/while/body/eval_jaxpr/cond
  2063.6 41.8 %collective-permute-start = (bf16[1024,768]{1,0:T(8,128)(2,1)}, bf16[1024,768]{1,0:T(8,128)(2,1)S(1)}, u32[]{:S(2)}, u32[]{:S(2)}) collective-permute-start(bf16[1024,768]{1,0:T(8,128)(2,1)} %get-tuple-element.2798), channel_id=1, source_target_pairs={{8,0},{16,8},{24,16},{9,1},{17,9},{25,17},{10,2},{18,10},{26,18},{... | collective-permute-start | bytes 4718600 | tf_op jit(solution)/shard_map/while/body/eval_jaxpr/ppermute | solution.py:22
  2129.2 318.4 %collective-permute-start = (bf16[1024,768]{1,0:T(8,128)(2,1)}, bf16[1024,768]{1,0:T(8,128)(2,1)S(1)}, u32[]{:S(2)}, u32[]{:S(2)}) collective-permute-start(bf16[1024,768]{1,0:T(8,128)(2,1)} %get-tuple-element.2798), channel_id=1, source_target_pairs={{8,0},{16,8},{24,16},{9,1},{17,9},{25,17},{10,2},{18,10},{26,18},{... | collective-permute-start | bytes 4718600 | tf_op jit(solution)/shard_map/while/body/eval_jaxpr/ppermute | solution.py:22
  2471.0 47.3 %collective-permute-start = (bf16[1024,768]{1,0:T(8,128)(2,1)}, bf16[1024,768]{1,0:T(8,128)(2,1)S(1)}, u32[]{:S(2)}, u32[]{:S(2)}) collective-permute-start(bf16[1024,768]{1,0:T(8,128)(2,1)} %get-tuple-element.2798), channel_id=1, source_target_pairs={{8,0},{16,8},{24,16},{9,1},{17,9},{25,17},{10,2},{18,10},{26,18},{... | collective-permute-start | bytes 4718600 | tf_op jit(solution)/shard_map/while/body/eval_jaxpr/ppermute | solution.py:22
  2541.7 322.6 %collective-permute-start = (bf16[1024,768]{1,0:T(8,128)(2,1)}, bf16[1024,768]{1,0:T(8,128)(2,1)S(1)}, u32[]{:S(2)}, u32[]{:S(2)}) collective-permute-start(bf16[1024,768]{1,0:T(8,128)(2,1)} %get-tuple-element.2798), channel_id=1, source_target_pairs={{8,0},{16,8},{24,16},{9,1},{17,9},{25,17},{10,2},{18,10},{26,18},{... | collective-permute-start | bytes 4718600 | tf_op jit(solution)/shard_map/while/body/eval_jaxpr/ppermute | solution.py:22
  2869.1 390.9 %reduce-scatter.39.cloned.1.call-start = ((), (), s32[]{:S(2)}) async-start(), calls=%async_computation.21 | async-start | bytes 442368
  2870.8 454.2 %reduce-scatter.37.cloned.1.call-start = ((), (), s32[]{:S(2)}) async-start(), calls=%async_computation.20 | async-start | bytes 884736
  2872.7 516.2 %reduce-scatter.43.cloned.1.call-start = ((), (), s32[]{:S(2)}) async-start(), calls=%async_computation.23 | async-start | bytes 442368
  2874.4 578.6 %reduce-scatter.41.cloned.1.call-start = ((), (), s32[]{:S(2)}) async-start(), calls=%async_computation.22 | async-start | bytes 442368
  2876.1 645.6 %reduce-scatter.45.cloned.1.call-start = ((), (), s32[]{:S(2)}) async-start(), calls=%async_computation.24 | async-start | bytes 1769472
  2877.9 684.0 %reduce-scatter.27.cloned.1.call-start = ((), (), s32[]{:S(2)}) async-start(), calls=%async_computation.15 | async-start | bytes 3932160 | tf_op jit(solution)/shard_map/reduce_scatter | solution.py:387
  2878.6 755.7 %reduce-scatter.31.cloned.1.call-start = ((), (), s32[]{:S(2)}) async-start(), calls=%async_computation.17 | async-start | bytes 2654208 | tf_op jit(solution)/shard_map/reduce_scatter | solution.py:377
  2879.2 888.8 %reduce-scatter.29.cloned.1.call-start = ((), (), s32[]{:S(2)}) async-start(), calls=%async_computation.16 | async-start | bytes 7962624 | tf_op jit(solution)/shard_map/reduce_scatter | solution.py:375
  2879.9 1054.2 %reduce-scatter.33.cloned.1.call-start = ((), (), s32[]{:S(2)}) async-start(), calls=%async_computation.18 | async-start | bytes 10616832 | tf_op jit(solution)/shard_map/reduce_scatter | solution.py:381
  2880.5 1220.2 %reduce-scatter.35.cloned.1.call-start = ((), (), s32[]{:S(2)}) async-start(), calls=%async_computation.19 | async-start | bytes 10616832 | tf_op jit(solution)/shard_map/reduce_scatter | solution.py:383
  2880.5 1220.2 %copy-start.1 = (bf16[768,32]{0,1:T(8,128)(2,1)S(1)}, bf16[768,32]{0,1:T(8,128)(2,1)}, u32[]{:S(2)}) copy-start(bf16[768,32]{0,1:T(8,128)(2,1)} %param.40) | copy-start | bytes 147460
  (260 other events, 2136.0 us)
Sparse Core Ops, SparseCore 0:
  10.2 29.5 all-gather.1
  1212.8 68.1 all-reduce.3
  1297.1 69.5 all-reduce.5
  1369.9 60.0 reduce-scatter.48
  2869.2 327.1 reduce-scatter.46
  3199.5 60.4 reduce-scatter.38
  3263.3 61.6 reduce-scatter.36
  3328.6 60.2 reduce-scatter.42
  3392.5 60.4 reduce-scatter.40
  3457.2 64.4 reduce-scatter.44
  3524.2 37.5 reduce-scatter.26
  3566.2 68.1 reduce-scatter.30
  3639.0 128.8 reduce-scatter.28
  3772.0 162.1 reduce-scatter.32
  3938.1 162.5 reduce-scatter.34
where the time goes:
time: 4120 us; the launch traced here: 4110 us
  waiting for transfers between devices  1560 us (38%)
  local copies, waits for them, and re-layouts  675 us (16%)
  other arithmetic  630 us (15%)
  matrix products  605 us (15%)
  starting transfers between devices  577 us (14%)
  loops' own time  41.2 us (1%)
    unnamed x22, waiting for transfers between devices  634 us
    ppermute x10, starting transfers between devices, passed_along(): lax.ppermute(value, axis, [(source, source + steps) for source in range(l...  576 us
    ppermute x10, waiting for transfers between devices, passed_along(): lax.ppermute(value, axis, [(source, source + steps) for source in range(l...  183 us
    add x40, other arithmetic, backward_tick(): before + added  177 us
    dynamic_slice x60, local copies, waits for them, and re-layouts, forward_tick(): buffer[slot_at]  173 us
    reduce_scatter x1, waiting for transfers between devices, body(): lax.psum_scatter(totals[8][None], 'dp', scatter_dimension=1, tiled=True)  167 us
    reduce_scatter x1, waiting for transfers between devices, body(): lax.psum_scatter(totals[6][None], 'dp', scatter_dimension=1, tiled=True)  166 us
    dynamic_update_slice x40, local copies, waits for them, and re-layouts, forward_tick(): lax.dynamic_update_index_in_dim(buffer, jnp.where(is_live, fresh_part, bu...  138 us
  transfers between devices with their start and end apart: 25, of which 15 were waited for; matrix products, arithmetic and copies ran while one was open for 34% of the time, Pallas kernels for 0%

commit v1 on v0

v1 whole, which is shorter than its diff:
```python
from functools import partial
import math

import jax
import jax.numpy as jnp
from jax import lax
from jax.experimental import pallas as pl
from jax.experimental.pallas import tpu as pltpu
from jax.sharding import PartitionSpec as P

HEAD = 64
PAIR = 2 * HEAD
GROUPS = 2
QB = 128
KB = 256
EPS_NORM = 1e-05
EPS_PROJ = 1e-06
NEG_FILL = -1e30
VMEM = 56 * 1024 * 1024
BF = jnp.bfloat16
F32 = jnp.float32

NT = (((1,), (1,)), ((), ()))
TN = (((0,), (0,)), ((), ()))


def dot(a, b):
    return jnp.dot(a, b, preferred_element_type=F32)


def dot_nt(a, b):
    return lax.dot_general(a, b, NT, preferred_element_type=F32)


def dot_tn(a, b):
    return lax.dot_general(a, b, TN, preferred_element_type=F32)


def pack_small(b_qv, b_out, gains, shifts, b_up, b_down):
    return jnp.concatenate(
        [b_up, b_qv, b_out, gains[0], gains[1], shifts[0], shifts[1], b_down]
    )


def small_spec(layer, width):
    return pl.BlockSpec((1, 1, width), lambda *_: (layer, 0, 0))


def attention_plan(starts, real_flags):
    length = real_flags.shape[0]
    places = jnp.arange(length, dtype=jnp.int32)
    segment = jnp.sum((starts[None, :] <= places[:, None]).astype(jnp.int32), axis=1)
    key_code = jnp.where(real_flags == 1, segment, -1).astype(F32)
    key_code = jnp.broadcast_to(key_code[:, None], (length, PAIR))
    query_code = segment.astype(F32).reshape(length // QB, QB)
    first = jnp.arange(length // QB, dtype=jnp.int32) * QB
    low = jnp.max(jnp.where(starts[None, :] <= first[:, None], starts[None, :], 0), axis=1)
    high = jnp.min(
        jnp.where(starts[None, :] > first[:, None] + (QB - 1), starts[None, :], length), axis=1
    )
    begin = (low // QB) * QB
    count = (high - begin + KB - 1) // KB
    begin = jnp.minimum(begin, length - KB * count)
    return (begin, count, key_code, query_code)


def pair_mask(rows):
    return lax.broadcasted_iota(jnp.int32, (rows, PAIR), 1) < HEAD


def stacked_heads(block):
    first = pair_mask(block.shape[0])
    zero = jnp.zeros_like(block)
    return jnp.concatenate([jnp.where(first, block, zero), jnp.where(first, zero, block)], axis=0)


def block_bias(key_code, query_code, key_at, query_at):
    keys = lax.broadcasted_iota(jnp.int32, (KB, QB), 0) + (key_at - query_at)
    same = keys == lax.broadcasted_iota(jnp.int32, (KB, QB), 1)
    bias = jnp.where((key_code == query_code) | same, 0.0, NEG_FILL)
    return jnp.concatenate([bias, bias], axis=1)


def top_rows(values, op):
    folded = values.reshape(values.shape[0] // 8, 8, values.shape[1])
    return op(folded, axis=0)


def unstack_heads(flat):
    rows = lax.broadcasted_iota(jnp.int32, (PAIR, QB), 0)
    return jnp.where(rows < HEAD, flat[:PAIR, :QB], flat[:PAIR, QB:]).T


def attend_forward_kernel(
    begin_ref, count_ref, qkv_ref, key_code_ref, query_code_ref, out_ref, logsum_ref,
    value_scr, query_scr, score_scr, total_scr,
):
    length = qkv_ref.shape[1]
    pairs = qkv_ref.shape[2] // PAIR
    cols = [slice(p * PAIR, (p + 1) * PAIR) for p in range(pairs)]
    for p in range(pairs):
        value_scr[p, :PAIR, :] = qkv_ref[2, :, cols[p]].T
        value_scr[p, PAIR:, :] = jnp.ones((value_scr.shape[1] - PAIR, length), BF)

    def one_query_block(i, _):
        query_at = pl.multiple_of(i * QB, QB)
        begin, count = begin_ref[i], count_ref[i]
        query_code = query_code_ref[pl.ds(i, 1), :]
        for p in range(pairs):
            query_scr[p] = stacked_heads(qkv_ref[0, pl.ds(query_at, QB), cols[p]])

        def scores(j, tops):
            key_at = pl.multiple_of(begin + j * KB, QB)
            bias = block_bias(key_code_ref[pl.ds(key_at, KB), :], query_code, key_at, query_at)
            fresh = []
            for p in range(pairs):
                part = dot_nt(qkv_ref[1, pl.ds(key_at, KB), cols[p]], query_scr[p]) + bias
                score_scr[p, pl.ds(j * KB, KB), :] = part
                fresh.append(jnp.maximum(tops[p], top_rows(part, jnp.max)))
            return tuple(fresh)

        tops = lax.fori_loop(
            0, count, scores, tuple(jnp.full((8, 2 * QB), NEG_FILL, F32) for _ in range(pairs))
        )
        tops = [jnp.max(top, axis=0, keepdims=True) for top in tops]
        total_scr[...] = jnp.zeros_like(total_scr)

        def sums(j, _):
            key_at = pl.multiple_of(begin + j * KB, QB)
            for p in range(pairs):
                probs = jnp.exp(score_scr[p, pl.ds(j * KB, KB), :] - tops[p]).astype(BF)
                total_scr[p] += dot(value_scr[p, :, pl.ds(key_at, KB)], probs)
            return 0

        lax.fori_loop(0, count, sums, 0)
        for p in range(pairs):
            weight = total_scr[p, PAIR : PAIR + 1, :]
            logsum_ref[0, pl.ds(p * (length // QB) + i, 1), :] = tops[p] + jnp.log(weight)
            out_ref[pl.ds(query_at, QB), cols[p]] = unstack_heads(
                total_scr[p, :PAIR, :] / weight
            ).astype(BF)
        return 0

    lax.fori_loop(0, length // QB, one_query_block, 0)


def attend_forward(qkv, plan):
    _, length, width = qkv.shape
    begin, count, key_code, query_code = plan
    group = width // GROUPS
    pairs = group // PAIR
    blocks = length // QB
    return pl.pallas_call(
        attend_forward_kernel,
        name="attend_forward",
        grid_spec=pltpu.PrefetchScalarGridSpec(
            num_scalar_prefetch=2,
            grid=(GROUPS,),
            in_specs=[
                pl.BlockSpec((3, length, group), lambda g, *_: (0, 0, g)),
                pl.BlockSpec((length, PAIR), lambda g, *_: (0, 0)),
                pl.BlockSpec((blocks, QB), lambda g, *_: (0, 0)),
            ],
            out_specs=[
                pl.BlockSpec((length, group), lambda g, *_: (0, g)),
                pl.BlockSpec((1, pairs * blocks, 2 * QB), lambda g, *_: (g, 0, 0)),
            ],
            scratch_shapes=[
                pltpu.VMEM((pairs, PAIR + 16, length), BF),
                pltpu.VMEM((pairs, 2 * QB, PAIR), BF),
                pltpu.VMEM((pairs, length, 2 * QB), F32),
                pltpu.VMEM((pairs, PAIR + 16, 2 * QB), F32),
            ],
        ),
        out_shape=[
            jax.ShapeDtypeStruct((length, width), BF),
            jax.ShapeDtypeStruct((GROUPS, pairs * blocks, 2 * QB), F32),
        ],
        compiler_params=pltpu.CompilerParams(vmem_limit_bytes=VMEM),
        cost_estimate=pl.CostEstimate(
            flops=4 * length * length * width, bytes_accessed=8 * length * width, transcendentals=0
        ),
    )(begin, count, qkv, key_code, query_code)


def attend_backward_kernel(
    begin_ref, count_ref, qkv_ref, key_code_ref, query_code_ref, context_ref, logsum_ref, grad_ref,
    out_ref, sums_ref, key_scr, query_scr, given_scr, down_scr, grad_key_scr, grad_value_scr,
):
    length = qkv_ref.shape[1]
    pairs = qkv_ref.shape[2] // PAIR
    blocks = length // QB
    cols = [slice(p * PAIR, (p + 1) * PAIR) for p in range(pairs)]
    for p in range(pairs):
        key_scr[p] = qkv_ref[1, :, cols[p]].T
    grad_key_scr[...] = jnp.zeros_like(grad_key_scr)
    grad_value_scr[...] = jnp.zeros_like(grad_value_scr)
    sums_ref[...] = jnp.zeros_like(sums_ref)

    def one_query_block(i, _):
        query_at = pl.multiple_of(i * QB, QB)
        begin, count = begin_ref[i], count_ref[i]
        query_code = query_code_ref[pl.ds(i, 1), :]
        inner, logsum = [], []
        for p in range(pairs):
            query_scr[p] = stacked_heads(qkv_ref[0, pl.ds(query_at, QB), cols[p]])
            given = grad_ref[pl.ds(query_at, QB), cols[p]]
            given_scr[p] = stacked_heads(given)
            both = (given.astype(F32) * context_ref[pl.ds(query_at, QB), cols[p]].astype(F32)).T
            inner.append(
                jnp.concatenate(
                    [
                        jnp.sum(both[:HEAD], axis=0, keepdims=True),
                        jnp.sum(both[HEAD:], axis=0, keepdims=True),
                    ],
                    axis=1,
                )
            )
            logsum.append(logsum_ref[0, pl.ds(p * blocks + i, 1), :])
        down_scr[...] = jnp.zeros_like(down_scr)

        def one_key_block(j, _):
            key_at = pl.multiple_of(begin + j * KB, QB)
            rows = pl.ds(key_at, KB)
            bias = block_bias(key_code_ref[rows, :], query_code, key_at, query_at)
            for p in range(pairs):
                part = dot_nt(qkv_ref[1, rows, cols[p]], query_scr[p]) + bias
                probs = jnp.exp(part - logsum[p])
                grad_probs = dot_nt(qkv_ref[2, rows, cols[p]], given_scr[p])
                grad_scores = (probs * (grad_probs - inner[p])).astype(BF)
                grad_value_scr[rows, cols[p]] += dot(probs.astype(BF), given_scr[p])
                grad_key_scr[rows, cols[p]] += dot(grad_scores, query_scr[p])
                down_scr[p] += dot(key_scr[p, :, rows], grad_scores)
            return 0

        lax.fori_loop(0, count, one_key_block, 0)
        for p in range(pairs):
            grad_query = (unstack_heads(down_scr[p]) * (HEAD**-0.5)).astype(BF)
            out_ref[0, pl.ds(query_at, QB), cols[p]] = grad_query
            sums_ref[0, 0:1, cols[p]] += jnp.sum(grad_query.astype(F32), axis=0, keepdims=True)
        return 0

    lax.fori_loop(0, blocks, one_query_block, 0)
    out_ref[1] = grad_key_scr[...].astype(BF)
    grad_value = grad_value_scr[...].astype(BF)
    out_ref[2] = grad_value
    sums_ref[0, 1:2, :] = jnp.sum(grad_value.astype(F32), axis=0, keepdims=True)


def attend_backward(qkv, context, logsum, grad_context, plan):
    _, length, width = qkv.shape
    begin, count, key_code, query_code = plan
    group = width // GROUPS
    pairs = group // PAIR
    blocks = length // QB
    return pl.pallas_call(
        attend_backward_kernel,
        name="attend_backward",
        grid_spec=pltpu.PrefetchScalarGridSpec(
            num_scalar_prefetch=2,
            grid=(GROUPS,),
            in_specs=[
                pl.BlockSpec((3, length, group), lambda g, *_: (0, 0, g)),
                pl.BlockSpec((length, PAIR), lambda g, *_: (0, 0)),
                pl.BlockSpec((blocks, QB), lambda g, *_: (0, 0)),
                pl.BlockSpec((length, group), lambda g, *_: (0, g)),
                pl.BlockSpec((1, pairs * blocks, 2 * QB), lambda g, *_: (g, 0, 0)),
                pl.BlockSpec((length, group), lambda g, *_: (0, g)),
            ],
            out_specs=[
                pl.BlockSpec((3, length, group), lambda g, *_: (0, 0, g)),
                pl.BlockSpec((1, 2, group), lambda g, *_: (g, 0, 0)),
            ],
            scratch_shapes=[
                pltpu.VMEM((pairs, PAIR, length), BF),
                pltpu.VMEM((pairs, 2 * QB, PAIR), BF),
                pltpu.VMEM((pairs, 2 * QB, PAIR), BF),
                pltpu.VMEM((pairs, PAIR, 2 * QB), F32),
                pltpu.VMEM((length, group), F32),
                pltpu.VMEM((length, group), F32),
            ],
        ),
        out_shape=[
            jax.ShapeDtypeStruct((3, length, width), BF),
            jax.ShapeDtypeStruct((GROUPS, 2, group), F32),
        ],
        compiler_params=pltpu.CompilerParams(vmem_limit_bytes=VMEM),
        cost_estimate=pl.CostEstimate(
            flops=10 * length * length * width, bytes_accessed=16 * length * width, transcendentals=0
        ),
    )(begin, count, qkv, key_code, query_code, context, logsum, grad_context)


def mix_kernel(x_ref, w_ref, small_ref, out_ref):
    part = pl.program_id(0)
    width = x_ref.shape[1]
    ff_width = small_ref.shape[2] - 8 * width
    at = ff_width + width * jnp.where(part == 2, 1, 0)
    shift = small_ref[0, :, pl.ds(pl.multiple_of(at, 128), width)]
    shift = jnp.where(part == 1, jnp.zeros_like(shift), shift)
    scale = jnp.where(part == 0, HEAD**-0.5, 1.0)
    for r in range(0, x_ref.shape[0], 256):
        rows = slice(r, r + 256)
        out_ref[0, rows, :] = ((dot(x_ref[rows, :], w_ref[0]) + shift) * scale).astype(BF)


def mix(x, w_qkv, small, layer):
    length, width = x.shape
    return pl.pallas_call(
        mix_kernel,
        name="mix",
        grid=(3,),
        in_specs=[
            pl.BlockSpec((length, width), lambda c: (0, 0)),
            pl.BlockSpec((1, width, width), lambda c: (layer, 0, c)),
            small_spec(layer, small.shape[2]),
        ],
        out_specs=pl.BlockSpec((1, length, width), lambda c: (c, 0, 0)),
        out_shape=jax.ShapeDtypeStruct((3, length, width), BF),
        compiler_params=pltpu.CompilerParams(vmem_limit_bytes=VMEM),
        cost_estimate=pl.CostEstimate(
            flops=6 * length * width * width, bytes_accessed=14 * length * width, transcendentals=0
        ),
    )(x, w_qkv, small)


def unmix_kernel(grad_ref, w_ref, skip_ref, out_ref, total):
    part = pl.program_id(0)

    @pl.when(part == 0)
    def _():
        total[...] = skip_ref[...].astype(F32)

    for r in range(0, total.shape[0], 256):
        rows = slice(r, r + 256)
        total[rows, :] += dot_nt(grad_ref[0, rows, :], w_ref[0])

    @pl.when(part == 2)
    def _():
        out_ref[...] = total[...].astype(BF)


def unmix(grad_mixed, w_qkv, skip, layer):
    _, length, width = grad_mixed.shape
    return pl.pallas_call(
        unmix_kernel,
        name="unmix",
        grid=(3,),
        in_specs=[
            pl.BlockSpec((1, length, width), lambda c: (c, 0, 0)),
            pl.BlockSpec((1, width, width), lambda c: (layer, 0, c)),
            pl.BlockSpec((length, width), lambda c: (0, 0)),
        ],
        out_specs=pl.BlockSpec((length, width), lambda c: (0, 0)),
        out_shape=jax.ShapeDtypeStruct((length, width), BF),
        scratch_shapes=[pltpu.VMEM((length, width), F32)],
        compiler_params=pltpu.CompilerParams(vmem_limit_bytes=VMEM),
        cost_estimate=pl.CostEstimate(
            flops=6 * length * width * width, bytes_accessed=14 * length * width, transcendentals=0
        ),
    )(grad_mixed, w_qkv, skip)


def normalized(values):
    centred = values - jnp.mean(values, axis=-1, keepdims=True)
    inverse = lax.rsqrt(jnp.mean(centred * centred, axis=-1, keepdims=True) + EPS_NORM)
    return (centred * inverse, inverse)


def normalized_pull(grad_hat, hat, inverse):
    return inverse * (
        grad_hat
        - jnp.mean(grad_hat, axis=-1, keepdims=True)
        - hat * jnp.mean(grad_hat * hat, axis=-1, keepdims=True)
    )


ERF = (0.254829592, -0.284496736, 1.421413741, -1.453152027, 1.061405429)
ERF_SLOPE = 0.3275911


def gelu_parts(x):
    t = pl.reciprocal(1.0 + (ERF_SLOPE * math.sqrt(0.5)) * jnp.abs(x), approx=True)
    bell = jnp.exp(-0.5 * (x * x))
    tail = 0.5 * ERF[4]
    for term in ERF[3::-1]:
        tail = tail * t + 0.5 * term
    tail = tail * t * bell
    below = jnp.where(x >= 0, 1.0 - tail, tail)
    return (x * below, below + x * bell * (1.0 / math.sqrt(2.0 * math.pi)))


FB = 512
ROWS = 256


def small_slices(width, ff_width):
    names = ("b_q", "b_v", "b_out", "gain1", "gain2", "shift1", "shift2", "b_down")
    at = {"b_up": slice(0, ff_width)}
    for n, name in enumerate(names):
        at[name] = slice(ff_width + n * width, ff_width + (n + 1) * width)
    return at


def refine_kernel(
    x_ref, context_ref, w_out_ref, w_up_ref, w_down_ref, small_ref, b_up_ref,
    out_ref, hidden_ref, hat1_ref, hat2_ref, scale1_ref, scale2_ref, active_ref, slope_ref,
    total,
):
    step = pl.program_id(0)
    length, width = x_ref.shape
    at = small_slices(width, small_ref.shape[2] - 8 * width)

    def vector(name):
        return small_ref[0, :, at[name]]

    @pl.when(step == 0)
    def _():
        for r in range(0, length, ROWS):
            rows = slice(r, r + ROWS)
            summed = x_ref[rows, :].astype(F32) + dot(context_ref[rows, :], w_out_ref[0])
            hat, inverse = normalized(summed + vector("b_out"))
            hidden = hat * vector("gain1") + vector("shift1")
            hat1_ref[rows, :] = hat.astype(BF)
            scale1_ref[rows, :] = jnp.broadcast_to(inverse, (ROWS, 128))
            hidden_ref[rows, :] = hidden.astype(BF)
            total[rows, :] = hidden + vector("b_down")

    for r in range(0, length, ROWS):
        rows = slice(r, r + ROWS)
        raised = dot(hidden_ref[rows, :], w_up_ref[0]) + b_up_ref[0]
        active, slope = gelu_parts(raised)
        active = active.astype(BF)
        active_ref[rows, :] = active
        slope_ref[rows, :] = slope.astype(BF)
        total[rows, :] += dot(active, w_down_ref[0])

    @pl.when(step == pl.num_programs(0) - 1)
    def _():
        for r in range(0, length, ROWS):
            rows = slice(r, r + ROWS)
            hat, inverse = normalized(total[rows, :])
            hat2_ref[rows, :] = hat.astype(BF)
            scale2_ref[rows, :] = jnp.broadcast_to(inverse, (ROWS, 128))
            out_ref[rows, :] = (hat * vector("gain2") + vector("shift2")).astype(BF)


def refine(x, context, weights, layer):
    w_out, w_up, w_down, small = weights
    length, width = x.shape
    ff_width = w_up.shape[2]
    whole = pl.BlockSpec((length, width), lambda f: (0, 0))
    lanes = pl.BlockSpec((length, 128), lambda f: (0, 0))
    part = pl.BlockSpec((length, FB), lambda f: (0, f))
    row_shape = jax.ShapeDtypeStruct((length, width), BF)
    lane_shape = jax.ShapeDtypeStruct((length, 128), F32)
    ff_shape = jax.ShapeDtypeStruct((length, ff_width), BF)
    return pl.pallas_call(
        refine_kernel,
        name="refine",
        grid=(ff_width // FB,),
        in_specs=[
            whole,
            whole,
            pl.BlockSpec((1, width, width), lambda f: (layer, 0, 0)),
            pl.BlockSpec((1, width, FB), lambda f: (layer, 0, f)),
            pl.BlockSpec((1, FB, width), lambda f: (layer, f, 0)),
            small_spec(layer, small.shape[2]),
            pl.BlockSpec((1, 1, FB), lambda f: (layer, 0, f)),
        ],
        out_specs=[whole, whole, whole, whole, lanes, lanes, part, part],
        out_shape=[row_shape] * 4 + [lane_shape] * 2 + [ff_shape] * 2,
        scratch_shapes=[pltpu.VMEM((length, width), F32)],
        compiler_params=pltpu.CompilerParams(vmem_limit_bytes=VMEM),
        cost_estimate=pl.CostEstimate(
            flops=2 * length * width * (width + 2 * ff_width),
            bytes_accessed=2 * width * (width + 2 * ff_width) + 4 * length * ff_width,
            transcendentals=0,
        ),
    )(x, context, w_out, w_up, w_down, small, small)


def refine_back_kernel(
    grad_ref, hat1_ref, hat2_ref, scale1_ref, scale2_ref, slope_ref,
    w_out_ref, w_up_ref, w_down_ref, small_ref,
    grad_low_ref, grad_raised_ref, grad_attn_ref, grad_context_ref, sums_ref, up_sums_ref,
    total,
):
    step = pl.program_id(0)
    length, width = grad_ref.shape
    at = small_slices(width, small_ref.shape[2] - 8 * width)

    def vector(name):
        return small_ref[0, :, at[name]]

    def add(row, values, first):
        part = jnp.sum(values, axis=0, keepdims=True)
        sums_ref[row : row + 1, :] = part if first else sums_ref[row : row + 1, :] + part

    @pl.when(step == 0)
    def _():
        for r in range(0, length, ROWS):
            rows = slice(r, r + ROWS)
            grad = grad_ref[rows, :].astype(F32)
            hat = hat2_ref[rows, :].astype(F32)
            joined = normalized_pull(grad * vector("gain2"), hat, scale2_ref[rows, :1])
            low = joined.astype(BF)
            grad_low_ref[rows, :] = low
            total[rows, :] = joined
            add(2, grad * hat, r == 0)
            add(4, grad, r == 0)
            add(5, low.astype(F32), r == 0)

    for r in range(0, length, ROWS):
        rows = slice(r, r + ROWS)
        grad_active = dot_nt(grad_low_ref[rows, :], w_down_ref[0])
        raised = (grad_active * slope_ref[rows, :].astype(F32)).astype(BF)
        grad_raised_ref[rows, :] = raised
        part = jnp.sum(raised.astype(F32), axis=0, keepdims=True)
        up_sums_ref[...] = part if r == 0 else up_sums_ref[...] + part
        total[rows, :] += dot_nt(raised, w_up_ref[0])

    @pl.when(step == pl.num_programs(0) - 1)
    def _():
        for r in range(0, length, ROWS):
            rows = slice(r, r + ROWS)
            grad = total[rows, :]
            hat = hat1_ref[rows, :].astype(F32)
            summed = normalized_pull(grad * vector("gain1"), hat, scale1_ref[rows, :1])
            attn = summed.astype(BF)
            grad_attn_ref[rows, :] = attn
            grad_context_ref[rows, :] = dot_nt(attn, w_out_ref[0]).astype(BF)
            add(1, grad * hat, r == 0)
            add(3, grad, r == 0)
            add(0, attn.astype(F32), r == 0)


def refine_back(grad, kept, weights, layer):
    w_out, w_up, w_down, small = weights
    hat1, hat2, scale1, scale2, slope = kept
    length, width = grad.shape
    ff_width = w_up.shape[2]
    whole = pl.BlockSpec((length, width), lambda f: (0, 0))
    lanes = pl.BlockSpec((length, 128), lambda f: (0, 0))
    part = pl.BlockSpec((length, FB), lambda f: (0, f))
    row_shape = jax.ShapeDtypeStruct((length, width), BF)
    return pl.pallas_call(
        refine_back_kernel,
        name="refine_back",
        grid=(ff_width // FB,),
        in_specs=[
            whole, whole, whole, lanes, lanes, part,
            pl.BlockSpec((1, width, width), lambda f: (layer, 0, 0)),
            pl.BlockSpec((1, width, FB), lambda f: (layer, 0, f)),
            pl.BlockSpec((1, FB, width), lambda f: (layer, f, 0)),
            small_spec(layer, small.shape[2]),
        ],
        out_specs=[
            whole, part, whole, whole,
            pl.BlockSpec((6, width), lambda f: (0, 0)),
            pl.BlockSpec((1, FB), lambda f: (0, f)),
        ],
        out_shape=[
            row_shape,
            jax.ShapeDtypeStruct((length, ff_width), BF),
            row_shape,
            row_shape,
            jax.ShapeDtypeStruct((6, width), F32),
            jax.ShapeDtypeStruct((1, ff_width), F32),
        ],
        scratch_shapes=[pltpu.VMEM((length, width), F32)],
        compiler_params=pltpu.CompilerParams(vmem_limit_bytes=VMEM),
        cost_estimate=pl.CostEstimate(
            flops=2 * length * width * (width + 2 * ff_width),
            bytes_accessed=2 * width * (width + 2 * ff_width) + 4 * length * ff_width,
            transcendentals=0,
        ),
    )(grad, hat1, hat2, scale1, scale2, slope, w_out, w_up, w_down, small)


def layer_forward(x, weights, layer, plan):
    w_qkv, w_out, w_up, w_down, small = weights
    qkv = mix(x, w_qkv, small, layer)
    context, logsum = attend_forward(qkv, plan)
    out, hidden, hat1, hat2, scale1, scale2, active, slope = refine(
        x, context, (w_out, w_up, w_down, small), layer
    )
    return (out, (x, qkv, context, logsum, hidden, hat1, hat2, scale1, scale2, active, slope))


def layer_backward(grad, kept, weights, layer, plan):
    w_qkv, w_out, w_up, w_down, small = weights
    x, qkv, context, logsum, hidden, hat1, hat2, scale1, scale2, active, slope = kept
    grad_low, grad_raised, grad_attn, grad_context, sums, up_sums = refine_back(
        grad, (hat1, hat2, scale1, scale2, slope), (w_out, w_up, w_down, small), layer
    )
    grad_mixed, mix_sums = attend_backward(qkv, context, logsum, grad_context, plan)
    grad_x = unmix(grad_mixed, w_qkv, grad_attn, layer)
    return (grad_x, (grad_low, grad_raised, grad_attn, grad_mixed), (sums, up_sums, mix_sums))


CORE_PAIRS = ((0, 1), (1, 0), (2, 3), (3, 2))


def pair_gather(value):
    return lax.all_gather(value, "section", axis_index_groups=[[0, 1], [2, 3]])


def send(value, routes):
    return lax.ppermute(value, "section", routes)


def swap_cores(value):
    return send(value, CORE_PAIRS)


def keep_half(value, core, axis):
    width = value.shape[axis] // 2
    return lax.dynamic_slice_in_dim(value, core * width, width, axis)


def weight_parts(kept, grads, half):
    x, context, hidden, active = kept[0], kept[2], kept[4], kept[9]
    grad_low, grad_raised, grad_attn, grad_mixed = grads

    def product(rows, cols):
        return dot_tn(rows, keep_half(cols, half, cols.ndim - 1)).astype(BF)

    return (
        product(active, grad_low),
        product(hidden, grad_raised),
        product(context, grad_attn),
        jnp.concatenate([product(x, grad_mixed[c]) for c in range(3)], axis=1),
    )


def sum_shards(kept, grads, core):
    theirs = weight_parts(kept, grads, 1 - core)
    arrived = [swap_cores(part) for part in theirs]
    mine = weight_parts(kept, grads, core)
    both = [(a.astype(F32) + b.astype(F32)).astype(BF) for a, b in zip(mine, arrived)]
    return [lax.psum_scatter(part, "dp", scatter_dimension=0, tiled=True) for part in both]


def small_sums(sums):
    sums, up_sums, mix_sums = sums
    rows = [up_sums[0], mix_sums.transpose(1, 0, 2).reshape(-1)]
    rows += [sums[n] for n in range(6)]
    shards = lax.axis_size("dp")
    return jnp.concatenate([row.reshape(shards, -1) for row in rows], axis=1)


def body(
    tokens_in, seg_starts, pad_mask, w_qkv, b_qv, w_attn_out, b_attn_out, ln_gain, ln_bias,
    w_up, b_up, w_down, b_down, w_proj, cotangent,
):
    section_at = lax.axis_index("section")
    core = section_at % 2
    is_late = section_at >= 2
    quarter = tokens_in.shape[1]
    length, width = 4 * quarter, tokens_in.shape[2]
    ff_width = w_up.shape[2]

    own = tokens_in[core]
    other = tokens_in[1 - core]
    near = swap_cores(other)
    straight = send(own, [(2, 0), (3, 1)])
    crossed = send(other, [(2, 1), (3, 0)])
    flip = core == 1
    x = jnp.concatenate(
        [
            jnp.where(flip, near, own),
            jnp.where(flip, own, near),
            jnp.where(flip, crossed, straight),
            jnp.where(flip, straight, crossed),
        ],
        axis=0,
    )
    small = pack_small(b_qv[0], b_attn_out[0], ln_gain[0], ln_bias[0], b_up[0], b_down[0])
    small = pair_gather(small[None])
    weights = (
        pair_gather(w_qkv[0]),
        pair_gather(w_attn_out[0]),
        pair_gather(w_up[0]),
        pair_gather(w_down[0]),
        small,
    )
    projection = lax.all_gather(w_proj, "section", axis=1, tiled=True)
    target = lax.all_gather(cotangent, "section", axis=2, tiled=True)[core]
    plan = attention_plan(seg_starts[core], pad_mask[core])

    def both_forward(rows):
        middle, kept_even = layer_forward(rows, weights, 0, plan)
        last, kept_odd = layer_forward(middle, weights, 1, plan)
        return (last, kept_even, kept_odd)

    early = both_forward(x)
    hopped = send(early[0], [(0, 2), (1, 3)])
    last, kept_even, kept_odd = lax.cond(
        is_late, lambda rows, _: both_forward(rows), lambda _, state: state, hopped, early
    )

    def head(rows):
        factor = math.sqrt(projection.shape[1])
        columns = dot(rows, projection)
        given = target.astype(F32)
        inverse = lax.rsqrt(jnp.sum(columns * columns, axis=1, keepdims=True) + EPS_PROJ)
        cross = jnp.sum(columns * given, axis=1, keepdims=True)
        embedded = (factor * columns * inverse).astype(BF)
        grad_columns = (factor * (given * inverse - columns * cross * inverse**3)).astype(BF)
        return (embedded, dot_tn(rows, grad_columns), dot_nt(grad_columns, projection).astype(BF))

    def layer_zero():
        row = jnp.zeros((length, width), BF)
        return (
            row,
            (row, jnp.zeros((length, ff_width), BF), row, jnp.zeros((3, length, width), BF)),
            (
                jnp.zeros((6, width), F32),
                jnp.zeros((1, ff_width), F32),
                jnp.zeros((GROUPS, 2, width // GROUPS), F32),
            ),
        )

    def back_late(rows):
        embedded, grad_proj, grad_last = head(rows)
        grad, grads_odd, sums_odd = layer_backward(grad_last, kept_odd, weights, 1, plan)
        grad, grads_even, sums_even = layer_backward(grad, kept_even, weights, 0, plan)
        return (embedded, grad_proj, grad, grads_odd, sums_odd, grads_even, sums_even)

    def back_none(rows):
        embedded = jnp.zeros((length, projection.shape[1]), BF)
        grad_proj = jnp.zeros(projection.shape, F32)
        grad, grads_odd, sums_odd = layer_zero()
        _, grads_even, sums_even = layer_zero()
        return (embedded, grad_proj, grad, grads_odd, sums_odd, grads_even, sums_even)

    embedded, grad_proj, grad_mid, grads_odd, sums_odd, grads_even, sums_even = lax.cond(
        is_late, back_late, back_none, last
    )
    hopped = send(grad_mid, [(2, 0), (3, 1)])

    def back_one(kept, layer):
        return lambda grad, late: layer_backward(grad, kept, weights, layer, plan)

    grad, grads_odd, sums_odd = lax.cond(
        is_late, lambda _, late: late, back_one(kept_odd, 1), hopped, (hopped, grads_odd, sums_odd)
    )
    shards_odd = sum_shards(kept_odd, grads_odd, core)
    grad, grads_even, sums_even = lax.cond(
        is_late, lambda _, late: late, back_one(kept_even, 0), grad, (grad, grads_even, sums_even)
    )
    shards_even = sum_shards(kept_even, grads_even, core)

    def owned(even, odd):
        mine = jnp.where(flip, odd, even)
        arrived = swap_cores(jnp.where(flip, even, odd))
        parts = (mine, arrived)
        return (jnp.where(flip, parts[1], parts[0]), jnp.where(flip, parts[0], parts[1]))

    owned_parts = [owned(even, odd) for even, odd in zip(shards_even, shards_odd)]

    def joined(pair):
        return jnp.concatenate(pair, axis=1).astype(F32)[None]

    grad_w_down, grad_w_up, grad_w_out = [joined(pair) for pair in owned_parts[:3]]
    first, second = owned_parts[3]
    third = first.shape[1] // 3
    pieces = []
    for c in range(3):
        pieces += [first[:, c * third : (c + 1) * third], second[:, c * third : (c + 1) * third]]
    grad_w_qkv = jnp.concatenate(pieces, axis=1).astype(F32)[None]

    small_even, small_odd = small_sums(sums_even), small_sums(sums_odd)
    small_mine = jnp.where(flip, small_odd, small_even) + swap_cores(
        jnp.where(flip, small_even, small_odd)
    )
    small_mine = lax.psum_scatter(small_mine, "dp", scatter_dimension=0, tiled=True)[0]
    share = width // lax.axis_size("dp")
    at = ff_width // lax.axis_size("dp")
    grad_b_up = small_mine[None, :at]
    grad_b_qv = small_mine[None, at : at + 2 * share]
    rows = small_mine[at + 2 * share :].reshape(6, share)

    shards = lax.axis_size("dp")
    proj_cols = w_proj.shape[1]
    grad_proj = grad_proj.reshape(shards, share, 4, proj_cols).transpose(2, 0, 1, 3)
    grad_w_proj = lax.psum_scatter(
        grad_proj.reshape(4 * shards, share * proj_cols),
        ("section", "dp"),
        scatter_dimension=0,
        tiled=True,
    ).reshape(share, proj_cols)

    spread = lax.all_gather(embedded, "section")[2:]
    embedded_out = lax.dynamic_slice_in_dim(spread, section_at * proj_cols, proj_cols, 2)

    quarters = grad.reshape(4, quarter, width)
    own_grad = quarters[core]
    near_grad = swap_cores(quarters[1 - core])
    straight_grad = send(quarters[2 + core], [(0, 2), (1, 3)])
    crossed_grad = send(quarters[3 - core], [(0, 3), (1, 2)])
    mine = jnp.where(is_late, straight_grad, own_grad)
    others = jnp.where(is_late, crossed_grad, near_grad)
    grad_in = jnp.stack(
        [jnp.where(flip, others, mine), jnp.where(flip, mine, others)]
    ).astype(F32)

    return (
        embedded_out,
        grad_in,
        grad_w_qkv,
        grad_b_qv,
        grad_w_out,
        rows[0][None],
        rows[1:3][None],
        rows[3:5][None],
        grad_w_up,
        grad_b_up,
        grad_w_down,
        rows[5][None],
        grad_w_proj,
    )


def solution(mesh):
    in_specs = (
        P("dp", "section", None),
        P("dp", None),
        P("dp", None),
        P("section", None, None),
        P("section", None),
        P("section", None, None),
        P("section", None),
        P("section", None, None),
        P("section", None, None),
        P("section", None, None),
        P("section", None),
        P("section", None, None),
        P("section", None),
        P(None, "section"),
        P("dp", None, "section"),
    )
    out_specs = (
        P("dp", None, "section"),
        P("dp", "section", None),
        P("section", "dp", None),
        P("section", "dp"),
        P("section", "dp", None),
        P("section", "dp"),
        P("section", None, "dp"),
        P("section", None, "dp"),
        P("section", "dp", None),
        P("section", "dp"),
        P("section", "dp", None),
        P("section", "dp"),
        P("dp", "section"),
    )
    return jax.shard_map(body, mesh=mesh, in_specs=in_specs, out_specs=out_specs, check_vma=False)
```

time: 4120 us -> 1270 us (0.31)
  waiting for transfers between devices: 1560 us -> 610 us
  local copies, waits for them, and re-layouts: 675 us -> 46.2 us
  other arithmetic: 630 us -> 23.9 us
  starting transfers between devices: 577 us -> 23.1 us
  matrix products: 605 us -> 75.4 us
  Pallas kernels: 0 us -> 387 us
  blocking collectives: 9.63 us -> 77 us
    ppermute x10 -> x21, starting transfers between devices: 576 us -> 21.6 us  [send(): return lax.ppermute(value, 'section', routes)]
    dot_general x54 -> x27, matrix products: 603 us -> 75.4 us  [the longest x25 71.8 us: dot_tn(): return lax.dot_general(a, b, TN, preferred_element_type=F32)]
    unnamed x22 -> x17, waiting for transfers between devices: 634 us -> 150 us
    pallas_call x0 -> x18, Pallas kernels: none -> 387 us  [the longest x4 117 us: refine(): pl.pallas_call(refine_kernel, name='refine', grid=(ff_width // FB,), in_s...]
    reduce_scatter x5 -> x6, waiting for transfers between devices: 575 us -> 279 us  [sum_shards(): lax.psum_scatter(part, 'dp', scatter_dimension=0, tiled=True)]
    dynamic_slice x75 -> x1, local copies, waits for them, and re-layouts: 191 us -> 0.21 us  [body(): lax.dynamic_slice_in_dim(spread, section_at * proj_cols, proj_cols, 2)]
    add x40 -> x1, other arithmetic: 177 us -> 0.01 us  [body(): jnp.where(flip, small_odd, small_even)]
    dynamic_update_slice x50 -> x0, local copies, waits for them, and re-layouts: 148 us -> none  [the longest x40 138 us: forward_tick(): lax.dynamic_update_index_in_dim(buffer, jnp.where(is_live, fresh_part, bu...]
  transfers between devices with their start and end apart: 25 -> 35, of which waited for: 15 -> 17; matrix products, arithmetic and copies ran while one was open for 34% -> 10% of each run, Pallas kernels for 0% -> 2%
where the time goes in v1:
time: 1270 us; the launch traced here: 1260 us
  waiting for transfers between devices  610 us (48%)
  Pallas kernels  387 us (30%)
  blocking collectives  77 us (6%)
  matrix products  75.4 us (6%)
  local copies, waits for them, and re-layouts  46.2 us (4%)
  other arithmetic  23.9 us (2%)
  starting transfers between devices  23.1 us (2%)
  between operations  15.4 us (1%)
    reduce_scatter x6, waiting for transfers between devices, sum_shards(): lax.psum_scatter(part, 'dp', scatter_dimension=0, tiled=True)  279 us
    ppermute x21, waiting for transfers between devices, send(): return lax.ppermute(value, 'section', routes)  152 us
    unnamed x17, waiting for transfers between devices  150 us
    pallas_call x4, Pallas kernels, refine(): pl.pallas_call(refine_kernel, name='refine', grid=(ff_width // FB,), in_s...  117 us
    pallas_call x4, Pallas kernels, attend_forward(): pl.pallas_call(attend_forward_kernel, name='attend_forward', grid_spec=pl...  96.8 us
    pallas_call x2, Pallas kernels, attend_backward(): pl.pallas_call(attend_backward_kernel, name='attend_backward', grid_spec=...  80.5 us
    dot_general x25, matrix products, dot_tn(): return lax.dot_general(a, b, TN, preferred_element_type=F32)  71.8 us
    pallas_call x2, Pallas kernels, refine_back(): pl.pallas_call(refine_back_kernel, name='refine_back', grid=(ff_width //...  49.2 us
  transfers between devices with their start and end apart: 35, of which 17 were waited for; matrix products, arithmetic and copies ran while one was open for 10% of the time, Pallas kernels for 2%

profile of v1, /device:TPU:13, one launch (start us, length us, event | category | flops | bytes accessed | tf_op | source)
XLA Modules:
  0.0 1259.2 jit_solution(3747843942506170055)
XLA Ops:
  21.7 8.4 collective-permute-done.2
  38.7 24.0 %attend_forward.6 = (bf16[1024,768]{1,0:T(8,128)(2,1)}, f32[2,24,256]{2,1,0:T(8,128)}) custom-call(s32[8]{0:T(128)S(1)} %get-tuple-element.865.begin_ref, s32[8]{0:T(128)S(1)} %get-tuple-element.866.count_ref, bf16[3,1024,768]{2,1,0:T(8,128)(2,1)S(1)} %mix.6.qkv_ref, f32[1024,128]{1,0:T(8,128)} %broadcast_in_dim.46.key_code_ref, ...), custom_call_target="tpu_custom_call" | custom-call | flops 3221225472 | bytes 6291456 | tf_op jit(solution)/shard_map/attend_forward/pallas_call | solution.py:153
  67.7 24.5 %all-gather.14.cloned.1.call-done.w_down_ref = bf16[2,3072,768]{2,1,0:T(8,128)(2,1)} async-done(((bf16[1,3072,768]{2,1,0:T(8,128)(2,1)}), bf16[2,3072,768]{2,1,0:T(8,128)(2,1)}) %all-gather.14.cloned.1.call-update) | async-done | bytes 9437200 | tf_op jit(solution)/shard_map/all_gather | solution.py:606
  92.2 29.9 %refine.6 = (bf16[1024,768]{1,0:T(8,128)(2,1)}, bf16[1024,768]{1,0:T(8,128)(2,1)}, bf16[1024,768]{1,0:T(8,128)(2,1)}, bf16[1024,768]{1,0:T(8,128)(2,1)}, f32[102...) custom-call(bf16[1024,768]{1,0:T(8,128)(2,1)} %copy-done.5, ...), custom_call_target="tpu_custom_call" | custom-call | flops 10871635968 | bytes 23199744 | tf_op jit(solution)/shard_map/refine/pallas_call | solution.py:458
  129.1 24.2 %attend_forward.7 = (bf16[1024,768]{1,0:T(8,128)(2,1)S(1)}, f32[2,24,256]{2,1,0:T(8,128)}) custom-call(s32[8]{0:T(128)S(1)} %get-tuple-element.865.begin_ref, s32[8]{0:T(128)S(1)} %get-tuple-element.866.count_ref, bf16[3,1024,768]{2,1,0:T(8,128)(2,1)} %mix.7.qkv_ref, f32[1024,128]{1,0:T(8,128)} %broadcast_in_dim.46.key_code_ref, ...), custom_call_target="tpu_custom_call" | custom-call | flops 3221225472 | bytes 6291456 | tf_op jit(solution)/shard_map/attend_forward/pallas_call | solution.py:153
  153.4 28.5 %refine.7 = (bf16[1024,768]{1,0:T(8,128)(2,1)S(1)}, bf16[1024,768]{1,0:T(8,128)(2,1)}, bf16[1024,768]{1,0:T(8,128)(2,1)}, bf16[1024,768]{1,0:T(8,128)(2,1)}, f32...) custom-call(bf16[1024,768]{1,0:T(8,128)(2,1)S(1)} %copy-done.9, ...), custom_call_target="tpu_custom_call" | custom-call | flops 10871635968 | bytes 23199744 | tf_op jit(solution)/shard_map/refine/pallas_call | solution.py:458
  183.2 39.1 %all_gather.32 = bf16[768,128]{0,1:T(8,128)(2,1)S(1)} all-gather(bf16[768,32]{0,1:T(8,128)(2,1)} %param.36), channel_id=1, replica_groups=mesh['section'=4,'dp'=8] {'section'}, dimensions={1}, use_global_device_ids=true | all-gather | bytes 245760 | tf_op jit(solution)/shard_map/all_gather | solution.py:688
  222.3 7.7 all_gather.33
  230.1 123.9 %conditional.4 = ((bf16[1024,768]{1,0:T(8,128)(2,1)S(1)}, bf16[1024,768]{1,0:T(8,128)(2,1)}, bf16[3,1024,768]{2,1,0:T(8,128)(2,1)}, bf16[1024,768]{1,0:T(8,128)(...) conditional(s32[]{:T(128)} %convert_element_type.228, ...), branch_computations={%region_3.4_spmd, %region_4.5_spmd} | conditional | flops 35433480192 | bytes 137888320 | solution.py:699
  230.1 7.8 mix.4.qkv_ref
  238.0 24.3 %attend_forward.4 = (bf16[1024,768]{1,0:T(8,128)(2,1)}, f32[2,24,256]{2,1,0:T(8,128)}) custom-call(s32[8]{0:T(128)S(1)} %get-tuple-element.274.begin_ref, s32[8]{0:T(128)S(1)} %copy-done.48, bf16[3,1024,768]{2,1,0:T(8,128)(2,1)} %mix.4.qkv_ref, f32[1024,128]{1,0:T(8,128)S(1)} %copy-done.28, f32[8,128]{1,0:T(8,128)S(1)} %get-tuple-element.279.query_code_ref), custom_call_target="tpu_custom_call" | custom-call | flops 3221225472 | bytes 6291456 | tf_op jit(solution)/shard_map/cond/branch_1_fun/attend_forward/pallas_call | solution.py:153
  262.2 29.9 %refine.4 = (bf16[1024,768]{1,0:T(8,128)(2,1)}, bf16[1024,768]{1,0:T(8,128)(2,1)}, bf16[1024,768]{1,0:T(8,128)(2,1)}, bf16[1024,768]{1,0:T(8,128)(2,1)}, f32[102...) custom-call(bf16[1024,768]{1,0:T(8,128)(2,1)} %copy-done.7, ...), custom_call_target="tpu_custom_call" | custom-call | flops 10871635968 | bytes 23199744 | tf_op jit(solution)/shard_map/cond/branch_1_fun/refine/pallas_call | solution.py:458
  299.2 24.3 %attend_forward.5 = (bf16[1024,768]{1,0:T(8,128)(2,1)}, f32[2,24,256]{2,1,0:T(8,128)}) custom-call(s32[8]{0:T(128)S(1)} %get-tuple-element.274.begin_ref, s32[8]{0:T(128)S(1)} %copy-done.48, bf16[3,1024,768]{2,1,0:T(8,128)(2,1)} %mix.5.qkv_ref, f32[1024,128]{1,0:T(8,128)S(1)} %copy-done.29, f32[8,128]{1,0:T(8,128)S(1)} %get-tuple-element.279.query_code_ref), custom_call_target="tpu_custom_call" | custom-call | flops 3221225472 | bytes 6291456 | tf_op jit(solution)/shard_map/cond/branch_1_fun/attend_forward/pallas_call | solution.py:153
  323.5 28.9 %refine.5 = (bf16[1024,768]{1,0:T(8,128)(2,1)S(1)}, bf16[1024,768]{1,0:T(8,128)(2,1)}, bf16[1024,768]{1,0:T(8,128)(2,1)}, bf16[1024,768]{1,0:T(8,128)(2,1)}, f32...) custom-call(bf16[1024,768]{1,0:T(8,128)(2,1)S(1)} %copy-done.10, ...), custom_call_target="tpu_custom_call" | custom-call | flops 10871635968 | bytes 23199744 | tf_op jit(solution)/shard_map/cond/branch_1_fun/refine/pallas_call | solution.py:458
  354.0 153.4 %conditional.5 = (bf16[1024,128]{0,1:T(8,128)(2,1)}, f32[768,128]{0,1:T(8,128)}, bf16[1024,768]{1,0:T(8,128)(2,1)}, bf16[1024,768]{1,0:T(8,128)(2,1)}, bf16[1024...) conditional(s32[]{:T(128)} %convert_element_type.228, () %tuple.42, ...), branch_computations={%region_5.6_spmd, %region_6.9_spmd} | conditional | flops 45703757824 | bytes 133866272 | solution.py:738
  359.1 24.7 %refine_back.6 = (bf16[1024,768]{1,0:T(8,128)(2,1)}, bf16[1024,3072]{1,0:T(8,128)(2,1)}, bf16[1024,768]{1,0:T(8,128)(2,1)}, bf16[1024,768]{1,0:T(8,128)(2,1)}, f...) custom-call(bf16[1024,768]{1,0:T(8,128)(2,1)} %convolution_convert_fusion.grad_ref, ...), custom_call_target="tpu_custom_call" | custom-call | flops 10871635968 | bytes 23199744 | tf_op jit(solution)/shard_map/cond/branch_1_fun/refine_back/pallas_call | solution.py:547
  383.8 40.2 %attend_backward.6 = (bf16[3,1024,768]{2,1,0:T(8,128)(2,1)}, f32[2,2,384]{2,1,0:T(2,128)S(1)}) custom-call(s32[8]{0:T(128)S(1)} %copy-done.45, s32[8]{0:T(128)S(1)} %copy-done.49, bf16[3,1024,768]{2,1,0:T(8,128)(2,1)} %get-tuple-element.314.qkv_ref, f32[1024,128]{1,0:T(8,128)S(1)} %copy-done.30, f32[8,128]{1,0:T(8,128)S(1)} %get-tuple-element.311.query_code_ref, ...), custom_call_target="tpu_custom_call" | custom-call | flops 8053063680 | bytes 12582912 | tf_op jit(solution)/shard_map/cond/branch_1_fun/attend_backward/pallas_call | solution.py:256
  424.0 7.8 unmix.5.grad_ref
  431.8 24.6 %refine_back.7 = (bf16[1024,768]{1,0:T(8,128)(2,1)}, bf16[1024,3072]{1,0:T(8,128)(2,1)}, bf16[1024,768]{1,0:T(8,128)(2,1)}, bf16[1024,768]{1,0:T(8,128)(2,1)}, f...) custom-call(bf16[1024,768]{1,0:T(8,128)(2,1)} %unmix.5.grad_ref, bf16[1024,768]{1,0:T(8,128)(2,1)} %get-tuple-element.330.hat1_ref, ...), custom_call_target="tpu_custom_call" | custom-call | flops 10871635968 | bytes 23199744 | tf_op jit(solution)/shard_map/cond/branch_1_fun/refine_back/pallas_call | solution.py:547
  456.4 40.3 %attend_backward.7 = (bf16[3,1024,768]{2,1,0:T(8,128)(2,1)}, f32[2,2,384]{2,1,0:T(2,128)S(1)}) custom-call(s32[8]{0:T(128)S(1)} %copy-done.45, s32[8]{0:T(128)S(1)} %copy-done.49, bf16[3,1024,768]{2,1,0:T(8,128)(2,1)} %get-tuple-element.309.qkv_ref, f32[1024,128]{1,0:T(8,128)S(1)} %copy-done.30, f32[8,128]{1,0:T(8,128)S(1)} %get-tuple-element.311.query_code_ref, ...), custom_call_target="tpu_custom_call" | custom-call | flops 8053063680 | bytes 12582912 | tf_op jit(solution)/shard_map/cond/branch_1_fun/attend_backward/pallas_call | solution.py:256
  496.7 7.8 unmix.6
  515.1 27.8 %collective-permute-done.4 = bf16[1024,768]{1,0:T(8,128)(2,1)} collective-permute-done((bf16[1024,768]{1,0:T(8,128)(2,1)}, bf16[1024,768]{1,0:T(8,128)(2,1)}, u32[]{:S(2)}, u32[]{:S(2)}) %collective-permute-start.4) | collective-permute-done | bytes 1572896 | tf_op jit(solution)/shard_map/ppermute | solution.py:610
  645.7 26.7 %all-reduce.4.cloned.1.call-done = f32[32,3072]{1,0:T(8,128)} async-done(((f32[32,3072]{1,0:T(8,128)}), f32[32,3072]{1,0:T(8,128)}) %all-reduce.4.cloned.1.call-update) | async-done | bytes 393232
  692.9 28.2 %all-reduce = f32[8,1152]{1,0:T(8,128)S(1)} all-reduce(f32[8,1152]{1,0:T(8,128)S(1)} %select_add_fusion), channel_id=6, replica_groups=mesh['section'=4,'dp'=8] {'dp'}, use_global_device_ids=true, to_apply=%region_15.16.clone | all-reduce | flops 9216 | bytes 73728
  726.1 99.9 %collective-permute-done.5 = bf16[256,768]{1,0:T(8,128)(2,1)S(1)} collective-permute-done((bf16[256,768]{1,0:T(8,128)(2,1)S(1)}, bf16[256,768]{1,0:T(8,128)(2,1)S(1)}, u32[]{:S(2)}, u32[]{:S(2)}) %collective-permute-start.5) | collective-permute-done | bytes 393248 | tf_op jit(solution)/shard_map/ppermute | solution.py:610
  826.0 7.9 collective-permute-done.7
  838.1 53.2 %reduce-scatter.27.cloned.1.call-done = bf16[96,1152]{1,0:T(8,128)(2,1)} async-done(((bf16[768,1152]{1,0:T(8,128)(2,1)}), bf16[96,1152]{1,0:T(8,128)(2,1)}) %reduce-scatter.27.cloned.1.call-update) | async-done | bytes 221200
  892.5 67.1 %reduce-scatter.25.cloned.1.call-done = bf16[96,1152]{1,0:T(8,128)(2,1)} async-done(((bf16[768,1152]{1,0:T(8,128)(2,1)}), bf16[96,1152]{1,0:T(8,128)(2,1)}) %reduce-scatter.25.cloned.1.call-update) | async-done | bytes 221200
  965.1 66.2 %reduce-scatter.23.cloned.1.call-done = bf16[384,384]{1,0:T(8,128)(2,1)} async-done(((bf16[3072,384]{1,0:T(8,128)(2,1)}), bf16[384,384]{1,0:T(8,128)(2,1)}) %reduce-scatter.23.cloned.1.call-update) | async-done | bytes 294928 | tf_op jit(solution)/shard_map/reduce_scatter | solution.py:642
  1031.4 71.8 %reduce-scatter.21.cloned.1.call-done = bf16[384,384]{1,0:T(8,128)(2,1)} async-done(((bf16[3072,384]{1,0:T(8,128)(2,1)}), bf16[384,384]{1,0:T(8,128)(2,1)}) %reduce-scatter.21.cloned.1.call-update) | async-done | bytes 294928 | tf_op jit(solution)/shard_map/reduce_scatter | solution.py:642
  1106.3 68.9 %reduce-scatter.19.cloned.1.call-done = bf16[96,1536]{1,0:T(8,128)(2,1)} async-done(((bf16[768,1536]{1,0:T(8,128)(2,1)}), bf16[96,1536]{1,0:T(8,128)(2,1)}) %reduce-scatter.19.cloned.1.call-update) | async-done | bytes 294928 | tf_op jit(solution)/shard_map/reduce_scatter | solution.py:642
  1175.2 71.7 %reduce-scatter.17.cloned.1.call-done = bf16[96,1536]{1,0:T(8,128)(2,1)} async-done(((bf16[768,1536]{1,0:T(8,128)(2,1)}), bf16[96,1536]{1,0:T(8,128)(2,1)}) %reduce-scatter.17.cloned.1.call-update) | async-done | bytes 294928 | tf_op jit(solution)/shard_map/reduce_scatter | solution.py:642
  (356 shorter events, 209.0 us)
Async XLA Ops:
  7.2 23.1 %all-gather.8.cloned.1.call-start = ((), (), s32[]{:S(2)}) async-start(), calls=%async_computation.8 | async-start | bytes 10616832 | tf_op jit(solution)/shard_map/all_gather | solution.py:606
  7.9 54.8 %all-gather.10.cloned.1.call-start = ((), (), s32[]{:S(2)}) async-start(), calls=%async_computation.9 | async-start | bytes 3538944 | tf_op jit(solution)/shard_map/all_gather | solution.py:606
  8.7 59.1 %all-gather.12.cloned.1.call-start = ((), (), s32[]{:S(2)}) async-start(), calls=%async_computation.10 | async-start | bytes 14155776 | tf_op jit(solution)/shard_map/all_gather | solution.py:606
  9.5 82.7 %all-gather.14.cloned.1.call-start = ((), (), s32[]{:S(2)}) async-start(), calls=%async_computation.11 | async-start | bytes 14155776 | tf_op jit(solution)/shard_map/all_gather | solution.py:606
  10.1 662.4 %all-reduce.4.cloned.1.call-start = ((), (), s32[]{:S(2)}) async-start(), calls=%async_computation.21 | async-start | bytes 786432
  10.6 5.5 collective-permute-start
  11.3 10.3 collective-permute-start.1
  16.2 13.9 %collective-permute-start.2 = (bf16[256,768]{1,0:T(8,128)(2,1)S(1)}, bf16[256,768]{1,0:T(8,128)(2,1)S(1)}, u32[]{:S(2)}, u32[]{:S(2)}) collective-permute-start(bf16[256,768]{1,0:T(8,128)(2,1)S(1)} %get-tuple-element.708), channel_id=1, source_target_pairs={{16,0},{24,8},{17,1},{25,9},{18,2},{26,10},{19,3},{27,11},{20,4},{... | collective-permute-start | bytes 1179656 | tf_op jit(solution)/shard_map/ppermute | solution.py:610
  181.9 48.2 %collective-permute-start.3 = (bf16[1024,768]{1,0:T(8,128)(2,1)S(1)}, bf16[1024,768]{1,0:T(8,128)(2,1)S(1)}, u32[]{:S(2)}, u32[]{:S(2)}) collective-permute-start(bf16[1024,768]{1,0:T(8,128)(2,1)S(1)} %get-tuple-element.500), channel_id=1, source_target_pairs={{0,16},{8,24},{1,17},{9,25},{2,18},{10,26},{3,19},{11,27},{4,20},{... | collective-permute-start | bytes 4718600 | tf_op jit(solution)/shard_map/ppermute | solution.py:610
  507.4 35.5 %collective-permute-start.4 = (bf16[1024,768]{1,0:T(8,128)(2,1)}, bf16[1024,768]{1,0:T(8,128)(2,1)}, u32[]{:S(2)}, u32[]{:S(2)}) collective-permute-start(bf16[1024,768]{1,0:T(8,128)(2,1)} %get-tuple-element.535), channel_id=1, source_target_pairs={{16,0},{24,8},{17,1},{25,9},{18,2},{26,10},{19,3},{27,11},{20,4},{... | collective-permute-start | bytes 4718600 | tf_op jit(solution)/shard_map/ppermute | solution.py:610
  513.2 177.5 %all-gather.16.cloned.1.call-start = ((), (), s32[]{:S(2)}) async-start(), calls=%async_computation.18 | async-start | bytes 1310720 | tf_op jit(solution)/shard_map/all_gather | solution.py:795
  515.1 321.3 %reduce-scatter.15.cloned.1.call-start = ((), (), s32[]{:S(2)}) async-start(), calls=%async_computation.13 | async-start | bytes 663552 | tf_op jit(solution)/shard_map/reduce_scatter | solution.py:642
  548.4 6.9 collective-permute-start.13
  558.9 277.5 %reduce-scatter.13.cloned.1.call-start = ((), (), s32[]{:S(2)}) async-start(), calls=%async_computation.12 | async-start | bytes 663552 | tf_op jit(solution)/shard_map/reduce_scatter | solution.py:642
  560.3 13.7 %collective-permute-start.9 = (bf16[768,1152]{0,1:T(8,128)(2,1)}, bf16[768,1152]{0,1:T(8,128)(2,1)}, u32[]{:S(2)}, u32[]{:S(2)}) collective-permute-start(bf16[768,1152]{0,1:T(8,128)(2,1)} %pad_maximum_fusion.1), channel_id=1, source_target_pairs={{0,8},{8,0},{16,24},{24,16},{1,9},{9,1},{17,25},{25,17},{2,10},{10... | collective-permute-start | bytes 5308424 | tf_op jit(solution)/shard_map/ppermute | solution.py:610
  569.3 322.0 %reduce-scatter.27.cloned.1.call-start = ((), (), s32[]{:S(2)}) async-start(), calls=%async_computation.20 | async-start | bytes 1990656
  578.3 381.3 %reduce-scatter.25.cloned.1.call-start = ((), (), s32[]{:S(2)}) async-start(), calls=%async_computation.19 | async-start | bytes 1990656
  583.8 3.8 collective-permute-start.8
  590.3 441.0 %reduce-scatter.23.cloned.1.call-start = ((), (), s32[]{:S(2)}) async-start(), calls=%async_computation.17 | async-start | bytes 2654208 | tf_op jit(solution)/shard_map/reduce_scatter | solution.py:642
  598.0 6.5 collective-permute-start.19
  606.7 496.5 %reduce-scatter.21.cloned.1.call-start = ((), (), s32[]{:S(2)}) async-start(), calls=%async_computation.16 | async-start | bytes 2654208 | tf_op jit(solution)/shard_map/reduce_scatter | solution.py:642
  614.3 6.7 collective-permute-start.18
  623.1 552.1 %reduce-scatter.19.cloned.1.call-start = ((), (), s32[]{:S(2)}) async-start(), calls=%async_computation.15 | async-start | bytes 2654208 | tf_op jit(solution)/shard_map/reduce_scatter | solution.py:642
  630.3 5.2 collective-permute-start.16
  637.7 609.3 %reduce-scatter.17.cloned.1.call-start = ((), (), s32[]{:S(2)}) async-start(), calls=%async_computation.14 | async-start | bytes 2654208 | tf_op jit(solution)/shard_map/reduce_scatter | solution.py:642
  644.8 37.6 %collective-permute-start.15 = (bf16[768,1536]{1,0:T(8,128)(2,1)}, bf16[768,1536]{1,0:T(8,128)(2,1)S(1)}, u32[]{:S(2)}, u32[]{:S(2)}) collective-permute-start(bf16[768,1536]{1,0:T(8,128)(2,1)} %convolution_convert_fusion.7), channel_id=1, source_target_pairs={{0,8},{8,0},{16,24},{24,16},{1,9},{9,1},{17,25},{25,17},{2,10},{10... | collective-permute-start | bytes 7077896 | tf_op jit(solution)/shard_map/ppermute | solution.py:610
  684.6 8.3 collective-permute-start.11
  688.0 138.0 %collective-permute-start.5 = (bf16[256,768]{1,0:T(8,128)(2,1)S(1)}, bf16[256,768]{1,0:T(8,128)(2,1)S(1)}, u32[]{:S(2)}, u32[]{:S(2)}) collective-permute-start(bf16[256,768]{1,0:T(8,128)(2,1)S(1)} %get-tuple-element.725), channel_id=1, source_target_pairs={{0,24},{8,16},{1,25},{9,17},{2,26},{10,18},{3,27},{11,19},{4,28},{... | collective-permute-start | bytes 1179656 | tf_op jit(solution)/shard_map/ppermute | solution.py:610
  689.3 136.7 %collective-permute-start.6 = (bf16[256,768]{1,0:T(8,128)(2,1)S(1)}, bf16[256,768]{1,0:T(8,128)(2,1)S(1)}, u32[]{:S(2)}, u32[]{:S(2)}) collective-permute-start(bf16[256,768]{1,0:T(8,128)(2,1)S(1)} %get-tuple-element.724), channel_id=1, source_target_pairs={{0,8},{8,0},{16,24},{24,16},{1,9},{9,1},{17,25},{25,17},{2,10},{10... | collective-permute-start | bytes 1179656 | tf_op jit(solution)/shard_map/ppermute | solution.py:610
  689.4 144.5 %collective-permute-start.7 = (bf16[256,768]{1,0:T(8,128)(2,1)S(1)}, bf16[256,768]{1,0:T(8,128)(2,1)S(1)}, u32[]{:S(2)}, u32[]{:S(2)}) collective-permute-start(bf16[256,768]{1,0:T(8,128)(2,1)S(1)} %get-tuple-element.723), channel_id=1, source_target_pairs={{0,16},{8,24},{1,17},{9,25},{2,18},{10,26},{3,19},{11,27},{4,20},{... | collective-permute-start | bytes 1179656 | tf_op jit(solution)/shard_map/ppermute | solution.py:610
  837.3 125.3 %collective-permute-start.14 = (bf16[96,384]{1,0:T(8,128)(2,1)S(1)}, bf16[96,384]{1,0:T(8,128)(2,1)S(1)}, u32[]{:S(2)}, u32[]{:S(2)}) collective-permute-start(bf16[96,384]{1,0:T(8,128)(2,1)S(1)} %broadcast_select_fusion.14), channel_id=1, source_target_pairs={{0,8},{8,0},{16,24},{24,16},{1,9},{9,1},{17,25},{25,17},{2,10},{10... | collective-permute-start | bytes 221192 | tf_op jit(solution)/shard_map/ppermute | solution.py:610
  1104.3 145.8 %collective-permute-start.20 = (bf16[384,384]{1,0:T(8,128)(2,1)S(1)}, bf16[384,384]{1,0:T(8,128)(2,1)S(1)}, u32[]{:S(2)}, u32[]{:S(2)}) collective-permute-start(bf16[384,384]{1,0:T(8,128)(2,1)S(1)} %broadcast_select_fusion.6), channel_id=1, source_target_pairs={{0,8},{8,0},{16,24},{24,16},{1,9},{9,1},{17,25},{25,17},{2,10},{10... | collective-permute-start | bytes 884744 | tf_op jit(solution)/shard_map/ppermute | solution.py:610
  (73 other events, 1895.4 us)
Sparse Core Ops, SparseCore 0:
  9.6 19.7 all-gather.7
  30.9 12.2 all-gather.9
  44.7 22.9 all-gather.11
  69.2 23.0 all-gather.13
  513.3 159.1 all-reduce.3
  674.0 16.5 all-gather.15
  694.8 60.6 reduce-scatter.14
  759.3 62.4 reduce-scatter.12
  825.7 65.6 reduce-scatter.26
  894.6 64.8 reduce-scatter.24
  963.5 67.8 reduce-scatter.22
  1035.1 67.9 reduce-scatter.20
  1107.1 68.0 reduce-scatter.18
  1179.0 67.9 reduce-scatter.16

commit v2 on v1

--- a/solution.py
+++ b/solution.py
@@ -16,7 +16,8 @@
 EPS_NORM = 1e-05
 EPS_PROJ = 1e-06
 NEG_FILL = -1e30
-VMEM = 56 * 1024 * 1024
+PARAMS = pltpu.CompilerParams(vmem_limit_bytes=56 * 1024 * 1024)
+COST = pl.CostEstimate(flops=1, bytes_accessed=1, transcendentals=0)
 BF = jnp.bfloat16
 F32 = jnp.float32
 
@@ -44,6 +45,20 @@
 
 def small_spec(layer, width):
     return pl.BlockSpec((1, 1, width), lambda *_: (layer, 0, 0))
+
+
+def weight_specs(block, index, layer):
+    def spec(wanted):
+        def at(*grid):
+            return tuple(jnp.where((grid[-1][0] == layer) == wanted, n, 0) for n in index(grid[0]))
+
+        return pl.BlockSpec(block, at)
+
+    return [spec(True), spec(False)]
+
+
+def pick(sel_ref, layer, pair):
+    return jnp.where(sel_ref[0] == layer, pair[0][...], pair[1][...])
 
 
 def attention_plan(starts, real_flags):
@@ -176,10 +191,8 @@
             jax.ShapeDtypeStruct((length, width), BF),
             jax.ShapeDtypeStruct((GROUPS, pairs * blocks, 2 * QB), F32),
         ],
-        compiler_params=pltpu.CompilerParams(vmem_limit_bytes=VMEM),
-        cost_estimate=pl.CostEstimate(
-            flops=4 * length * length * width, bytes_accessed=8 * length * width, transcendentals=0
-        ),
+        compiler_params=PARAMS,
+        cost_estimate=COST,
     )(begin, count, qkv, key_code, query_code)
 
 
@@ -284,14 +297,12 @@
             jax.ShapeDtypeStruct((3, length, width), BF),
             jax.ShapeDtypeStruct((GROUPS, 2, group), F32),
         ],
-        compiler_params=pltpu.CompilerParams(vmem_limit_bytes=VMEM),
-        cost_estimate=pl.CostEstimate(
-            flops=10 * length * length * width, bytes_accessed=16 * length * width, transcendentals=0
-        ),
+        compiler_params=PARAMS,
+        cost_estimate=COST,
     )(begin, count, qkv, key_code, query_code, context, logsum, grad_context)
 
 
-def mix_kernel(x_ref, w_ref, small_ref, out_ref):
+def mix_kernel(layer, sel_ref, x_ref, own_ref, other_ref, small_ref, out_ref):
     part = pl.program_id(0)
     width = x_ref.shape[1]
     ff_width = small_ref.shape[2] - 8 * width
@@ -299,66 +310,70 @@
     shift = small_ref[0, :, pl.ds(pl.multiple_of(at, 128), width)]
     shift = jnp.where(part == 1, jnp.zeros_like(shift), shift)
     scale = jnp.where(part == 0, HEAD**-0.5, 1.0)
+    weight = pick(sel_ref, layer, (own_ref, other_ref))
     for r in range(0, x_ref.shape[0], 256):
         rows = slice(r, r + 256)
-        out_ref[0, rows, :] = ((dot(x_ref[rows, :], w_ref[0]) + shift) * scale).astype(BF)
-
-
-def mix(x, w_qkv, small, layer):
+        out_ref[0, rows, :] = ((dot(x_ref[rows, :], weight) + shift) * scale).astype(BF)
+
+
+def mix(sel, x, w_qkv, small, layer):
     length, width = x.shape
     return pl.pallas_call(
-        mix_kernel,
+        partial(mix_kernel, layer),
         name="mix",
-        grid=(3,),
-        in_specs=[
-            pl.BlockSpec((length, width), lambda c: (0, 0)),
-            pl.BlockSpec((1, width, width), lambda c: (layer, 0, c)),
-            small_spec(layer, small.shape[2]),
-        ],
-        out_specs=pl.BlockSpec((1, length, width), lambda c: (c, 0, 0)),
+        grid_spec=pltpu.PrefetchScalarGridSpec(
+            num_scalar_prefetch=1,
+            grid=(3,),
+            in_specs=[
+                pl.BlockSpec((length, width), lambda c, _: (0, 0)),
+                *weight_specs((width, width), lambda c: (0, c), layer),
+                small_spec(layer, small.shape[2]),
+            ],
+            out_specs=pl.BlockSpec((1, length, width), lambda c, _: (c, 0, 0)),
+        ),
         out_shape=jax.ShapeDtypeStruct((3, length, width), BF),
-        compiler_params=pltpu.CompilerParams(vmem_limit_bytes=VMEM),
-        cost_estimate=pl.CostEstimate(
-            flops=6 * length * width * width, bytes_accessed=14 * length * width, transcendentals=0
-        ),
-    )(x, w_qkv, small)
-
-
-def unmix_kernel(grad_ref, w_ref, skip_ref, out_ref, total):
+        compiler_params=PARAMS,
+        cost_estimate=COST,
+    )(sel, x, *w_qkv, small)
+
+
+def unmix_kernel(layer, sel_ref, grad_ref, own_ref, other_ref, skip_ref, out_ref, total):
     part = pl.program_id(0)
 
     @pl.when(part == 0)
     def _():
         total[...] = skip_ref[...].astype(F32)
 
+    weight = pick(sel_ref, layer, (own_ref, other_ref))
     for r in range(0, total.shape[0], 256):
         rows = slice(r, r + 256)
-        total[rows, :] += dot_nt(grad_ref[0, rows, :], w_ref[0])
+        total[rows, :] += dot_nt(grad_ref[0, rows, :], weight)
 
     @pl.when(part == 2)
     def _():
         out_ref[...] = total[...].astype(BF)
 
 
-def unmix(grad_mixed, w_qkv, skip, layer):
+def unmix(sel, grad_mixed, w_qkv, skip, layer):
     _, length, width = grad_mixed.shape
     return pl.pallas_call(
-        unmix_kernel,
+        partial(unmix_kernel, layer),
         name="unmix",
-        grid=(3,),
-        in_specs=[
-            pl.BlockSpec((1, length, width), lambda c: (c, 0, 0)),
-            pl.BlockSpec((1, width, width), lambda c: (layer, 0, c)),
-            pl.BlockSpec((length, width), lambda c: (0, 0)),
-        ],
-        out_specs=pl.BlockSpec((length, width), lambda c: (0, 0)),
+        grid_spec=pltpu.PrefetchScalarGridSpec(
+            num_scalar_prefetch=1,
+            grid=(3,),
+            in_specs=[
+                pl.BlockSpec((1, length, width), lambda c, _: (c, 0, 0)),
+                *weight_specs((width, width), lambda c: (0, c), layer),
+                pl.BlockSpec((length, width), lambda c, _: (0, 0)),
+            ],
+            out_specs=pl.BlockSpec((length, width), lambda c, _: (0, 0)),
+            scratch_shapes=[pltpu.VMEM((length, width), F32)],
+        ),
         out_shape=jax.ShapeDtypeStruct((length, width), BF),
-        scratch_shapes=[pltpu.VMEM((length, width), F32)],
-        compiler_params=pltpu.CompilerParams(vmem_limit_bytes=VMEM),
-        cost_estimate=pl.CostEstimate(
-            flops=6 * length * width * width, bytes_accessed=14 * length * width, transcendentals=0
-        ),
-    )(grad_mixed, w_qkv, skip)
+        compiler_params=PARAMS,
+        cost_estimate=COST,
+    )(sel, grad_mixed, *w_qkv, skip)
 
 
 def normalized(values):
@@ -403,7 +418,9 @@
 
 
 def refine_kernel(
-    x_ref, context_ref, w_out_ref, w_up_ref, w_down_ref, small_ref, b_up_ref,
+    layer, sel_ref, x_ref, context_ref,
+    out_own_ref, out_other_ref, up_own_ref, up_other_ref, down_own_ref, down_other_ref,
+    small_ref, b_up_ref,
     out_ref, hidden_ref, hat1_ref, hat2_ref, scale1_ref, scale2_ref, active_ref, slope_ref,
     total,
 ):
@@ -416,9 +433,10 @@
 
     @pl.when(step == 0)
     def _():
+        w_out = pick(sel_ref, layer, (out_own_ref, out_other_ref))
         for r in range(0, length, ROWS):
             rows = slice(r, r + ROWS)
-            summed = x_ref[rows, :].astype(F32) + dot(context_ref[rows, :], w_out_ref[0])
+            summed = x_ref[rows, :].astype(F32) + dot(context_ref[rows, :], w_out)
             hat, inverse = normalized(summed + vector("b_out"))
             hidden = hat * vector("gain1") + vector("shift1")
             hat1_ref[rows, :] = hat.astype(BF)
@@ -426,14 +444,16 @@
             hidden_ref[rows, :] = hidden.astype(BF)
             total[rows, :] = hidden + vector("b_down")
 
+    w_up = pick(sel_ref, layer, (up_own_ref, up_other_ref))
+    w_down = pick(sel_ref, layer, (down_own_ref, down_other_ref))
     for r in range(0, length, ROWS):
         rows = slice(r, r + ROWS)
-        raised = dot(hidden_ref[rows, :], w_up_ref[0]) + b_up_ref[0]
+        raised = dot(hidden_ref[rows, :], w_up) + b_up_ref[0]
         active, slope = gelu_parts(raised)
         active = active.astype(BF)
         active_ref[rows, :] = active
         slope_ref[rows, :] = slope.astype(BF)
-        total[rows, :] += dot(active, w_down_ref[0])
+        total[rows, :] += dot(active, w_down)
 
     @pl.when(step == pl.num_programs(0) - 1)
     def _():
@@ -445,44 +465,49 @@
             out_ref[rows, :] = (hat * vector("gain2") + vector("shift2")).astype(BF)
 
 
-def refine(x, context, weights, layer):
+def weights_specs(width, layer):
+    return [
+        *weight_specs((width, width), lambda f: (0, 0), layer),
+        *weight_specs((width, FB), lambda f: (0, f), layer),
+        *weight_specs((FB, width), lambda f: (f, 0), layer),
+    ]
+
+
+def refine(sel, x, context, weights, layer):
     w_out, w_up, w_down, small = weights
     length, width = x.shape
-    ff_width = w_up.shape[2]
-    whole = pl.BlockSpec((length, width), lambda f: (0, 0))
-    lanes = pl.BlockSpec((length, 128), lambda f: (0, 0))
-    part = pl.BlockSpec((length, FB), lambda f: (0, f))
+    ff_width = w_up[0].shape[1]
+    whole = pl.BlockSpec((length, width), lambda f, _: (0, 0))
+    lanes = pl.BlockSpec((length, 128), lambda f, _: (0, 0))
+    part = pl.BlockSpec((length, FB), lambda f, _: (0, f))
     row_shape = jax.ShapeDtypeStruct((length, width), BF)
     lane_shape = jax.ShapeDtypeStruct((length, 128), F32)
     ff_shape = jax.ShapeDtypeStruct((length, ff_width), BF)
     return pl.pallas_call(
-        refine_kernel,
+        partial(refine_kernel, layer),
         name="refine",
-        grid=(ff_width // FB,),
-        in_specs=[
-            whole,
-            whole,
-            pl.BlockSpec((1, width, width), lambda f: (layer, 0, 0)),
-            pl.BlockSpec((1, width, FB), lambda f: (layer, 0, f)),
-            pl.BlockSpec((1, FB, width), lambda f: (layer, f, 0)),
-            small_spec(layer, small.shape[2]),
-            pl.BlockSpec((1, 1, FB), lambda f: (layer, 0, f)),
-        ],
-        out_specs=[whole, whole, whole, whole, lanes, lanes, part, part],
+        grid_spec=pltpu.PrefetchScalarGridSpec(
+            num_scalar_prefetch=1,
+            grid=(ff_width // FB,),
+            in_specs=[
+                whole,
+                whole,
+                *weights_specs(width, layer),
+                small_spec(layer, small.shape[2]),
+                pl.BlockSpec((1, 1, FB), lambda f, _: (layer, 0, f)),
+            ],
+            out_specs=[whole, whole, whole, whole, lanes, lanes, part, part],
+            scratch_shapes=[pltpu.VMEM((length, width), F32)],
+        ),
         out_shape=[row_shape] * 4 + [lane_shape] * 2 + [ff_shape] * 2,
-        scratch_shapes=[pltpu.VMEM((length, width), F32)],
-        compiler_params=pltpu.CompilerParams(vmem_limit_bytes=VMEM),
-        cost_estimate=pl.CostEstimate(
-            flops=2 * length * width * (width + 2 * ff_width),
-            bytes_accessed=2 * width * (width + 2 * ff_width) + 4 * length * ff_width,
-            transcendentals=0,
-        ),
-    )(x, context, w_out, w_up, w_down, small, small)
+        compiler_params=PARAMS,
+        cost_estimate=COST,
+    )(sel, x, context, *w_out, *w_up, *w_down, small, small)
 
 
 def refine_back_kernel(
-    grad_ref, hat1_ref, hat2_ref, scale1_ref, scale2_ref, slope_ref,
-    w_out_ref, w_up_ref, w_down_ref, small_ref,
+    layer, sel_ref, grad_ref, hat1_ref, hat2_ref, scale1_ref, scale2_ref, slope_ref,
+    out_own_ref, out_other_ref, up_own_ref, up_other_ref, down_own_ref, down_other_ref, small_ref,
     grad_low_ref, grad_raised_ref, grad_attn_ref, grad_context_ref, sums_ref, up_sums_ref,
     total,
 ):
@@ -511,17 +536,20 @@
             add(4, grad, r == 0)
             add(5, low.astype(F32), r == 0)
 
+    w_up = pick(sel_ref, layer, (up_own_ref, up_other_ref))
+    w_down = pick(sel_ref, layer, (down_own_ref, down_other_ref))
     for r in range(0, length, ROWS):
         rows = slice(r, r + ROWS)
-        grad_active = dot_nt(grad_low_ref[rows, :], w_down_ref[0])
+        grad_active = dot_nt(grad_low_ref[rows, :], w_down)
         raised = (grad_active * slope_ref[rows, :].astype(F32)).astype(BF)
         grad_raised_ref[rows, :] = raised
         part = jnp.sum(raised.astype(F32), axis=0, keepdims=True)
         up_sums_ref[...] = part if r == 0 else up_sums_ref[...] + part
-        total[rows, :] += dot_nt(raised, w_up_ref[0])
+        total[rows, :] += dot_nt(raised, w_up)
 
     @pl.when(step == pl.num_programs(0) - 1)
     def _():
+        w_out = pick(sel_ref, layer, (out_own_ref, out_other_ref))
         for r in range(0, length, ROWS):
             rows = slice(r, r + ROWS)
             grad = total[rows, :]
@@ -529,37 +557,39 @@
             summed = normalized_pull(grad * vector("gain1"), hat, scale1_ref[rows, :1])
             attn = summed.astype(BF)
             grad_attn_ref[rows, :] = attn
-            grad_context_ref[rows, :] = dot_nt(attn, w_out_ref[0]).astype(BF)
+            grad_context_ref[rows, :] = dot_nt(attn, w_out).astype(BF)
             add(1, grad * hat, r == 0)
             add(3, grad, r == 0)
             add(0, attn.astype(F32), r == 0)
 
 
-def refine_back(grad, kept, weights, layer):
+def refine_back(sel, grad, kept, weights, layer):
     w_out, w_up, w_down, small = weights
     hat1, hat2, scale1, scale2, slope = kept
     length, width = grad.shape
-    ff_width = w_up.shape[2]
-    whole = pl.BlockSpec((length, width), lambda f: (0, 0))
-    lanes = pl.BlockSpec((length, 128), lambda f: (0, 0))
-    part = pl.BlockSpec((length, FB), lambda f: (0, f))
+    ff_width = w_up[0].shape[1]
+    whole = pl.BlockSpec((length, width), lambda f, _: (0, 0))
+    lanes = pl.BlockSpec((length, 128), lambda f, _: (0, 0))
+    part = pl.BlockSpec((length, FB), lambda f, _: (0, f))
     row_shape = jax.ShapeDtypeStruct((length, width), BF)
     return pl.pallas_call(
-        refine_back_kernel,
+        partial(refine_back_kernel, layer),
         name="refine_back",
-        grid=(ff_width // FB,),
-        in_specs=[
-            whole, whole, whole, lanes, lanes, part,
-            pl.BlockSpec((1, width, width), lambda f: (layer, 0, 0)),
-            pl.BlockSpec((1, width, FB), lambda f: (layer, 0, f)),
-            pl.BlockSpec((1, FB, width), lambda f: (layer, f, 0)),
-            small_spec(layer, small.shape[2]),
-        ],
-        out_specs=[
-            whole, part, whole, whole,
-            pl.BlockSpec((6, width), lambda f: (0, 0)),
-            pl.BlockSpec((1, FB), lambda f: (0, f)),
-        ],
+        grid_spec=pltpu.PrefetchScalarGridSpec(
+            num_scalar_prefetch=1,
+            grid=(ff_width // FB,),
+            in_specs=[
+                whole, whole, whole, lanes, lanes, part,
+                *weights_specs(width, layer),
+                small_spec(layer, small.shape[2]),
+            ],
+            out_specs=[
+                whole, part, whole, whole,
+                pl.BlockSpec((6, width), lambda f, _: (0, 0)),
+                pl.BlockSpec((1, FB), lambda f, _: (0, f)),
+            ],
+            scratch_shapes=[pltpu.VMEM((length, width), F32)],
+        ),
         out_shape=[
             row_shape,
             jax.ShapeDtypeStruct((length, ff_width), BF),
@@ -568,86 +598,247 @@
             jax.ShapeDtypeStruct((6, width), F32),
             jax.ShapeDtypeStruct((1, ff_width), F32),
         ],
-        scratch_shapes=[pltpu.VMEM((length, width), F32)],
-        compiler_params=pltpu.CompilerParams(vmem_limit_bytes=VMEM),
-        cost_estimate=pl.CostEstimate(
-            flops=2 * length * width * (width + 2 * ff_width),
-            bytes_accessed=2 * width * (width + 2 * ff_width) + 4 * length * ff_width,
-            transcendentals=0,
+        compiler_params=PARAMS,
+        cost_estimate=COST,
+    )(sel, grad, hat1, hat2, scale1, scale2, slope, *w_out, *w_up, *w_down, small)
+
+
+HALF = 384
+SHARDS = 8
+
+
+def feed_grads_kernel(
+    sel_ref, hidden_ref, raised_late_ref, raised_ref, active_ref, low_late_ref, low_ref, out_ref,
+    hidden_scr, low_scr, raised_scr,
+):
+    step = pl.program_id(0)
+    blocks = raised_ref.shape[1] // HALF
+    share = hidden_ref.shape[1] // SHARDS
+    late = sel_ref[1] == 1
+
+    @pl.when(step == 0)
+    def _():
+        hidden_scr[...] = hidden_ref[...].T
+        low_scr[...] = jnp.where(late, low_late_ref[...], low_ref[...]).T
+        raised_scr[...] = jnp.where(late, raised_late_ref[...], raised_ref[...])
+
+    @pl.when(step < 4)
+    def _():
+        at = pl.multiple_of(step * (2 * share), 2 * share)
+        part = dot(hidden_scr[pl.ds(at, 2 * share), :], raised_scr[...]).astype(BF)
+        for m in range(2):
+            for n in range(blocks):
+                out_ref[m, n * share : (n + 1) * share, :] = part[
+                    m * share : (m + 1) * share, n * HALF : (n + 1) * HALF
+                ]
+
+    @pl.when(step >= 4)
+    def _():
+        rows = out_ref.shape[1]
+        for m in range(2):
+            part = dot(low_scr[...], active_ref[:, m * rows : (m + 1) * rows])
+            out_ref[m] = part.T.astype(BF)
+
+
+def feed_grads(sel, hidden, raised_late, raised, active, low_late, low):
+    length, width = hidden.shape
+    ff_width = active.shape[1]
+    half_ff = ff_width // 2
+
+    def late_spec(shape, wanted):
+        return pl.BlockSpec(shape, lambda n, sel: (0, jnp.where(sel[1] == wanted, sel[2], 0)))
+
+    return pl.pallas_call(
+        feed_grads_kernel,
+        name="feed_grads",
+        grid_spec=pltpu.PrefetchScalarGridSpec(
+            num_scalar_prefetch=1,
+            grid=(8,),
+            in_specs=[
+                pl.BlockSpec((length, width), lambda n, _: (0, 0)),
+                late_spec((length, half_ff), 1),
+                late_spec((length, half_ff), 0),
+                pl.BlockSpec((length, ff_width // 4), lambda n, _: (0, jnp.maximum(n - 4, 0))),
+                late_spec((length, width // 2), 1),
+                late_spec((length, width // 2), 0),
+            ],
+            out_specs=pl.BlockSpec(
+                (2, ff_width // SHARDS, HALF), lambda n, _: (lax.rem(n, 4), n // 4, 0)
+            ),
+            scratch_shapes=[
+                pltpu.VMEM((width, length), BF),
+                pltpu.VMEM((width // 2, length), BF),
+                pltpu.VMEM((length, half_ff), BF),
+            ],
         ),
-    )(grad, hat1, hat2, scale1, scale2, slope, w_out, w_up, w_down, small)
-
-
-def layer_forward(x, weights, layer, plan):
+        out_shape=jax.ShapeDtypeStruct((SHARDS, 2 * (ff_width // SHARDS), HALF), BF),
+        compiler_params=PARAMS,
+        cost_estimate=COST,
+    )(sel, hidden, raised_late, raised, active, low_late, low)
+
+
+def attend_grads_kernel(
+    sel_ref, context_ref, x_ref, attn_late_ref, attn_ref, mixed_late_ref, mixed_ref, out_ref, turned
+):
+    step = pl.program_id(0)
+    late = sel_ref[1] == 1
+
+    def store(cols):
+        out_ref[...] = dot(turned[...], cols).astype(BF).reshape(out_ref.shape)
+
+    @pl.when(step == 0)
+    def _():
+        turned[...] = context_ref[...].T
+        store(jnp.where(late, attn_late_ref[...], attn_ref[...]))
+
+    @pl.when(step == 1)
+    def _():
+        turned[...] = x_ref[...].T
+
+    @pl.when(step > 0)
+    def _():
+        store(jnp.where(late, mixed_late_ref[0], mixed_ref[0]))
+
+
+def attend_grads(sel, context, x, attn_late, attn, mixed_late, mixed):
+    length, width = x.shape
+
+    def late_spec(wanted):
+        return pl.BlockSpec(
+            (length, HALF), lambda n, sel: (0, jnp.where(sel[1] == wanted, sel[2], 0))
+        )
+
+    def mixed_spec(wanted):
+        def at(n, sel):
+            return (
+                jnp.where(sel[1] == wanted, jnp.maximum(n - 1, 0), 0),
+                0,
+                jnp.where(sel[1] == wanted, sel[2], 0),
+            )
+
+        return pl.BlockSpec((1, length, HALF), at)
+
+    whole = pl.BlockSpec((length, width), lambda n, _: (0, 0))
+    share = width // SHARDS
+    return pl.pallas_call(
+        attend_grads_kernel,
+        name="attend_grads",
+        grid_spec=pltpu.PrefetchScalarGridSpec(
+            num_scalar_prefetch=1,
+            grid=(4,),
+            in_specs=[whole, whole, late_spec(1), late_spec(0), mixed_spec(1), mixed_spec(0)],
+            out_specs=pl.BlockSpec((SHARDS, share, HALF), lambda n, _: (0, n, 0)),
+            scratch_shapes=[pltpu.VMEM((width, length), BF)],
+        ),
+        out_shape=jax.ShapeDtypeStruct((SHARDS, 4 * share, HALF), BF),
+        compiler_params=PARAMS,
+        cost_estimate=COST,
+    )(sel, context, x, attn_late, attn, mixed_late, mixed)
+
+
+def layer_forward(sel, x, weights, layer, plan):
     w_qkv, w_out, w_up, w_down, small = weights
-    qkv = mix(x, w_qkv, small, layer)
+    qkv = mix(sel, x, w_qkv, small, layer)
     context, logsum = attend_forward(qkv, plan)
     out, hidden, hat1, hat2, scale1, scale2, active, slope = refine(
-        x, context, (w_out, w_up, w_down, small), layer
+        sel, x, context, (w_out, w_up, w_down, small), layer
     )
     return (out, (x, qkv, context, logsum, hidden, hat1, hat2, scale1, scale2, active, slope))
 
 
-def layer_backward(grad, kept, weights, layer, plan):
-    w_qkv, w_out, w_up, w_down, small = weights
-    x, qkv, context, logsum, hidden, hat1, hat2, scale1, scale2, active, slope = kept
+def feed_backward(sel, grad, kept, weights, layer):
+    _, w_out, w_up, w_down, small = weights
+    hat1, hat2, scale1, scale2 = kept[5:9]
     grad_low, grad_raised, grad_attn, grad_context, sums, up_sums = refine_back(
-        grad, (hat1, hat2, scale1, scale2, slope), (w_out, w_up, w_down, small), layer
-    )
-    grad_mixed, mix_sums = attend_backward(qkv, context, logsum, grad_context, plan)
-    grad_x = unmix(grad_mixed, w_qkv, grad_attn, layer)
-    return (grad_x, (grad_low, grad_raised, grad_attn, grad_mixed), (sums, up_sums, mix_sums))
-
-
-CORE_PAIRS = ((0, 1), (1, 0), (2, 3), (3, 2))
-
-
-def pair_gather(value):
-    return lax.all_gather(value, "section", axis_index_groups=[[0, 1], [2, 3]])
+        sel, grad, (hat1, hat2, scale1, scale2, kept[10]), (w_out, w_up, w_down, small), layer
+    )
+    return (grad_context, (grad_low, grad_raised, grad_attn), (sums, up_sums))
+
+
+def mixed_backward(grad_context, kept, plan):
+    return attend_backward(kept[1], kept[2], kept[3], grad_context, plan)
+
+
+def layer_backward(sel, grad, kept, weights, layer, plan):
+    grad_context, grads, sums = feed_backward(sel, grad, kept, weights, layer)
+    grad_mixed, mix_sums = mixed_backward(grad_context, kept, plan)
+    grad_x = unmix(sel, grad_mixed, weights[0], grads[2], layer)
+    return (grad_x, grads + (grad_mixed,), sums + (mix_sums,))
+
+
+def swap_cores(value):
+    return send(value, ((0, 1), (1, 0), (2, 3), (3, 2)))
 
 
 def send(value, routes):
     return lax.ppermute(value, "section", routes)
 
 
-def swap_cores(value):
-    return send(value, CORE_PAIRS)
-
-
-def keep_half(value, core, axis):
-    width = value.shape[axis] // 2
-    return lax.dynamic_slice_in_dim(value, core * width, width, axis)
-
-
-def weight_parts(kept, grads, half):
-    x, context, hidden, active = kept[0], kept[2], kept[4], kept[9]
-    grad_low, grad_raised, grad_attn, grad_mixed = grads
-
-    def product(rows, cols):
-        return dot_tn(rows, keep_half(cols, half, cols.ndim - 1)).astype(BF)
-
-    return (
-        product(active, grad_low),
-        product(hidden, grad_raised),
-        product(context, grad_attn),
-        jnp.concatenate([product(x, grad_mixed[c]) for c in range(3)], axis=1),
-    )
-
-
-def sum_shards(kept, grads, core):
-    theirs = weight_parts(kept, grads, 1 - core)
-    arrived = [swap_cores(part) for part in theirs]
-    mine = weight_parts(kept, grads, core)
-    both = [(a.astype(F32) + b.astype(F32)).astype(BF) for a, b in zip(mine, arrived)]
-    return [lax.psum_scatter(part, "dp", scatter_dimension=0, tiled=True) for part in both]
-
-
-def small_sums(sums):
-    sums, up_sums, mix_sums = sums
-    rows = [up_sums[0], mix_sums.transpose(1, 0, 2).reshape(-1)]
-    rows += [sums[n] for n in range(6)]
-    shards = lax.axis_size("dp")
-    return jnp.concatenate([row.reshape(shards, -1) for row in rows], axis=1)
+def pick_row(value, at, axis=0):
+    return lax.dynamic_index_in_dim(value, at, axis, keepdims=False)
+
+
+def plus(*values):
+    return sum(value.astype(F32) for value in values).astype(BF)
+
+
+class RowSum:
+    def __init__(self, value, x_first):
+        at = lax.axis_index("dp")
+        self.z, self.x, self.x_first = at // 2, at % 2, x_first
+        self.value = value.reshape(4, 2, *value.shape[1:])
+        self.travelling = None
+        self.steps = [self.cross, self.line, self.line, self.line]
+        if not x_first:
+            self.steps = self.steps[1:] + self.steps[:1]
+        self.line_at = 0
+
+    def cross(self):
+        axis = 1 if self.x_first else 0
+        other = pick_row(self.value, 1 - self.x, axis)
+        arrived = lax.ppermute(other, "dp", [(n, n ^ 1) for n in range(8)])
+        self.value = plus(pick_row(self.value, self.x, axis), arrived)
+
+    def line(self):
+        self.line_at += 1
+        far = 4 - self.line_at
+        right = pick_row(self.value, jnp.minimum(self.z + far, 3))
+        left = pick_row(self.value, jnp.maximum(self.z - far, 0))
+        if self.travelling is not None:
+            right, left = plus(right, self.travelling[0]), plus(left, self.travelling[1])
+        self.travelling = (
+            lax.ppermute(right, "dp", [(n, n + 2) for n in range(6)]),
+            lax.ppermute(left, "dp", [(n + 2, n) for n in range(6)]),
+        )
+        if self.line_at == 3:
+            self.value = plus(pick_row(self.value, self.z), *self.travelling)
+
+    def step(self):
+        if self.steps:
+            self.steps.pop(0)()
+
+    def result(self):
+        while self.steps:
+            self.step()
+        return self.value
+
+
+class PlainSum:
+    def __init__(self, value, blocks):
+        shards = lax.axis_size("dp")
+        parts, at = [], 0
+        for rows in blocks:
+            part = value[:, at : at + rows].reshape(shards, -1, value.shape[2])
+            parts, at = parts + [part], at + rows
+        whole = jnp.concatenate(parts, axis=1)
+        self.value = lax.psum_scatter(whole, "dp", scatter_dimension=0, tiled=True)[0]
+        self.travelling = None
+
+    def step(self):
+        pass
+
+    def result(self):
+        return self.value
 
 
 def body(
@@ -657,16 +848,28 @@
     section_at = lax.axis_index("section")
     core = section_at % 2
     is_late = section_at >= 2
+    flip = core == 1
     quarter = tokens_in.shape[1]
     length, width = 4 * quarter, tokens_in.shape[2]
     ff_width = w_up.shape[2]
-
-    own = tokens_in[core]
-    other = tokens_in[1 - core]
-    near = swap_cores(other)
+    proj_cols = w_proj.shape[1]
+    shards = lax.axis_size("dp")
+    share = width // shards
+
+    def sel_for(half):
+        return jnp.stack([core, section_at // 2, half]).astype(jnp.int32)
+
+    sel_mine, sel_theirs = sel_for(core), sel_for(1 - core)
+
+    own = pick_row(tokens_in, core)
+    other = pick_row(tokens_in, 1 - core)
     straight = send(own, [(2, 0), (3, 1)])
     crossed = send(other, [(2, 1), (3, 0)])
-    flip = core == 1
+    near = swap_cores(other)
+    small = pack_small(b_qv[0], b_attn_out[0], ln_gain[0], ln_bias[0], b_up[0], b_down[0])[None]
+    small_other = swap_cores(small)
+    small = jnp.stack([jnp.where(flip, small_other, small), jnp.where(flip, small, small_other)])
+    weights = tuple((w[0], swap_cores(w[0])) for w in (w_qkv, w_attn_out, w_up, w_down)) + (small,)
     x = jnp.concatenate(
         [
             jnp.where(flip, near, own),
@@ -676,31 +879,36 @@
         ],
         axis=0,
     )
-    small = pack_small(b_qv[0], b_attn_out[0], ln_gain[0], ln_bias[0], b_up[0], b_down[0])
-    small = pair_gather(small[None])
-    weights = (
-        pair_gather(w_qkv[0]),
-        pair_gather(w_attn_out[0]),
-        pair_gather(w_up[0]),
-        pair_gather(w_down[0]),
-        small,
-    )
-    projection = lax.all_gather(w_proj, "section", axis=1, tiled=True)
-    target = lax.all_gather(cotangent, "section", axis=2, tiled=True)[core]
-    plan = attention_plan(seg_starts[core], pad_mask[core])
+
+    head_own = jnp.concatenate([w_proj, pick_row(cotangent, core)], axis=0)
+    head_other = jnp.concatenate([w_proj, pick_row(cotangent, 1 - core)], axis=0)
+    head_own = head_own.reshape(-1, 4 * proj_cols)
+    head_other = head_other.reshape(-1, 4 * proj_cols)
+    head_parts = (
+        head_own,
+        send(head_other, [(2, 3), (3, 2)]),
+        send(head_own, [(0, 2), (1, 3)]),
+        send(head_other, [(0, 3), (1, 2)]),
+    )
+    plan = attention_plan(pick_row(seg_starts, core), pick_row(pad_mask, core))
 
     def both_forward(rows):
-        middle, kept_even = layer_forward(rows, weights, 0, plan)
-        last, kept_odd = layer_forward(middle, weights, 1, plan)
+        middle, kept_even = layer_forward(sel_mine, rows, weights, 0, plan)
+        last, kept_odd = layer_forward(sel_mine, middle, weights, 1, plan)
         return (last, kept_even, kept_odd)
 
-    early = both_forward(x)
-    hopped = send(early[0], [(0, 2), (1, 3)])
-    last, kept_even, kept_odd = lax.cond(
-        is_late, lambda rows, _: both_forward(rows), lambda _, state: state, hopped, early
-    )
-
     def head(rows):
+        mine, late, straight, crossed = [part.reshape(-1, proj_cols) for part in head_parts]
+        joined_parts = jnp.concatenate(
+            [
+                jnp.where(flip, crossed, straight),
+                jnp.where(flip, straight, crossed),
+                jnp.where(flip, late, mine),
+                jnp.where(flip, mine, late),
+            ],
+            axis=1,
+        )
+        projection, target = joined_parts[:width], joined_parts[width:]
         factor = math.sqrt(projection.shape[1])
         columns = dot(rows, projection)
         given = target.astype(F32)
@@ -708,99 +916,178 @@
         cross = jnp.sum(columns * given, axis=1, keepdims=True)
         embedded = (factor * columns * inverse).astype(BF)
         grad_columns = (factor * (given * inverse - columns * cross * inverse**3)).astype(BF)
-        return (embedded, dot_tn(rows, grad_columns), dot_nt(grad_columns, projection).astype(BF))
-
-    def layer_zero():
-        row = jnp.zeros((length, width), BF)
         return (
-            row,
-            (row, jnp.zeros((length, ff_width), BF), row, jnp.zeros((3, length, width), BF)),
-            (
-                jnp.zeros((6, width), F32),
-                jnp.zeros((1, ff_width), F32),
-                jnp.zeros((GROUPS, 2, width // GROUPS), F32),
-            ),
+            embedded,
+            dot_tn(rows, grad_columns).astype(BF),
+            dot_nt(grad_columns, projection).astype(BF),
         )
 
-    def back_late(rows):
-        embedded, grad_proj, grad_last = head(rows)
-        grad, grads_odd, sums_odd = layer_backward(grad_last, kept_odd, weights, 1, plan)
-        grad, grads_even, sums_even = layer_backward(grad, kept_even, weights, 0, plan)
-        return (embedded, grad_proj, grad, grads_odd, sums_odd, grads_even, sums_even)
-
-    def back_none(rows):
-        embedded = jnp.zeros((length, projection.shape[1]), BF)
-        grad_proj = jnp.zeros(projection.shape, F32)
-        grad, grads_odd, sums_odd = layer_zero()
-        _, grads_even, sums_even = layer_zero()
-        return (embedded, grad_proj, grad, grads_odd, sums_odd, grads_even, sums_even)
-
-    embedded, grad_proj, grad_mid, grads_odd, sums_odd, grads_even, sums_even = lax.cond(
-        is_late, back_late, back_none, last
-    )
-    hopped = send(grad_mid, [(2, 0), (3, 1)])
-
-    def back_one(kept, layer):
-        return lambda grad, late: layer_backward(grad, kept, weights, layer, plan)
-
-    grad, grads_odd, sums_odd = lax.cond(
-        is_late, lambda _, late: late, back_one(kept_odd, 1), hopped, (hopped, grads_odd, sums_odd)
-    )
-    shards_odd = sum_shards(kept_odd, grads_odd, core)
-    grad, grads_even, sums_even = lax.cond(
-        is_late, lambda _, late: late, back_one(kept_even, 0), grad, (grad, grads_even, sums_even)
-    )
-    shards_even = sum_shards(kept_even, grads_even, core)
-
-    def owned(even, odd):
+    early, kept_even, kept_odd = both_forward(x)
+    hopped = send(early, [(0, 2), (1, 3)])
+    hopped, head_parts = lax.optimization_barrier((hopped, head_parts))
+
+    def late_turn(rows, *_):
+        last, kept_even, kept_odd = both_forward(rows)
+        embedded, grad_proj, grad = head(last)
+        grad, grads_odd, sums_odd = layer_backward(sel_mine, grad, kept_odd, weights, 1, plan)
+        grad, grads_even, sums_even = layer_backward(sel_mine, grad, kept_even, weights, 0, plan)
+        return (
+            kept_even, kept_odd, embedded, grad_proj, grad,
+            grads_odd, sums_odd, grads_even, sums_even,
+        )
+
+    def early_turn(rows, kept_even, kept_odd):
+        row, ff = jnp.zeros((length, width), BF), jnp.zeros((length, ff_width), BF)
+        grads = (row, ff, row, jnp.zeros((3, length, width), BF))
+        sums = (
+            jnp.zeros((6, width), F32),
+            jnp.zeros((1, ff_width), F32),
+            jnp.zeros((GROUPS, 2, width // GROUPS), F32),
+        )
+        return (
+            kept_even, kept_odd, jnp.zeros((length, 4 * proj_cols), BF),
+            jnp.zeros((width, 4 * proj_cols), BF), row, grads, sums, grads, sums,
+        )
+
+    (
+        kept_even, kept_odd, embedded, grad_proj, grad_mid,
+        late_odd, late_sums_odd, late_even, late_sums_even,
+    ) = lax.cond(is_late, late_turn, early_turn, hopped, kept_even, kept_odd)
+
+    grad = send(grad_mid, [(2, 0), (3, 1)])
+    embedded_cols = embedded.reshape(length, 4, proj_cols).transpose(1, 0, 2)
+
+    rows_of_one = width // SHARDS
+    attend_blocks = (rows_of_one,) * 4
+    feed_blocks = (rows_of_one,) * (ff_width // (2 * HALF)) + (ff_width // SHARDS,)
+
+    def row_sum(value, blocks):
+        return RowSum(value, True) if shards == SHARDS else PlainSum(value, blocks)
+
+    def feed_sum(kept, late, now):
+        args = (kept[4], late[1], now[1], kept[9], late[0], now[0])
+        arrived = swap_cores(feed_grads(sel_theirs, *args))
+        return row_sum(plus(feed_grads(sel_mine, *args), arrived), feed_blocks)
+
+    def attend_parts(kept, late, now, mixed):
+        args = (kept[2], kept[0], late[2], now[2], late[3], mixed)
+        return (attend_grads(sel_theirs, *args), attend_grads(sel_mine, *args))
+
+    def merged(late_sums, sums):
+        return tuple(jnp.where(is_late, a, b) for a, b in zip(late_sums, sums))
+
+    def tie(*values):
+        return lax.optimization_barrier(values)
+
+    grad_context, grads_odd, sums_odd = feed_backward(sel_mine, grad, kept_odd, weights, 1)
+    feed_odd = feed_sum(kept_odd, late_odd, grads_odd)
+    grad_context, feed_odd.value = tie(grad_context, feed_odd.value)
+    feed_odd.step()
+    mixed_odd, mix_sums = mixed_backward(grad_context, kept_odd, plan)
+    sums_odd = merged(late_sums_odd, sums_odd + (mix_sums,))
+    grad = unmix(sel_mine, mixed_odd, weights[0], grads_odd[2], 1)
+    theirs, mine = attend_parts(kept_odd, late_odd, grads_odd, mixed_odd)
+    attend_odd = row_sum(plus(mine, swap_cores(theirs)), attend_blocks)
+    grad, attend_odd.value, feed_odd.value = tie(grad, attend_odd.value, feed_odd.value)
+    feed_odd.step()
+    attend_odd.step()
+
+    grad_context, grads_even, sums_even = feed_backward(sel_mine, grad, kept_even, weights, 0)
+    feed_even = feed_sum(kept_even, late_even, grads_even)
+    grad_context, feed_even.value, feed_odd.travelling, attend_odd.value = tie(
+        grad_context, feed_even.value, feed_odd.travelling, attend_odd.value
+    )
+    feed_odd.step()
+    feed_even.step()
+    attend_odd.step()
+    mixed_even, mix_sums = mixed_backward(grad_context, kept_even, plan)
+    sums_even = merged(late_sums_even, sums_even + (mix_sums,))
+    mixed_even, feed_odd.travelling, attend_odd.travelling = tie(
+        mixed_even, feed_odd.travelling, attend_odd.travelling
+    )
+    feed_odd.step()
+    attend_odd.step()
+    theirs, mine = attend_parts(kept_even, late_even, grads_even, mixed_even)
+    arrived = swap_cores(theirs)
+    grad = unmix(sel_mine, mixed_even, weights[0], grads_even[2], 0)
+
+    def small_rows(sums):
+        sums, up_sums, mix_sums = sums
+        rows = [up_sums[0], mix_sums.transpose(1, 0, 2).reshape(-1)]
+        rows += [sums[n] for n in range(6)]
+        return jnp.concatenate([row.reshape(shards, -1) for row in rows], axis=1)
+
+    extras = jnp.concatenate(
+        [small_rows(sums_even), small_rows(sums_odd), grad_proj.reshape(shards, -1).astype(F32)],
+        axis=1,
+    )
+    small_width = 12 * share
+    lines = -(-extras.shape[1] // HALF)
+    lines = -(-lines // 16) * 16
+    extras = jnp.pad(extras, ((0, 0), (0, lines * HALF - extras.shape[1])))
+    extras = extras.reshape(shards, lines, HALF).astype(BF)
+    extras = plus(extras, swap_cores(extras))
+    attend_even = plus(mine, arrived)
+    if shards == SHARDS:
+        tail = RowSum(jnp.concatenate([attend_even, extras], axis=1), True)
+        feed_odd, attend_odd = feed_odd.result(), attend_odd.result()
+        tail.step()
+        feed_even = feed_even.result()
+        tail = tail.result()
+        attend_even, extras = tail[: 4 * share], tail[4 * share :]
+    else:
+        feed_odd, attend_odd, feed_even = [
+            part.result() for part in (feed_odd, attend_odd, feed_even)
+        ]
+        attend_even = PlainSum(attend_even, attend_blocks).result()
+        extras = lax.psum_scatter(extras, "dp", scatter_dimension=0, tiled=True)[0]
+
+    routes_odd, routes_even = ((0, 1), (2, 3)), ((1, 0), (3, 2))
+
+    def halves(even, odd):
+        arrived = jnp.where(flip, send(odd, routes_odd), send(even, routes_even))
         mine = jnp.where(flip, odd, even)
-        arrived = swap_cores(jnp.where(flip, even, odd))
-        parts = (mine, arrived)
-        return (jnp.where(flip, parts[1], parts[0]), jnp.where(flip, parts[0], parts[1]))
-
-    owned_parts = [owned(even, odd) for even, odd in zip(shards_even, shards_odd)]
-
-    def joined(pair):
-        return jnp.concatenate(pair, axis=1).astype(F32)[None]
-
-    grad_w_down, grad_w_up, grad_w_out = [joined(pair) for pair in owned_parts[:3]]
-    first, second = owned_parts[3]
-    third = first.shape[1] // 3
-    pieces = []
-    for c in range(3):
-        pieces += [first[:, c * third : (c + 1) * third], second[:, c * third : (c + 1) * third]]
-    grad_w_qkv = jnp.concatenate(pieces, axis=1).astype(F32)[None]
-
-    small_even, small_odd = small_sums(sums_even), small_sums(sums_odd)
-    small_mine = jnp.where(flip, small_odd, small_even) + swap_cores(
-        jnp.where(flip, small_even, small_odd)
-    )
-    small_mine = lax.psum_scatter(small_mine, "dp", scatter_dimension=0, tiled=True)[0]
-    share = width // lax.axis_size("dp")
-    at = ff_width // lax.axis_size("dp")
+        return (jnp.where(flip, arrived, mine), jnp.where(flip, mine, arrived))
+
+    blocks = ff_width // (2 * HALF)
+    feed_halves = halves(feed_even, feed_odd)
+    attend_halves = halves(attend_even, attend_odd)
+
+    def columns(pair, first, count):
+        parts = [part[n * share : (n + 1) * share] for part in pair for n in range(first, first + count)]
+        return jnp.concatenate(parts, axis=1).astype(F32)
+
+    grad_w_up = columns(feed_halves, 0, blocks)[None]
+    grad_w_down = jnp.concatenate([part[blocks * share :] for part in feed_halves], axis=1)
+    grad_w_down = grad_w_down.astype(F32)[None]
+    grad_w_out = columns(attend_halves, 0, 1)[None]
+    grad_w_qkv = jnp.concatenate([columns(attend_halves, 1 + c, 1) for c in range(3)], axis=1)[None]
+
+    extras = extras.reshape(-1).astype(F32)
+    small_mine = jnp.where(flip, extras[small_width : 2 * small_width], extras[:small_width])
+    at = ff_width // shards
     grad_b_up = small_mine[None, :at]
     grad_b_qv = small_mine[None, at : at + 2 * share]
     rows = small_mine[at + 2 * share :].reshape(6, share)
-
-    shards = lax.axis_size("dp")
-    proj_cols = w_proj.shape[1]
-    grad_proj = grad_proj.reshape(shards, share, 4, proj_cols).transpose(2, 0, 1, 3)
-    grad_w_proj = lax.psum_scatter(
-        grad_proj.reshape(4 * shards, share * proj_cols),
-        ("section", "dp"),
-        scatter_dimension=0,
-        tiled=True,
-    ).reshape(share, proj_cols)
-
-    spread = lax.all_gather(embedded, "section")[2:]
-    embedded_out = lax.dynamic_slice_in_dim(spread, section_at * proj_cols, proj_cols, 2)
+    grad_proj = extras[2 * small_width : 2 * small_width + share * 4 * proj_cols]
+    grad_proj = grad_proj.reshape(share, 4 * proj_cols).astype(BF)
+    grad_proj = jnp.where(is_late, grad_proj, send(grad_proj, [(2, 0), (3, 1)])).astype(F32)
+    grad_w_proj = lax.dynamic_slice_in_dim(grad_proj, section_at * proj_cols, proj_cols, 1)
+
+    straight_cols = send(pick_row(embedded_cols, core), [(2, 0), (3, 1)])
+    crossed_cols = send(pick_row(embedded_cols, 1 - core), [(2, 1), (3, 0)])
+    near_cols = swap_cores(pick_row(embedded_cols, 3 - core))
+    own_cols = jnp.where(is_late, pick_row(embedded_cols, section_at), straight_cols)
+    other_cols = jnp.where(is_late, near_cols, crossed_cols)
+    embedded_out = jnp.stack(
+        [jnp.where(flip, other_cols, own_cols), jnp.where(flip, own_cols, other_cols)]
+    )
 
     quarters = grad.reshape(4, quarter, width)
-    own_grad = quarters[core]
-    near_grad = swap_cores(quarters[1 - core])
-    straight_grad = send(quarters[2 + core], [(0, 2), (1, 3)])
-    crossed_grad = send(quarters[3 - core], [(0, 3), (1, 2)])
-    mine = jnp.where(is_late, straight_grad, own_grad)
+    straight_grad = send(pick_row(quarters, 2 + core), [(0, 2), (1, 3)])
+    crossed_grad = send(pick_row(quarters, 3 - core), [(0, 3), (1, 2)])
+    near_grad = swap_cores(pick_row(quarters, 1 - core))
+    mine = jnp.where(is_late, straight_grad, pick_row(quarters, core))
     others = jnp.where(is_late, crossed_grad, near_grad)
     grad_in = jnp.stack(
         [jnp.where(flip, others, mine), jnp.where(flip, mine, others)]

time: 1270 us -> 1090 us (0.86)
  waiting for transfers between devices: 610 us -> 127 us
  Pallas kernels: 387 us -> 657 us
  starting transfers between devices: 23.1 us -> 156 us
  blocking collectives: 77 us -> 0 us
  matrix products: 75.4 us -> 6.2 us
  other arithmetic: 23.9 us -> 58.3 us
  local copies, waits for them, and re-layouts: 46.2 us -> 68.5 us
  between operations: 15.4 us -> 2.37 us
    reduce_scatter x6 -> x0, waiting for transfers between devices: 279 us -> none  [sum_shards(): lax.psum_scatter(part, 'dp', scatter_dimension=0, tiled=True)]
    pallas_call x12 -> x24, Pallas kernels: 210 us -> 399 us  [the longest x4 127 us: refine(): pl.pallas_call(partial(refine_kernel, layer), name='refine', grid_spec=pl...]
    unnamed x17 -> x0, waiting for transfers between devices: 150 us -> none
    ppermute x0 -> x28, starting transfers between devices: none -> 112 us  [the longest x12 46.5 us: line(): lax.ppermute(left, 'dp', [(n + 2, n) for n in range(6)])]
    pallas_call x2 -> x4, Pallas kernels: 80.5 us -> 162 us  [attend_backward(): pl.pallas_call(attend_backward_kernel, name='attend_backward', grid_spec=...]
    ppermute x21 -> x29, waiting for transfers between devices: 152 us -> 73.4 us  [send(): return lax.ppermute(value, 'section', routes)]
    dot_general x25 -> x1, matrix products: 71.8 us -> 1.29 us  [dot_tn(): return lax.dot_general(a, b, TN, preferred_element_type=F32)]
    ppermute x0 -> x28, waiting for transfers between devices: none -> 53.3 us  [the longest x12 32 us: line(): lax.ppermute(left, 'dp', [(n + 2, n) for n in range(6)])]
  transfers between devices with their start and end apart: 35 -> 57, of which waited for: 17 -> 15; matrix products, arithmetic and copies ran while one was open for 10% -> 8% of each run, Pallas kernels for 2% -> 18%
where the time goes in v2:
time: 1090 us; the launch traced here: 1080 us
  Pallas kernels  657 us (60%)
  starting transfers between devices  156 us (14%)
  waiting for transfers between devices  127 us (12%)
  local copies, waits for them, and re-layouts  68.5 us (6%)
  other arithmetic  58.3 us (5%)
    pallas_call x4, Pallas kernels, attend_backward(): pl.pallas_call(attend_backward_kernel, name='attend_backward', grid_spec=...  162 us
    pallas_call x4, Pallas kernels, refine(): pl.pallas_call(partial(refine_kernel, layer), name='refine', grid_spec=pl...  127 us
    pallas_call x4, Pallas kernels, refine_back(): pl.pallas_call(partial(refine_back_kernel, layer), name='refine_back', gr...  106 us
    pallas_call x4, Pallas kernels, attend_forward(): pl.pallas_call(attend_forward_kernel, name='attend_forward', grid_spec=pl...  96 us
    ppermute x29, waiting for transfers between devices, send(): return lax.ppermute(value, 'section', routes)  73.4 us
    pallas_call x4, Pallas kernels, feed_grads(): pl.pallas_call(feed_grads_kernel, name='feed_grads', grid_spec=pltpu.Pref...  62.6 us
    ppermute x12, starting transfers between devices, line(): lax.ppermute(left, 'dp', [(n + 2, n) for n in range(6)])  46.5 us
    ppermute x29, starting transfers between devices, send(): return lax.ppermute(value, 'section', routes)  43.8 us
  transfers between devices with their start and end apart: 57, of which 15 were waited for; matrix products, arithmetic and copies ran while one was open for 8% of the time, Pallas kernels for 18%

profile of v2, /device:TPU:13, one launch (start us, length us, event | category | flops | bytes accessed | tf_op | source)
XLA Modules:
  0.0 1075.0 jit_solution(15633553817552693929)
XLA Ops:
  38.9 24.0 %attend_forward.6 = (bf16[1024,768]{1,0:T(8,128)(2,1)}, f32[2,24,256]{2,1,0:T(8,128)}) custom-call(s32[8]{0:T(128)S(1)} %get-tuple-element.414.begin_ref, s32[8]{0:T(128)S(1)} %get-tuple-element.415.count_ref, bf16[3,1024,768]{2,1,0:T(8,128)(2,1)} %mix.6.qkv_ref, f32[1024,128]{1,0:T(8,128)} %broadcast_in_dim.62.key_code_ref, ...), custom_call_target="tpu_custom_call" | custom-call | flops 1 | bytes 1 | tf_op jit(solution)/shard_map/attend_forward/pallas_call | solution.py:168
  62.9 31.6 %refine.6 = (bf16[1024,768]{1,0:T(8,128)(2,1)}, bf16[1024,768]{1,0:T(8,128)(2,1)}, bf16[1024,768]{1,0:T(8,128)(2,1)}, bf16[1024,768]{1,0:T(8,128)(2,1)}, f32[102...) custom-call(s32[3]{0:T(128)S(1)} %pad_add_fusion.sel_ref, ...), custom_call_target="tpu_custom_call" | custom-call | flops 1 | bytes 1 | tf_op jit(solution)/shard_map/refine/pallas_call | solution.py:486
  102.5 24.0 %attend_forward.7 = (bf16[1024,768]{1,0:T(8,128)(2,1)}, f32[2,24,256]{2,1,0:T(8,128)}) custom-call(s32[8]{0:T(128)S(1)} %get-tuple-element.414.begin_ref, s32[8]{0:T(128)S(1)} %get-tuple-element.415.count_ref, bf16[3,1024,768]{2,1,0:T(8,128)(2,1)} %mix.7.qkv_ref, f32[1024,128]{1,0:T(8,128)} %broadcast_in_dim.62.key_code_ref, ...), custom_call_target="tpu_custom_call" | custom-call | flops 1 | bytes 1 | tf_op jit(solution)/shard_map/attend_forward/pallas_call | solution.py:168
  126.4 32.0 %refine.7 = (bf16[1024,768]{1,0:T(8,128)(2,1)}, bf16[1024,768]{1,0:T(8,128)(2,1)}, bf16[1024,768]{1,0:T(8,128)(2,1)}, bf16[1024,768]{1,0:T(8,128)(2,1)}, f32[102...) custom-call(s32[3]{0:T(128)S(1)} %pad_add_fusion.sel_ref, ...), custom_call_target="tpu_custom_call" | custom-call | flops 1 | bytes 1 | tf_op jit(solution)/shard_map/refine/pallas_call | solution.py:486
  173.8 25.1 %collective-permute-done.10 = bf16[448,128]{1,0:T(8,128)(2,1)} collective-permute-done((bf16[448,128]{1,0:T(8,128)(2,1)}, bf16[448,128]{1,0:T(8,128)(2,1)}, u32[]{:S(2)}, u32[]{:S(2)}) %collective-permute-start.10) | collective-permute-done | bytes 114720 | tf_op jit(solution)/shard_map/ppermute | solution.py:774
  201.7 310.4 %conditional.1 = (bf16[1024,768]{1,0:T(8,128)(2,1)}, bf16[3,1024,768]{2,1,0:T(8,128)(2,1)}, bf16[1024,768]{1,0:T(8,128)(2,1)}, f32[2,24,256]{2,1,0:T(8,128)}, bf...) conditional(s32[]{:T(128)} %convert_element_type.444, ...), branch_computations={%region_3.4_spmd, %region_4.7_spmd} | conditional | flops 610338816 | bytes 65905212 | solution.py:955
  210.6 24.0 %attend_forward.4 = (bf16[1024,768]{1,0:T(8,128)(2,1)}, f32[2,24,256]{2,1,0:T(8,128)}) custom-call(s32[8]{0:T(128)S(1)} %get-tuple-element.113.begin_ref, s32[8]{0:T(128)S(1)} %get-tuple-element.114.count_ref, bf16[3,1024,768]{2,1,0:T(8,128)(2,1)} %mix.4.qkv_ref, f32[1024,128]{1,0:T(8,128)} %get-tuple-element.115.key_code_ref, ...), custom_call_target="tpu_custom_call" | custom-call | flops 1 | bytes 1 | tf_op jit(solution)/shard_map/cond/branch_1_fun/attend_forward/pallas_call | solution.py:168
  234.6 31.9 %refine.4 = (bf16[1024,768]{1,0:T(8,128)(2,1)}, bf16[1024,768]{1,0:T(8,128)(2,1)}, bf16[1024,768]{1,0:T(8,128)(2,1)}, bf16[1024,768]{1,0:T(8,128)(2,1)}, f32[102...) custom-call(s32[3]{0:T(128)S(1)} %get-tuple-element.109.sel_ref, ...), custom_call_target="tpu_custom_call" | custom-call | flops 1 | bytes 1 | tf_op jit(solution)/shard_map/cond/branch_1_fun/refine/pallas_call | solution.py:486
  274.4 24.0 %attend_forward.5 = (bf16[1024,768]{1,0:T(8,128)(2,1)}, f32[2,24,256]{2,1,0:T(8,128)}) custom-call(s32[8]{0:T(128)S(1)} %get-tuple-element.113.begin_ref, s32[8]{0:T(128)S(1)} %get-tuple-element.114.count_ref, bf16[3,1024,768]{2,1,0:T(8,128)(2,1)} %mix.5.qkv_ref, f32[1024,128]{1,0:T(8,128)} %get-tuple-element.115.key_code_ref, ...), custom_call_target="tpu_custom_call" | custom-call | flops 1 | bytes 1 | tf_op jit(solution)/shard_map/cond/branch_1_fun/attend_forward/pallas_call | solution.py:168
  298.3 31.8 %refine.5 = (bf16[1024,768]{1,0:T(8,128)(2,1)}, bf16[1024,768]{1,0:T(8,128)(2,1)}, bf16[1024,768]{1,0:T(8,128)(2,1)}, bf16[1024,768]{1,0:T(8,128)(2,1)}, f32[102...) custom-call(s32[3]{0:T(128)S(1)} %get-tuple-element.109.sel_ref, ...), custom_call_target="tpu_custom_call" | custom-call | flops 1 | bytes 1 | tf_op jit(solution)/shard_map/cond/branch_1_fun/refine/pallas_call | solution.py:486
  357.7 27.3 %refine_back.4 = (bf16[1024,768]{1,0:T(8,128)(2,1)}, bf16[1024,3072]{1,0:T(8,128)(2,1)}, bf16[1024,768]{1,0:T(8,128)(2,1)}, bf16[1024,768]{1,0:T(8,128)(2,1)}, f32[6,768]{1,0:T(8,128)}, /*index=5*/f32[1,3072]{1,0:T(1,128)}) custom-call(s32[3]{0:T(128)S(1)} %get-tuple-element.109.sel_ref, bf16[1024,768]{1,0:T(8,128)(2,1)} %convolution_convert_fusion.grad_ref, ...), custom_call_target="tpu_custom_call" | custom-call | flops 1 | bytes 1 | tf_op jit(solution)/shard_map/cond/branch_1_fun/refine_back/pallas_call | solution.py:575
  385.0 39.7 %attend_backward.4 = (bf16[3,1024,768]{2,1,0:T(8,128)(2,1)}, f32[2,2,384]{2,1,0:T(2,128)}) custom-call(s32[8]{0:T(128)S(1)} %get-tuple-element.113.begin_ref, s32[8]{0:T(128)S(1)} %get-tuple-element.114.count_ref, bf16[3,1024,768]{2,1,0:T(8,128)(2,1)S(1)} %bitcast.251, f32[1024,128]{1,0:T(8,128)} %get-tuple-element.115.key_code_ref, ...), custom_call_target="tpu_custom_call" | custom-call | flops 1 | bytes 1 | tf_op jit(solution)/shard_map/cond/branch_1_fun/attend_backward/pallas_call | solution.py:269
  424.7 9.1 unmix.4.grad_ref
  433.8 25.9 %refine_back.5 = (bf16[1024,768]{1,0:T(8,128)(2,1)}, bf16[1024,3072]{1,0:T(8,128)(2,1)}, bf16[1024,768]{1,0:T(8,128)(2,1)}, bf16[1024,768]{1,0:T(8,128)(2,1)}, f32[6,768]{1,0:T(8,128)}, /*index=5*/f32[1,3072]{1,0:T(1,128)}) custom-call(s32[3]{0:T(128)S(1)} %get-tuple-element.109.sel_ref, bf16[1024,768]{1,0:T(8,128)(2,1)} %unmix.4.grad_ref, ...), custom_call_target="tpu_custom_call" | custom-call | flops 1 | bytes 1 | tf_op jit(solution)/shard_map/cond/branch_1_fun/refine_back/pallas_call | solution.py:575
  459.7 40.6 %attend_backward.5 = (bf16[3,1024,768]{2,1,0:T(8,128)(2,1)}, f32[2,2,384]{2,1,0:T(2,128)}) custom-call(s32[8]{0:T(128)S(1)} %get-tuple-element.113.begin_ref, s32[8]{0:T(128)S(1)} %get-tuple-element.114.count_ref, bf16[3,1024,768]{2,1,0:T(8,128)(2,1)} %mix.4.qkv_ref, f32[1024,128]{1,0:T(8,128)} %get-tuple-element.115.key_code_ref, ...), custom_call_target="tpu_custom_call" | custom-call | flops 1 | bytes 1 | tf_op jit(solution)/shard_map/cond/branch_1_fun/attend_backward/pallas_call | solution.py:269
  500.3 9.0 unmix.5
  514.1 33.8 %collective-permute-done.15.grad_ref = bf16[1024,768]{1,0:T(8,128)(2,1)S(1)} collective-permute-done((bf16[1024,768]{1,0:T(8,128)(2,1)}, bf16[1024,768]{1,0:T(8,128)(2,1)S(1)}, u32[]{:S(2)}, u32[]{:S(2)}) %collective-permute-start.15) | collective-permute-done | bytes 1572896 | tf_op jit(solution)/shard_map/ppermute | solution.py:774
  549.1 26.7 %refine_back.6 = (bf16[1024,768]{1,0:T(8,128)(2,1)}, bf16[1024,3072]{1,0:T(8,128)(2,1)}, bf16[1024,768]{1,0:T(8,128)(2,1)}, bf16[1024,768]{1,0:T(8,128)(2,1)}, f32[6,768]{1,0:T(8,128)}, /*index=5*/f32[1,3072]{1,0:T(1,128)}) custom-call(s32[3]{0:T(128)S(1)} %pad_add_fusion.sel_ref, bf16[1024,768]{1,0:T(8,128)(2,1)} %copy-done.23, ...), custom_call_target="tpu_custom_call" | custom-call | flops 1 | bytes 1 | tf_op jit(solution)/shard_map/refine_back/pallas_call | solution.py:575
  575.8 15.1 %feed_grads.5 = bf16[8,768,384]{2,1,0:T(8,128)(2,1)} custom-call(s32[3]{0:T(128)} %pad_add_fusion.2.sel_ref, bf16[1024,768]{1,0:T(8,128)(2,1)S(1)} %copy-done.21, bf16[1024,3072]{1,0:T(8,128)(2,1)} %get-tuple-element.312.raised_late_ref, bf16[1024,3072]{1,0:T(8,128)(2,1)} %get-tuple-element.313.raised_ref, bf16[1024,3072]{1,0:T(8,128)(2,1)} %get-tuple-element.314.active_ref, ...), custom_call_target="tpu_custom_call" | custom-call | flops 1 | bytes 1 | tf_op jit(solution)/shard_map/feed_grads/pallas_call | solution.py:651
  591.1 16.1 %feed_grads.4 = bf16[8,768,384]{2,1,0:T(8,128)(2,1)} custom-call(s32[3]{0:T(128)S(1)} %pad_add_fusion.sel_ref, bf16[1024,768]{1,0:T(8,128)(2,1)} %get-tuple-element.311.hidden_ref, bf16[1024,3072]{1,0:T(8,128)(2,1)} %get-tuple-element.312.raised_late_ref, bf16[1024,3072]{1,0:T(8,128)(2,1)} %get-tuple-element.313.raised_ref, ...), custom_call_target="tpu_custom_call" | custom-call | flops 1 | bytes 1 | tf_op jit(solution)/shard_map/feed_grads/pallas_call | solution.py:651
  615.3 12.8 %collective-permute-start.18 = (bf16[4,768,384]{2,1,0:T(8,128)(2,1)}, bf16[4,768,384]{2,1,0:T(8,128)(2,1)}, u32[]{:S(2)}, u32[]{:S(2)}) collective-permute-start(bf16[4,768,384]{2,1,0:T(8,128)(2,1)} %dynamic-slice_bitcast_fusion.1), channel_id=1, source_target_pairs={{0,1},{1,0},{2,3},{3,2},{4,5},{5,4},{6,7},{7,6},{8,9},{9,8},{10,11... | collective-permute-start | bytes 7077896 | tf_op jit(solution)/shard_map/ppermute | solution.py:799
  628.1 39.9 %attend_backward.6 = (bf16[3,1024,768]{2,1,0:T(8,128)(2,1)}, f32[2,2,384]{2,1,0:T(2,128)}) custom-call(s32[8]{0:T(128)S(1)} %get-tuple-element.414.begin_ref, s32[8]{0:T(128)S(1)} %get-tuple-element.415.count_ref, bf16[3,1024,768]{2,1,0:T(8,128)(2,1)} %get-tuple-element.301.qkv_ref, f32[1024,128]{1,0:T(8,128)S(1)} %copy-done.7, ...), custom_call_target="tpu_custom_call" | custom-call | flops 1 | bytes 1 | tf_op jit(solution)/shard_map/attend_backward/pallas_call | solution.py:269
  676.3 9.4 attend_grads.4
  685.7 8.8 unmix.6.grad_ref
  702.6 26.0 %refine_back.7 = (bf16[1024,768]{1,0:T(8,128)(2,1)}, bf16[1024,3072]{1,0:T(8,128)(2,1)}, bf16[1024,768]{1,0:T(8,128)(2,1)}, bf16[1024,768]{1,0:T(8,128)(2,1)}, f32[6,768]{1,0:T(8,128)}, /*index=5*/f32[1,3072]{1,0:T(1,128)}) custom-call(s32[3]{0:T(128)S(1)} %pad_add_fusion.sel_ref, bf16[1024,768]{1,0:T(8,128)(2,1)} %unmix.6.grad_ref, ...), custom_call_target="tpu_custom_call" | custom-call | flops 1 | bytes 1 | tf_op jit(solution)/shard_map/refine_back/pallas_call | solution.py:575
  728.7 15.8 %feed_grads.7 = bf16[8,768,384]{2,1,0:T(8,128)(2,1)} custom-call(s32[3]{0:T(128)} %pad_add_fusion.2.sel_ref, bf16[1024,768]{1,0:T(8,128)(2,1)} %get-tuple-element.331.hidden_ref, bf16[1024,3072]{1,0:T(8,128)(2,1)} %get-tuple-element.332.raised_late_ref, bf16[1024,3072]{1,0:T(8,128)(2,1)} %get-tuple-element.333.raised_ref, ...), custom_call_target="tpu_custom_call" | custom-call | flops 1 | bytes 1 | tf_op jit(solution)/shard_map/feed_grads/pallas_call | solution.py:651
  754.7 15.7 %feed_grads.6 = bf16[8,768,384]{2,1,0:T(8,128)(2,1)} custom-call(s32[3]{0:T(128)S(1)} %pad_add_fusion.sel_ref, bf16[1024,768]{1,0:T(8,128)(2,1)} %get-tuple-element.331.hidden_ref, bf16[1024,3072]{1,0:T(8,128)(2,1)} %get-tuple-element.332.raised_late_ref, bf16[1024,3072]{1,0:T(8,128)(2,1)} %get-tuple-element.333.raised_ref, ...), custom_call_target="tpu_custom_call" | custom-call | flops 1 | bytes 1 | tf_op jit(solution)/shard_map/feed_grads/pallas_call | solution.py:651
  773.5 15.0 %collective-permute-start.21 = (bf16[768,384]{1,0:T(8,128)(2,1)}, bf16[768,384]{1,0:T(8,128)(2,1)}, u32[]{:S(2)}, u32[]{:S(2)}) collective-permute-start(bf16[768,384]{1,0:T(8,128)(2,1)} %get-tuple-element.442), channel_id=1, source_target_pairs={{2,0},{3,1},{4,2},{5,3},{6,4},{7,5},{10,8},{11,9},{12,10},{13,11},... | collective-permute-start | bytes 1769480 | tf_op jit(solution)/shard_map/ppermute | solution.py:811
  829.5 41.4 %attend_backward.7 = (bf16[3,1024,768]{2,1,0:T(8,128)(2,1)}, f32[2,2,384]{2,1,0:T(2,128)}) custom-call(s32[8]{0:T(128)S(1)} %get-tuple-element.414.begin_ref, s32[8]{0:T(128)S(1)} %get-tuple-element.415.count_ref, bf16[3,1024,768]{2,1,0:T(8,128)(2,1)} %get-tuple-element.298.qkv_ref, f32[1024,128]{1,0:T(8,128)} %broadcast_in_dim.62.key_code_ref, ...), custom_call_target="tpu_custom_call" | custom-call | flops 1 | bytes 1 | tf_op jit(solution)/shard_map/attend_backward/pallas_call | solution.py:269
  919.3 9.0 unmix.7
  930.7 10.3 collective-permute-start.49
  986.0 21.4 %collective-permute-done.53 = bf16[768,384]{1,0:T(8,128)(2,1)S(1)} collective-permute-done((bf16[768,384]{1,0:T(8,128)(2,1)S(1)}, bf16[768,384]{1,0:T(8,128)(2,1)S(1)}, u32[]{:S(2)}, u32[]{:S(2)}) %collective-permute-start.53) | collective-permute-done | bytes 589856 | tf_op jit(solution)/shard_map/ppermute | solution.py:811
  (369 shorter events, 355.2 us)
Async XLA Ops:
  9.6 53.3 %collective-permute-start.6 = (bf16[768,3072]{1,0:T(8,128)(2,1)}, bf16[768,3072]{1,0:T(8,128)(2,1)}, u32[]{:S(2)}, u32[]{:S(2)}) collective-permute-start(bf16[768,3072]{1,0:T(8,128)(2,1)} %bitcast.224), channel_id=1, source_target_pairs={{0,8},{8,0},{16,24},{24,16},{1,9},{9,1},{17,25},{25,17},{2,10},{10... | collective-permute-start | bytes 14155784 | tf_op jit(solution)/shard_map/ppermute | solution.py:774
  9.7 53.2 %collective-permute-start.7 = (bf16[3072,768]{1,0:T(8,128)(2,1)}, bf16[3072,768]{1,0:T(8,128)(2,1)}, u32[]{:S(2)}, u32[]{:S(2)}) collective-permute-start(bf16[3072,768]{1,0:T(8,128)(2,1)} %bitcast.238), channel_id=1, source_target_pairs={{0,8},{8,0},{16,24},{24,16},{1,9},{9,1},{17,25},{25,17},{2,10},{10... | collective-permute-start | bytes 14155784 | tf_op jit(solution)/shard_map/ppermute | solution.py:774
  12.0 50.9 %collective-permute-start.5 = (bf16[768,768]{1,0:T(8,128)(2,1)}, bf16[768,768]{1,0:T(8,128)(2,1)}, u32[]{:S(2)}, u32[]{:S(2)}) collective-permute-start(bf16[768,768]{1,0:T(8,128)(2,1)} %bitcast.252), channel_id=1, source_target_pairs={{0,8},{8,0},{16,24},{24,16},{1,9},{9,1},{17,25},{25,17},{2,10},{10... | collective-permute-start | bytes 3538952 | tf_op jit(solution)/shard_map/ppermute | solution.py:774
  158.5 43.3 %collective-permute-start.8 = (bf16[1024,768]{1,0:T(8,128)(2,1)}, bf16[1024,768]{1,0:T(8,128)(2,1)}, u32[]{:S(2)}, u32[]{:S(2)}) collective-permute-start(bf16[1024,768]{1,0:T(8,128)(2,1)} %get-tuple-element.291), channel_id=1, source_target_pairs={{0,16},{8,24},{1,17},{9,25},{2,18},{10,26},{3,19},{11,27},{4,20},{... | collective-permute-start | bytes 4718600 | tf_op jit(solution)/shard_map/ppermute | solution.py:774
  165.3 33.7 %collective-permute-start.10 = (bf16[448,128]{1,0:T(8,128)(2,1)}, bf16[448,128]{1,0:T(8,128)(2,1)}, u32[]{:S(2)}, u32[]{:S(2)}) collective-permute-start(bf16[448,128]{1,0:T(8,128)(2,1)} %reshape.360), channel_id=1, source_target_pairs={{0,16},{8,24},{1,17},{9,25},{2,18},{10,26},{3,19},{11,27},{4,20},{... | collective-permute-start | bytes 344072 | tf_op jit(solution)/shard_map/ppermute | solution.py:774
  170.5 31.3 %collective-permute-start.11 = (bf16[448,128]{1,0:T(8,128)(2,1)}, bf16[448,128]{1,0:T(8,128)(2,1)}, u32[]{:S(2)}, u32[]{:S(2)}) collective-permute-start(bf16[448,128]{1,0:T(8,128)(2,1)} %reshape.361), channel_id=1, source_target_pairs={{0,24},{8,16},{1,25},{9,17},{2,26},{10,18},{3,27},{11,19},{4,28},{... | collective-permute-start | bytes 344072 | tf_op jit(solution)/shard_map/ppermute | solution.py:774
  171.7 30.0 %collective-permute-start.9 = (bf16[448,128]{1,0:T(8,128)(2,1)}, bf16[448,128]{1,0:T(8,128)(2,1)}, u32[]{:S(2)}, u32[]{:S(2)}) collective-permute-start(bf16[448,128]{1,0:T(8,128)(2,1)} %reshape.361), channel_id=1, source_target_pairs={{16,24},{24,16},{17,25},{25,17},{18,26},{26,18},{19,27},{27,19},{2... | collective-permute-start | bytes 344072 | tf_op jit(solution)/shard_map/ppermute | solution.py:774
  512.1 35.8 %collective-permute-start.15 = (bf16[1024,768]{1,0:T(8,128)(2,1)}, bf16[1024,768]{1,0:T(8,128)(2,1)S(1)}, u32[]{:S(2)}, u32[]{:S(2)}) collective-permute-start(bf16[1024,768]{1,0:T(8,128)(2,1)} %get-tuple-element.304), channel_id=1, source_target_pairs={{16,0},{24,8},{17,1},{25,9},{18,2},{26,10},{19,3},{27,11},{20,4},{... | collective-permute-start | bytes 4718600 | tf_op jit(solution)/shard_map/ppermute | solution.py:774
  615.3 79.2 %collective-permute-start.18 = (bf16[4,768,384]{2,1,0:T(8,128)(2,1)}, bf16[4,768,384]{2,1,0:T(8,128)(2,1)}, u32[]{:S(2)}, u32[]{:S(2)}) collective-permute-start(bf16[4,768,384]{2,1,0:T(8,128)(2,1)} %dynamic-slice_bitcast_fusion.1), channel_id=1, source_target_pairs={{0,1},{1,0},{2,3},{3,2},{4,5},{5,4},{6,7},{7,6},{8,9},{9,8},{10,11... | collective-permute-start | bytes 7077896 | tf_op jit(solution)/shard_map/ppermute | solution.py:799
  744.4 45.7 %collective-permute-start.19 = (bf16[8,768,384]{2,1,0:T(8,128)(2,1)}, bf16[8,768,384]{2,1,0:T(8,128)(2,1)}, u32[]{:S(2)}, u32[]{:S(2)}) collective-permute-start(bf16[8,768,384]{2,1,0:T(8,128)(2,1)} %feed_grads.7), channel_id=1, source_target_pairs={{0,8},{8,0},{16,24},{24,16},{1,9},{9,1},{17,25},{25,17},{2,10},{10... | collective-permute-start | bytes 14155784 | tf_op jit(solution)/shard_map/ppermute | solution.py:774
  746.3 42.2 %collective-permute-start.22 = (bf16[4,384,384]{2,1,0:T(8,128)(2,1)}, bf16[4,384,384]{2,1,0:T(8,128)(2,1)}, u32[]{:S(2)}, u32[]{:S(2)}) collective-permute-start(bf16[4,384,384]{2,1,0:T(8,128)(2,1)} %dynamic-slice_bitcast_fusion.3), channel_id=1, source_target_pairs={{0,1},{1,0},{2,3},{3,2},{4,5},{5,4},{6,7},{7,6},{8,9},{9,8},{10,11... | collective-permute-start | bytes 3538952 | tf_op jit(solution)/shard_map/ppermute | solution.py:799
  771.5 27.9 %collective-permute-start.20 = (bf16[768,384]{1,0:T(8,128)(2,1)}, bf16[768,384]{1,0:T(8,128)(2,1)}, u32[]{:S(2)}, u32[]{:S(2)}) collective-permute-start(bf16[768,384]{1,0:T(8,128)(2,1)} %get-tuple-element.443), channel_id=1, source_target_pairs={{0,2},{1,3},{2,4},{3,5},{4,6},{5,7},{8,10},{9,11},{10,12},{11,13},... | collective-permute-start | bytes 1769480 | tf_op jit(solution)/shard_map/ppermute | solution.py:810
  773.5 27.5 %collective-permute-start.21 = (bf16[768,384]{1,0:T(8,128)(2,1)}, bf16[768,384]{1,0:T(8,128)(2,1)}, u32[]{:S(2)}, u32[]{:S(2)}) collective-permute-start(bf16[768,384]{1,0:T(8,128)(2,1)} %get-tuple-element.442), channel_id=1, source_target_pairs={{2,0},{3,1},{4,2},{5,3},{6,4},{7,5},{10,8},{11,9},{12,10},{13,11},... | collective-permute-start | bytes 1769480 | tf_op jit(solution)/shard_map/ppermute | solution.py:811
  803.6 73.2 %collective-permute-start.23 = (bf16[768,384]{1,0:T(8,128)(2,1)}, bf16[768,384]{1,0:T(8,128)(2,1)}, u32[]{:S(2)}, u32[]{:S(2)}) collective-permute-start(bf16[768,384]{1,0:T(8,128)(2,1)} %get-tuple-element.441), channel_id=1, source_target_pairs={{0,2},{1,3},{2,4},{3,5},{4,6},{5,7},{8,10},{9,11},{10,12},{11,13},... | collective-permute-start | bytes 1769480 | tf_op jit(solution)/shard_map/ppermute | solution.py:810
  805.5 73.1 %collective-permute-start.24 = (bf16[768,384]{1,0:T(8,128)(2,1)}, bf16[768,384]{1,0:T(8,128)(2,1)}, u32[]{:S(2)}, u32[]{:S(2)}) collective-permute-start(bf16[768,384]{1,0:T(8,128)(2,1)} %get-tuple-element.440), channel_id=1, source_target_pairs={{2,0},{3,1},{4,2},{5,3},{6,4},{7,5},{10,8},{11,9},{12,10},{13,11},... | collective-permute-start | bytes 1769480 | tf_op jit(solution)/shard_map/ppermute | solution.py:811
  811.6 116.7 %collective-permute-start.48 = (bf16[4,768,384]{2,1,0:T(8,128)(2,1)}, bf16[4,768,384]{2,1,0:T(8,128)(2,1)}, u32[]{:S(2)}, u32[]{:S(2)}) collective-permute-start(bf16[4,768,384]{2,1,0:T(8,128)(2,1)} %dynamic-slice_bitcast_fusion), channel_id=1, source_target_pairs={{0,1},{1,0},{2,3},{3,2},{4,5},{5,4},{6,7},{7,6},{8,9},{9,8},{10,11... | collective-permute-start | bytes 7077896 | tf_op jit(solution)/shard_map/ppermute | solution.py:799
  814.4 56.6 %collective-permute-start.25 = (bf16[384,384]{1,0:T(8,128)(2,1)}, bf16[384,384]{1,0:T(8,128)(2,1)}, u32[]{:S(2)}, u32[]{:S(2)}) collective-permute-start(bf16[384,384]{1,0:T(8,128)(2,1)} %get-tuple-element.456), channel_id=1, source_target_pairs={{0,2},{1,3},{2,4},{3,5},{4,6},{5,7},{8,10},{9,11},{10,12},{11,13},... | collective-permute-start | bytes 884744 | tf_op jit(solution)/shard_map/ppermute | solution.py:810
  816.3 56.8 %collective-permute-start.26 = (bf16[384,384]{1,0:T(8,128)(2,1)}, bf16[384,384]{1,0:T(8,128)(2,1)}, u32[]{:S(2)}, u32[]{:S(2)}) collective-permute-start(bf16[384,384]{1,0:T(8,128)(2,1)} %get-tuple-element.455), channel_id=1, source_target_pairs={{2,0},{3,1},{4,2},{5,3},{6,4},{7,5},{10,8},{11,9},{12,10},{13,11},... | collective-permute-start | bytes 884744 | tf_op jit(solution)/shard_map/ppermute | solution.py:811
  871.0 32.0 %collective-permute-start.12 = (bf16[1024,32]{0,1:T(8,128)(2,1)}, bf16[1024,32]{0,1:T(8,128)(2,1)}, u32[]{:S(2)}, u32[]{:S(2)}) collective-permute-start(bf16[1024,32]{0,1:T(8,128)(2,1)} %get-tuple-element.467), channel_id=1, source_target_pairs={{0,8},{8,0},{16,24},{24,16},{1,9},{9,1},{17,25},{25,17},{2,10},{10... | collective-permute-start | bytes 196616 | tf_op jit(solution)/shard_map/ppermute | solution.py:774
  873.1 29.9 %collective-permute-start.13 = (bf16[1024,32]{0,1:T(8,128)(2,1)}, bf16[1024,32]{0,1:T(8,128)(2,1)}, u32[]{:S(2)}, u32[]{:S(2)}) collective-permute-start(bf16[1024,32]{0,1:T(8,128)(2,1)} %get-tuple-element.466), channel_id=1, source_target_pairs={{16,8},{24,0},{17,9},{25,1},{18,10},{26,2},{19,11},{27,3},{20,12},... | collective-permute-start | bytes 196616 | tf_op jit(solution)/shard_map/ppermute | solution.py:774
  876.7 26.3 %collective-permute-start.14 = (bf16[1024,32]{0,1:T(8,128)(2,1)}, bf16[1024,32]{0,1:T(8,128)(2,1)}, u32[]{:S(2)}, u32[]{:S(2)}) collective-permute-start(bf16[1024,32]{0,1:T(8,128)(2,1)} %get-tuple-element.465), channel_id=1, source_target_pairs={{16,0},{24,8},{17,1},{25,9},{18,2},{26,10},{19,3},{27,11},{20,4},{... | collective-permute-start | bytes 196616 | tf_op jit(solution)/shard_map/ppermute | solution.py:774
  887.1 55.9 %collective-permute-start.35 = (bf16[8,384,384]{2,1,0:T(8,128)(2,1)}, bf16[8,384,384]{2,1,0:T(8,128)(2,1)}, u32[]{:S(2)}, u32[]{:S(2)}) collective-permute-start(bf16[8,384,384]{2,1,0:T(8,128)(2,1)} %attend_grads.7), channel_id=1, source_target_pairs={{0,8},{8,0},{16,24},{24,16},{1,9},{9,1},{17,25},{25,17},{2,10},{10... | collective-permute-start | bytes 7077896 | tf_op jit(solution)/shard_map/ppermute | solution.py:774
  916.2 44.7 %collective-permute-start.30 = (bf16[384,384]{1,0:T(8,128)(2,1)}, bf16[384,384]{1,0:T(8,128)(2,1)}, u32[]{:S(2)}, u32[]{:S(2)}) collective-permute-start(bf16[384,384]{1,0:T(8,128)(2,1)} %fusion.29), channel_id=1, source_target_pairs={{0,2},{1,3},{2,4},{3,5},{4,6},{5,7},{8,10},{9,11},{10,12},{11,13},... | collective-permute-start | bytes 884744 | tf_op jit(solution)/shard_map/ppermute | solution.py:810
  945.7 36.4 %collective-permute-start.37 = (bf16[4,432,384]{2,1,0:T(8,128)(2,1)S(1)}, bf16[4,432,384]{2,1,0:T(8,128)(2,1)S(1)}, u32[]{:S(2)}, u32[]{:S(2)}) collective-permute-start(bf16[4,432,384]{2,1,0:T(8,128)(2,1)S(1)} %dynamic-slice_bitcast_fusion.2), channel_id=1, source_target_pairs={{0,1},{1,0},{2,3},{3,2},{4,5},{5,4},{6,7},{7,6},{8,9},{9,8},{10,11... | collective-permute-start | bytes 3981320 | tf_op jit(solution)/shard_map/ppermute | solution.py:799
  969.4 40.9 %collective-permute-start.45 = (bf16[768,384]{1,0:T(8,128)(2,1)S(1)}, bf16[768,384]{1,0:T(8,128)(2,1)S(1)}, u32[]{:S(2)}, u32[]{:S(2)}) collective-permute-start(bf16[768,384]{1,0:T(8,128)(2,1)S(1)} %get-tuple-element.438), channel_id=1, source_target_pairs={{0,2},{1,3},{2,4},{3,5},{4,6},{5,7},{8,10},{9,11},{10,12},{11,13},... | collective-permute-start | bytes 1769480 | tf_op jit(solution)/shard_map/ppermute | solution.py:810
  973.9 38.3 %collective-permute-start.46 = (bf16[768,384]{1,0:T(8,128)(2,1)S(1)}, bf16[768,384]{1,0:T(8,128)(2,1)S(1)}, u32[]{:S(2)}, u32[]{:S(2)}) collective-permute-start(bf16[768,384]{1,0:T(8,128)(2,1)S(1)} %get-tuple-element.439), channel_id=1, source_target_pairs={{2,0},{3,1},{4,2},{5,3},{6,4},{7,5},{10,8},{11,9},{12,10},{13,11},... | collective-permute-start | bytes 1769480 | tf_op jit(solution)/shard_map/ppermute | solution.py:811
  975.8 42.1 %collective-permute-start.32 = (bf16[384,384]{1,0:T(8,128)(2,1)S(1)}, bf16[384,384]{1,0:T(8,128)(2,1)S(1)}, u32[]{:S(2)}, u32[]{:S(2)}) collective-permute-start(bf16[384,384]{1,0:T(8,128)(2,1)S(1)} %get-tuple-element.454), channel_id=1, source_target_pairs={{2,0},{3,1},{4,2},{5,3},{6,4},{7,5},{10,8},{11,9},{12,10},{13,11},... | collective-permute-start | bytes 884744 | tf_op jit(solution)/shard_map/ppermute | solution.py:811
  980.1 27.3 %collective-permute-start.53 = (bf16[768,384]{1,0:T(8,128)(2,1)S(1)}, bf16[768,384]{1,0:T(8,128)(2,1)S(1)}, u32[]{:S(2)}, u32[]{:S(2)}) collective-permute-start(bf16[768,384]{1,0:T(8,128)(2,1)S(1)} %get-tuple-element.435), channel_id=1, source_target_pairs={{2,0},{3,1},{4,2},{5,3},{6,4},{7,5},{10,8},{11,9},{12,10},{13,11},... | collective-permute-start | bytes 1769480 | tf_op jit(solution)/shard_map/ppermute | solution.py:811
  982.1 64.8 %collective-permute-start.31 = (bf16[384,384]{1,0:T(8,128)(2,1)S(1)}, bf16[384,384]{1,0:T(8,128)(2,1)S(1)}, u32[]{:S(2)}, u32[]{:S(2)}) collective-permute-start(bf16[384,384]{1,0:T(8,128)(2,1)S(1)} %get-tuple-element.453), channel_id=1, source_target_pairs={{0,2},{1,3},{2,4},{3,5},{4,6},{5,7},{8,10},{9,11},{10,12},{11,13},... | collective-permute-start | bytes 884744 | tf_op jit(solution)/shard_map/ppermute | solution.py:810
  1028.1 29.0 %collective-permute-start.47 = (bf16[768,384]{1,0:T(8,128)(2,1)S(1)}, bf16[768,384]{1,0:T(8,128)(2,1)S(1)}, u32[]{:S(2)}, u32[]{:S(2)}) collective-permute-start(bf16[768,384]{1,0:T(8,128)(2,1)S(1)} %fusion.18), channel_id=1, source_target_pairs={{0,8},{16,24},{1,9},{17,25},{2,10},{18,26},{3,11},{19,27},{4,12},{... | collective-permute-start | bytes 1769480 | tf_op jit(solution)/shard_map/ppermute | solution.py:774
  1033.0 24.1 %collective-permute-start.55 = (bf16[768,384]{1,0:T(8,128)(2,1)S(1)}, bf16[768,384]{1,0:T(8,128)(2,1)S(1)}, u32[]{:S(2)}, u32[]{:S(2)}) collective-permute-start(bf16[768,384]{1,0:T(8,128)(2,1)S(1)} %fusion.14), channel_id=1, source_target_pairs={{8,0},{24,16},{9,1},{25,17},{10,2},{26,18},{11,3},{27,19},{12,4},{... | collective-permute-start | bytes 1769480 | tf_op jit(solution)/shard_map/ppermute | solution.py:774
  1047.0 25.6 %collective-permute-start.34 = (bf16[384,384]{1,0:T(8,128)(2,1)S(1)}, bf16[384,384]{1,0:T(8,128)(2,1)S(1)}, u32[]{:S(2)}, u32[]{:S(2)}) collective-permute-start(bf16[384,384]{1,0:T(8,128)(2,1)S(1)} %fusion.32), channel_id=1, source_target_pairs={{0,8},{16,24},{1,9},{17,25},{2,10},{18,26},{3,11},{19,27},{4,12},{... | collective-permute-start | bytes 884744 | tf_op jit(solution)/shard_map/ppermute | solution.py:774
  (71 other events, 1185.6 us)

commit v3 on v2

v3 whole, which is shorter than its diff:
```python
from functools import partial
import math

import jax
import jax.numpy as jnp
from jax import lax
from jax.experimental import pallas as pl
from jax.experimental.pallas import tpu as pltpu
from jax.sharding import PartitionSpec as P

HEAD = 64
PAIR = 2 * HEAD
QB = 128
KB = 512
EPS_NORM = 1e-05
EPS_PROJ = 1e-06
NEG_FILL = -1e30
PARAMS = pltpu.CompilerParams(vmem_limit_bytes=60 * 1024 * 1024)
COST = pl.CostEstimate(flops=1, bytes_accessed=1, transcendentals=0)
BF = jnp.bfloat16
F32 = jnp.float32

NT = (((1,), (1,)), ((), ()))
TN = (((0,), (0,)), ((), ()))


def dot(a, b):
    return jnp.dot(a, b, preferred_element_type=F32)


def dot_nt(a, b):
    return lax.dot_general(a, b, NT, preferred_element_type=F32)


def dot_tn(a, b):
    return lax.dot_general(a, b, TN, preferred_element_type=F32)


def pack_small(b_qv, b_out, gains, shifts, b_up, b_down):
    return jnp.concatenate(
        [b_up, b_qv, b_out, gains[0], gains[1], shifts[0], shifts[1], b_down]
    )


def small_spec(layer, width):
    return pl.BlockSpec((1, 1, width), lambda *_: (layer, 0, 0))


def attention_plan(starts, real_flags):
    length = real_flags.shape[0]
    places = jnp.arange(length, dtype=jnp.int32)
    segment = jnp.sum((starts[None, :] <= places[:, None]).astype(jnp.int32), axis=1)
    key_code = jnp.where(real_flags == 1, segment, -1).astype(F32)
    key_code = jnp.broadcast_to(key_code[:, None], (length, PAIR))
    query_code = segment.astype(F32).reshape(length // QB, QB)
    first = jnp.arange(length // QB, dtype=jnp.int32) * QB
    low = jnp.max(jnp.where(starts[None, :] <= first[:, None], starts[None, :], 0), axis=1)
    high = jnp.min(
        jnp.where(starts[None, :] > first[:, None] + (QB - 1), starts[None, :], length), axis=1
    )
    begin = (low // QB) * QB
    count = (high - begin + KB - 1) // KB
    begin = jnp.minimum(begin, length - KB * count)
    return (begin, count, key_code, query_code)


def pair_mask(rows):
    return lax.broadcasted_iota(jnp.int32, (rows, PAIR), 1) < HEAD


def stacked_heads(block):
    first = pair_mask(block.shape[0])
    zero = jnp.zeros_like(block)
    return jnp.concatenate([jnp.where(first, block, zero), jnp.where(first, zero, block)], axis=0)


def block_bias(key_code, query_code, key_at, query_at):
    keys = lax.broadcasted_iota(jnp.int32, (KB, QB), 0) + (key_at - query_at)
    same = keys == lax.broadcasted_iota(jnp.int32, (KB, QB), 1)
    bias = jnp.where((key_code == query_code) | same, 0.0, NEG_FILL)
    return jnp.concatenate([bias, bias], axis=1)


def top_rows(values, op):
    folded = values.reshape(values.shape[0] // 8, 8, values.shape[1])
    return op(folded, axis=0)


def unstack_heads(flat):
    rows = lax.broadcasted_iota(jnp.int32, (PAIR, QB), 0)
    return jnp.where(rows < HEAD, flat[:PAIR, :QB], flat[:PAIR, QB:]).T


def attend_forward(
    begin_ref, count_ref, qkv_ref, key_code_ref, query_code_ref, out_ref, logsum_ref,
    value_scr, query_scr, total_scr,
):
    length = qkv_ref.shape[1]
    pairs = qkv_ref.shape[2] // PAIR
    every = range(pairs)
    cols = [slice(p * PAIR, (p + 1) * PAIR) for p in every]
    for p in every:
        value_scr[p, :PAIR, :] = qkv_ref[2, :, cols[p]].T
        value_scr[p, PAIR:, :] = jnp.ones((value_scr.shape[1] - PAIR, length), BF)

    def one_query_block(i, _):
        query_at = pl.multiple_of(i * QB, QB)
        begin, count = begin_ref[i], count_ref[i]
        query_code = query_code_ref[pl.ds(i, 1), :]
        for p in every:
            query_scr[p] = stacked_heads(qkv_ref[0, pl.ds(query_at, QB), cols[p]])
        total_scr[...] = jnp.zeros_like(total_scr)

        def one_key_block(j, tops):
            key_at = pl.multiple_of(begin + j * KB, QB)
            rows = pl.ds(key_at, KB)
            bias = block_bias(key_code_ref[rows, :], query_code, key_at, query_at)
            scores = [dot_nt(qkv_ref[1, rows, cols[p]], query_scr[p]) + bias for p in every]
            fresh = [
                jnp.maximum(tops[p], jnp.max(scores[p], axis=0, keepdims=True)) for p in every
            ]
            probs = [jnp.exp(scores[p] - fresh[p]).astype(BF) for p in every]
            for p in every:
                total_scr[p] = total_scr[p] * jnp.exp(tops[p] - fresh[p]) + dot(
                    value_scr[p, :, rows], probs[p]
                )
            return tuple(fresh)

        tops = lax.fori_loop(
            0, count, one_key_block, tuple(jnp.full((1, 2 * QB), 2 * NEG_FILL, F32) for _ in every)
        )
        for p in every:
            weight = total_scr[p, PAIR : PAIR + 1, :]
            logsum_ref[pl.ds(p * (length // QB) + i, 1), :] = tops[p] + jnp.log(weight)
            out_ref[pl.ds(query_at, QB), cols[p]] = unstack_heads(
                total_scr[p, :PAIR, :] * (1.0 / weight)
            ).astype(BF)
        return 0

    lax.fori_loop(0, length // QB, one_query_block, 0)


def attend_backward(
    begin_ref, count_ref, qkv, key_code_ref, query_code_ref, context, logsum_ref, grad, sums_ref,
    key_scr, query_scr, given_scr, down_scr, grad_key_scr, grad_value_scr,
):
    length = qkv.shape[1]
    pairs = qkv.shape[2] // PAIR
    every = range(pairs)
    blocks = length // QB
    cols = [slice(p * PAIR, (p + 1) * PAIR) for p in every]
    for p in every:
        key_scr[p] = qkv[1, :, cols[p]].T
    grad_key_scr[...] = jnp.zeros_like(grad_key_scr)
    grad_value_scr[...] = jnp.zeros_like(grad_value_scr)
    sums_ref[...] = jnp.zeros_like(sums_ref)

    def one_query_block(i, _):
        query_at = pl.multiple_of(i * QB, QB)
        queries = pl.ds(query_at, QB)
        begin, count = begin_ref[i], count_ref[i]
        query_code = query_code_ref[pl.ds(i, 1), :]
        inner, logsum = [], []
        for p in every:
            query_scr[p] = stacked_heads(qkv[0, queries, cols[p]])
            given = grad[queries, cols[p]]
            given_scr[p] = stacked_heads(given)
            both = (given.astype(F32) * context[queries, cols[p]].astype(F32)).T
            inner.append(
                jnp.concatenate(
                    [
                        jnp.sum(both[:HEAD], axis=0, keepdims=True),
                        jnp.sum(both[HEAD:], axis=0, keepdims=True),
                    ],
                    axis=1,
                )
            )
            logsum.append(logsum_ref[pl.ds(p * blocks + i, 1), :])
        down_scr[...] = jnp.zeros_like(down_scr)

        def one_key_block(j, _):
            key_at = pl.multiple_of(begin + j * KB, QB)
            rows = pl.ds(key_at, KB)
            bias = block_bias(key_code_ref[rows, :], query_code, key_at, query_at)
            parts = [dot_nt(qkv[1, rows, cols[p]], query_scr[p]) + bias for p in every]
            grads = [dot_nt(qkv[2, rows, cols[p]], given_scr[p]) - inner[p] for p in every]
            probs = [jnp.exp(parts[p] - logsum[p]) for p in every]
            scores = [(probs[p] * grads[p]).astype(BF) for p in every]
            probs = [probs[p].astype(BF) for p in every]
            for p in every:
                grad_value_scr[rows, cols[p]] += dot(probs[p], given_scr[p])
            for p in every:
                grad_key_scr[rows, cols[p]] += dot(scores[p], query_scr[p])
            for p in every:
                down_scr[p] += dot(key_scr[p, :, rows], scores[p])
            return 0

        lax.fori_loop(0, count, one_key_block, 0)
        for p in every:
            grad_query = (unstack_heads(down_scr[p]) * (HEAD**-0.5)).astype(BF)
            qkv[0, queries, cols[p]] = grad_query
            sums_ref[0:1, cols[p]] += jnp.sum(grad_query.astype(F32), axis=0, keepdims=True)
        return 0

    lax.fori_loop(0, blocks, one_query_block, 0)
    qkv[1] = grad_key_scr[...].astype(BF)
    grad_value = grad_value_scr[...].astype(BF)
    qkv[2] = grad_value
    sums_ref[1:2, :] = jnp.sum(grad_value.astype(F32), axis=0, keepdims=True)


ANY = pl.BlockSpec(memory_space=pl.ANY)
ROWS = 256


class Held:
    def __init__(self, sel_ref, layer, pairs, held, sems, first=None):
        self.own = sel_ref[0] == layer
        self.items = list(zip(pairs, held, range(len(held))))
        self.sems = sems
        self.first = pl.program_id(0) == 0 if first is None else first

    def start(self):
        for pair, held, n in self.items:
            for wanted, source in zip((self.own, jnp.logical_not(self.own)), pair):

                @pl.when(self.first & wanted)
                def _():
                    pltpu.make_async_copy(source, held, self.sems.at[n]).start()

    def wait(self, n):
        pair, held, _ = self.items[n]

        @pl.when(self.first)
        def _():
            pltpu.make_async_copy(pair[0], held, self.sems.at[n]).wait()


def held_shapes(*weights):
    return [pltpu.VMEM(own.shape, own.dtype) for own, _ in weights]


def normalized(values):
    centred = values - jnp.mean(values, axis=-1, keepdims=True)
    inverse = lax.rsqrt(jnp.mean(centred * centred, axis=-1, keepdims=True) + EPS_NORM)
    return (centred * inverse, inverse)


def normalized_pull(grad_hat, hat, inverse):
    return inverse * (
        grad_hat
        - jnp.mean(grad_hat, axis=-1, keepdims=True)
        - hat * jnp.mean(grad_hat * hat, axis=-1, keepdims=True)
    )


ERF = (0.254829592, -0.284496736, 1.421413741, -1.453152027, 1.061405429)
ERF_SLOPE = 0.3275911


def gelu_parts(x):
    t = pl.reciprocal(1.0 + (ERF_SLOPE * math.sqrt(0.5)) * jnp.abs(x), approx=True)
    bell = jnp.exp(-0.5 * (x * x))
    tail = 0.5 * ERF[4]
    for term in ERF[3::-1]:
        tail = tail * t + 0.5 * term
    tail = tail * t * bell
    below = jnp.where(x >= 0, 1.0 - tail, tail)
    return (x * below, below + x * bell * (1.0 / math.sqrt(2.0 * math.pi)))


FB = 1024


def small_slices(width, ff_width):
    names = ("b_q", "b_v", "b_out", "gain1", "gain2", "shift1", "shift2", "b_down")
    at = {"b_up": slice(0, ff_width)}
    for n, name in enumerate(names):
        at[name] = slice(ff_width + n * width, ff_width + (n + 1) * width)
    return at


def refine_back_kernel(
    layer, sel_ref, grad_ref, hidden_ref, out_ref, scale1_ref, scale2_ref, slope_ref,
    out_own_ref, out_other_ref, up_own_ref, up_other_ref, down_own_ref, down_other_ref, small_ref,
    grad_low_ref, grad_raised_ref, grad_attn_ref, grad_context_ref, sums_ref, up_sums_ref,
    w_out, w_up, w_down, sems,
):
    pairs = [(out_own_ref, out_other_ref), (up_own_ref, up_other_ref), (down_own_ref, down_other_ref)]
    weights = Held(sel_ref, layer, pairs, [w_out, w_up, w_down], sems)
    weights.start()
    rows, width = grad_ref.shape
    ff_width = slope_ref.shape[1]
    at = small_slices(width, ff_width)

    @pl.when(pl.program_id(0) == 0)
    def _():
        sums_ref[...] = jnp.zeros_like(sums_ref)
        up_sums_ref[...] = jnp.zeros_like(up_sums_ref)

    def vector(name):
        return small_ref[0, :, at[name]]

    def add(row, values):
        sums_ref[row : row + 1, :] += jnp.sum(values, axis=0, keepdims=True)

    grad = grad_ref[...].astype(F32)
    hat = (out_ref[...].astype(F32) - vector("shift2")) * (1.0 / vector("gain2"))
    joined = normalized_pull(grad * vector("gain2"), hat, scale2_ref[:, :1])
    low = joined.astype(BF)
    grad_low_ref[...] = low
    add(2, grad * hat)
    add(4, grad)
    add(5, low.astype(F32))
    weights.wait(2)
    weights.wait(1)
    total = joined
    parts = [slice(f, f + FB) for f in range(0, ff_width, FB)]
    active = dot_nt(low, w_down[parts[0], :])
    for n, part in enumerate(parts):
        following = dot_nt(low, w_down[parts[n + 1], :]) if n + 1 < len(parts) else None
        raised = active * slope_ref[:, part].astype(F32)
        up_sums_ref[:, part] += jnp.sum(raised, axis=0, keepdims=True)
        raised = raised.astype(BF)
        grad_raised_ref[:, part] = raised
        total += dot_nt(raised, w_up[:, part])
        active = following
    hat = (hidden_ref[...].astype(F32) - vector("shift1")) * (1.0 / vector("gain1"))
    summed = normalized_pull(total * vector("gain1"), hat, scale1_ref[:, :1])
    attn = summed.astype(BF)
    grad_attn_ref[...] = attn
    weights.wait(0)
    grad_context_ref[...] = dot_nt(attn, w_out[...]).astype(BF)
    add(1, total * hat)
    add(3, total)
    add(0, attn.astype(F32))


def refine_back(sel, grad, kept, weights, layer):
    w_out, w_up, w_down, small = weights
    hidden, out, scale1, scale2, slope = kept
    length, width = grad.shape
    ff_width = w_up[0].shape[1]
    rows = pl.BlockSpec((ROWS, width), lambda n, _: (n, 0))
    lanes = pl.BlockSpec((ROWS, 128), lambda n, _: (n, 0))
    part = pl.BlockSpec((ROWS, ff_width), lambda n, _: (n, 0))
    row_shape = jax.ShapeDtypeStruct((length, width), BF)
    return pl.pallas_call(
        partial(refine_back_kernel, layer),
        name="refine_back",
        grid_spec=pltpu.PrefetchScalarGridSpec(
            num_scalar_prefetch=1,
            grid=(length // ROWS,),
            in_specs=[rows, rows, rows, lanes, lanes, part]
            + [ANY] * 6
            + [small_spec(layer, small.shape[2])],
            out_specs=[
                rows, part, rows, rows,
                pl.BlockSpec((6, width), lambda n, _: (0, 0)),
                pl.BlockSpec((1, ff_width), lambda n, _: (0, 0)),
            ],
            scratch_shapes=[
                *held_shapes(w_out, w_up, w_down),
                pltpu.SemaphoreType.DMA((3,)),
            ],
        ),
        out_shape=[
            row_shape,
            jax.ShapeDtypeStruct((length, ff_width), BF),
            row_shape,
            row_shape,
            jax.ShapeDtypeStruct((6, width), F32),
            jax.ShapeDtypeStruct((1, ff_width), F32),
        ],
        compiler_params=PARAMS,
        cost_estimate=COST,
    )(sel, grad, hidden, out, scale1, scale2, slope, *w_out, *w_up, *w_down, small)


def head_kernel(rows_ref, proj_ref, given_ref, embedded_ref, grad_proj_ref, grad_rows_ref):
    factor = math.sqrt(proj_ref.shape[0])
    columns = dot_nt(proj_ref[...], rows_ref[...])
    given = given_ref[...].astype(F32)
    inverse = lax.rsqrt(jnp.sum(columns * columns, axis=0, keepdims=True) + EPS_PROJ)
    cross = jnp.sum(columns * given, axis=0, keepdims=True)
    embedded_ref[...] = (factor * columns * inverse).astype(BF)
    grad = (factor * (given * inverse - columns * (cross * inverse * inverse * inverse))).astype(BF)
    grad_proj_ref[...] = dot(grad, rows_ref[...]).T.astype(BF)
    grad_rows_ref[...] = dot_tn(grad, proj_ref[...]).astype(BF)


def head(rows, proj, given):
    length, width = rows.shape
    cols = proj.shape[0]
    return pl.pallas_call(
        head_kernel,
        name="head",
        out_shape=[
            jax.ShapeDtypeStruct((cols, length), BF),
            jax.ShapeDtypeStruct((width, cols), BF),
            jax.ShapeDtypeStruct((length, width), BF),
        ],
        compiler_params=PARAMS,
        cost_estimate=COST,
    )(rows, proj, given)


HALF = 384
SHARDS = 8


def feed_grads_kernel(
    sel_ref, hidden_ref, raised_late_ref, raised_ref, active_ref, low_late_ref, low_ref, out_ref,
    hidden_scr, low_scr, raised_scr,
):
    step = pl.program_id(0)
    blocks = raised_ref.shape[1] // HALF
    share = hidden_ref.shape[1] // SHARDS
    late = sel_ref[1] == 1

    @pl.when(step == 0)
    def _():
        hidden_scr[...] = hidden_ref[...].T
        low_scr[...] = jnp.where(late, low_late_ref[...], low_ref[...]).T
        raised_scr[...] = jnp.where(late, raised_late_ref[...], raised_ref[...])

    @pl.when(step < 4)
    def _():
        at = pl.multiple_of(step * (2 * share), 2 * share)
        part = dot(hidden_scr[pl.ds(at, 2 * share), :], raised_scr[...]).astype(BF)
        for m in range(2):
            for n in range(blocks):
                out_ref[m, n * share : (n + 1) * share, :] = part[
                    m * share : (m + 1) * share, n * HALF : (n + 1) * HALF
                ]

    @pl.when(step >= 4)
    def _():
        rows = out_ref.shape[1]
        for m in range(2):
            part = dot(low_scr[...], active_ref[:, m * rows : (m + 1) * rows])
            out_ref[m] = part.T.astype(BF)


def feed_grads(sel, hidden, raised_late, raised, active, low_late, low):
    length, width = hidden.shape
    ff_width = active.shape[1]
    half_ff = ff_width // 2

    def late_spec(shape, wanted):
        return pl.BlockSpec(shape, lambda n, sel: (0, jnp.where(sel[1] == wanted, sel[2], 0)))

    return pl.pallas_call(
        feed_grads_kernel,
        name="feed_grads",
        grid_spec=pltpu.PrefetchScalarGridSpec(
            num_scalar_prefetch=1,
            grid=(8,),
            in_specs=[
                pl.BlockSpec((length, width), lambda n, _: (0, 0)),
                late_spec((length, half_ff), 1),
                late_spec((length, half_ff), 0),
                pl.BlockSpec((length, ff_width // 4), lambda n, _: (0, jnp.maximum(n - 4, 0))),
                late_spec((length, width // 2), 1),
                late_spec((length, width // 2), 0),
            ],
            out_specs=pl.BlockSpec(
                (2, ff_width // SHARDS, HALF), lambda n, _: (lax.rem(n, 4), n // 4, 0)
            ),
            scratch_shapes=[
                pltpu.VMEM((width, length), BF),
                pltpu.VMEM((width // 2, length), BF),
                pltpu.VMEM((length, half_ff), BF),
            ],
        ),
        out_shape=jax.ShapeDtypeStruct((SHARDS, 2 * (ff_width // SHARDS), HALF), BF),
        compiler_params=PARAMS,
        cost_estimate=COST,
    )(sel, hidden, raised_late, raised, active, low_late, low)


def attend_grads_kernel(
    sel_ref, context_ref, x_ref, attn_late_ref, attn_ref, mixed_late_ref, mixed_ref, out_ref, turned
):
    step = pl.program_id(0)
    late = sel_ref[1] == 1

    def store(cols):
        out_ref[...] = dot(turned[...], cols).astype(BF).reshape(out_ref.shape)

    @pl.when(step == 0)
    def _():
        turned[...] = context_ref[...].T
        store(jnp.where(late, attn_late_ref[...], attn_ref[...]))

    @pl.when(step == 1)
    def _():
        turned[...] = x_ref[...].T

    @pl.when(step > 0)
    def _():
        store(jnp.where(late, mixed_late_ref[0], mixed_ref[0]))


def attend_grads(sel, context, x, attn_late, attn, mixed_late, mixed):
    length, width = x.shape

    def late_spec(wanted):
        return pl.BlockSpec(
            (length, HALF), lambda n, sel: (0, jnp.where(sel[1] == wanted, sel[2], 0))
        )

    def mixed_spec(wanted):
        def at(n, sel):
            return (
                jnp.where(sel[1] == wanted, jnp.maximum(n - 1, 0), 0),
                0,
                jnp.where(sel[1] == wanted, sel[2], 0),
            )

        return pl.BlockSpec((1, length, HALF), at)

    whole = pl.BlockSpec((length, width), lambda n, _: (0, 0))
    share = width // SHARDS
    return pl.pallas_call(
        attend_grads_kernel,
        name="attend_grads",
        grid_spec=pltpu.PrefetchScalarGridSpec(
            num_scalar_prefetch=1,
            grid=(4,),
            in_specs=[whole, whole, late_spec(1), late_spec(0), mixed_spec(1), mixed_spec(0)],
            out_specs=pl.BlockSpec((SHARDS, share, HALF), lambda n, _: (0, n, 0)),
            scratch_shapes=[pltpu.VMEM((width, length), BF)],
        ),
        out_shape=jax.ShapeDtypeStruct((SHARDS, 4 * share, HALF), BF),
        compiler_params=PARAMS,
        cost_estimate=COST,
    )(sel, context, x, attn_late, attn, mixed_late, mixed)


def forward_kernel(
    layer, begin_ref, count_ref, sel_ref, x_hbm, key_code_ref, query_code_ref,
    mix_own_ref, mix_other_ref, out_own_ref, out_other_ref,
    up_own_ref, up_other_ref, down_own_ref, down_other_ref, small_ref,
    qkv_hbm, context_hbm, logsum_ref, out_hbm, hidden_hbm, scale1_ref, scale2_ref,
    active_hbm, slope_hbm,
    w_mix, w_out, w_up, w_down, x, qkv, context, hidden_rows, out_rows, active_rows, slope_rows,
    value_scr, query_scr, total_scr, weight_sems, in_sems, qkv_sems, row_sems, context_sem,
):
    pairs = [
        (mix_own_ref, mix_other_ref), (out_own_ref, out_other_ref),
        (up_own_ref, up_other_ref), (down_own_ref, down_other_ref),
    ]
    length, width = x.shape
    ff_width = w_up.shape[1]
    blocks = length // ROWS
    at = small_slices(width, ff_width)

    def vector(name):
        return small_ref[0, :, at[name]]

    def rows_of(n):
        return pl.ds(pl.multiple_of(n * ROWS, ROWS), ROWS)

    def x_copy(n):
        return pltpu.make_async_copy(x_hbm.at[rows_of(n)], x.at[rows_of(n)], in_sems.at[n])

    def qkv_copy(n):
        return pltpu.make_async_copy(
            qkv.at[:, rows_of(n)], qkv_hbm.at[:, rows_of(n)], qkv_sems.at[n]
        )

    saved = [
        (hidden_rows, hidden_hbm), (out_rows, out_hbm),
        (active_rows, active_hbm), (slope_rows, slope_hbm),
    ]

    def row_copies(n):
        return [
            pltpu.make_async_copy(rows.at[rows_of(n)], whole.at[rows_of(n)], row_sems.at[k, n])
            for k, (rows, whole) in enumerate(saved)
        ]

    weights = Held(sel_ref, layer, pairs, [w_mix, w_out, w_up, w_down], weight_sems, True)
    for n in range(blocks):
        x_copy(n).start()
    weights.start()
    weights.wait(0)

    def mix_rows(n, _):
        x_copy(n).wait()
        rows = rows_of(n)
        part = dot(x[rows, :], w_mix[...])
        qkv[0, rows, :] = ((part[:, :width] + vector("b_q")) * HEAD**-0.5).astype(BF)
        qkv[1, rows, :] = part[:, width : 2 * width].astype(BF)
        qkv[2, rows, :] = (part[:, 2 * width :] + vector("b_v")).astype(BF)
        qkv_copy(n).start()
        return 0

    lax.fori_loop(0, blocks, mix_rows, 0)
    attend_forward(
        begin_ref, count_ref, qkv, key_code_ref, query_code_ref, context, logsum_ref,
        value_scr, query_scr, total_scr,
    )
    context_copy = pltpu.make_async_copy(context, context_hbm, context_sem)
    context_copy.start()
    for n in (1, 2, 3):
        weights.wait(n)

    def refine_rows(n, _):
        rows = rows_of(n)
        summed = x[rows, :].astype(F32) + dot(context[rows, :], w_out[...]) + vector("b_out")
        hat, inverse = normalized(summed)
        hidden = hat * vector("gain1") + vector("shift1")
        scale1_ref[rows, :] = jnp.broadcast_to(inverse, (ROWS, 128))
        hidden_low = hidden.astype(BF)
        hidden_rows[rows, :] = hidden_low
        total = hidden + vector("b_down")
        parts = [slice(f, f + FB) for f in range(0, ff_width, FB)]
        raised = dot(hidden_low, w_up[:, parts[0]])
        for m, part in enumerate(parts):
            following = dot(hidden_low, w_up[:, parts[m + 1]]) if m + 1 < len(parts) else None
            active, slope = gelu_parts(raised + small_ref[0, :, part])
            active = active.astype(BF)
            active_rows[rows, part] = active
            slope_rows[rows, part] = slope.astype(BF)
            total += dot(active, w_down[part, :])
            raised = following
        hat, inverse = normalized(total)
        scale2_ref[rows, :] = jnp.broadcast_to(inverse, (ROWS, 128))
        out_rows[rows, :] = (hat * vector("gain2") + vector("shift2")).astype(BF)
        for copy in row_copies(n):
            copy.start()
        return 0

    lax.fori_loop(0, blocks, refine_rows, 0)
    context_copy.wait()
    for n in range(blocks):
        qkv_copy(n).wait()
        for copy in row_copies(n):
            copy.wait()


def layer_forward(sel, x, weights, layer, plan):
    w_qkv, w_out, w_up, w_down, small = weights
    begin, count, key_code, query_code = plan
    length, width = x.shape
    ff_width = w_up[0].shape[1]
    pairs = width // PAIR
    blocks = length // ROWS

    def whole(shape):
        return pl.BlockSpec(shape, lambda *_: (0,) * len(shape))

    row = jax.ShapeDtypeStruct((length, width), BF)
    lanes = jax.ShapeDtypeStruct((length, 128), F32)
    wide = jax.ShapeDtypeStruct((length, ff_width), BF)
    logsum_shape = (pairs * (length // QB), 2 * QB)
    qkv, context, logsum, out, hidden, scale1, scale2, active, slope = pl.pallas_call(
        partial(forward_kernel, layer),
        name="layer_forward",
        grid_spec=pltpu.PrefetchScalarGridSpec(
            num_scalar_prefetch=3,
            grid=(1,),
            in_specs=[ANY, whole(key_code.shape), whole(query_code.shape)]
            + [ANY] * 8
            + [small_spec(layer, small.shape[2])],
            out_specs=[
                ANY, ANY, whole(logsum_shape), ANY, ANY,
                whole((length, 128)), whole((length, 128)), ANY, ANY,
            ],
            scratch_shapes=[
                *held_shapes(w_qkv, w_out, w_up, w_down),
                pltpu.VMEM((length, width), BF),
                pltpu.VMEM((3, length, width), BF),
                pltpu.VMEM((length, width), BF),
                pltpu.VMEM((length, width), BF),
                pltpu.VMEM((length, width), BF),
                pltpu.VMEM((length, ff_width), BF),
                pltpu.VMEM((length, ff_width), BF),
                pltpu.VMEM((pairs, PAIR + 16, length), BF),
                pltpu.VMEM((pairs, 2 * QB, PAIR), BF),
                pltpu.VMEM((pairs, PAIR + 16, 2 * QB), F32),
                pltpu.SemaphoreType.DMA((4,)),
                pltpu.SemaphoreType.DMA((blocks,)),
                pltpu.SemaphoreType.DMA((blocks,)),
                pltpu.SemaphoreType.DMA((4, blocks)),
                pltpu.SemaphoreType.DMA,
            ],
        ),
        out_shape=[
            jax.ShapeDtypeStruct((3, length, width), BF), row,
            jax.ShapeDtypeStruct(logsum_shape, F32), row, row, lanes, lanes, wide, wide,
        ],
        compiler_params=PARAMS,
        cost_estimate=COST,
    )(begin, count, sel, x, key_code, query_code, *w_qkv, *w_out, *w_up, *w_down, small)
    return (out, (x, qkv, context, logsum, hidden, out, scale1, scale2, slope, active))


def feed_backward(sel, grad, kept, weights, layer):
    grad_low, grad_raised, grad_attn, grad_context, sums, up_sums = refine_back(
        sel, grad, kept[4:9], weights[1:], layer
    )
    return (grad_context, (grad_low, grad_raised, grad_attn), (sums, up_sums))


def mixed_backward_kernel(
    layer, begin_ref, count_ref, sel_ref, qkv_hbm, key_code_ref, query_code_ref, context_hbm,
    logsum_ref, grad_hbm, skip_hbm, mix_own_ref, mix_other_ref,
    mixed_hbm, grad_x_hbm, sums_ref,
    w_mix, qkv, context, grad, skip, key_scr, query_scr, given_scr, down_scr,
    grad_key_scr, grad_value_scr, weight_sems, in_sems, mixed_sems, row_sems,
):
    length, width = skip.shape
    blocks = length // ROWS
    weights = Held(sel_ref, layer, [(mix_own_ref, mix_other_ref)], [w_mix], weight_sems, True)
    arrays = [(qkv_hbm, qkv), (context_hbm, context), (grad_hbm, grad), (skip_hbm, skip)]
    loads = [
        pltpu.make_async_copy(whole, held, in_sems.at[n]) for n, (whole, held) in enumerate(arrays)
    ]
    for load in loads:
        load.start()
    weights.start()
    for load in loads:
        load.wait()
    attend_backward(
        begin_ref, count_ref, qkv, key_code_ref, query_code_ref, context, logsum_ref, grad,
        sums_ref, key_scr, query_scr, given_scr, down_scr, grad_key_scr, grad_value_scr,
    )
    store = pltpu.make_async_copy(qkv, mixed_hbm, mixed_sems.at[0])
    store.start()
    weights.wait(0)

    def rows_of(n):
        return pl.ds(pl.multiple_of(n * ROWS, ROWS), ROWS)

    def row_copy(n):
        return pltpu.make_async_copy(skip.at[rows_of(n)], grad_x_hbm.at[rows_of(n)], row_sems.at[n])

    def unmix_rows(n, _):
        rows = rows_of(n)
        total = skip[rows, :].astype(F32)
        for c in range(3):
            total += dot_nt(qkv[c, rows, :], w_mix[:, c * width : (c + 1) * width])
        skip[rows, :] = total.astype(BF)
        row_copy(n).start()
        return 0

    lax.fori_loop(0, blocks, unmix_rows, 0)
    store.wait()
    for n in range(blocks):
        row_copy(n).wait()


def mixed_backward(sel, grad_context, skip, kept, weights, layer, plan):
    _, qkv, context, logsum = kept[:4]
    begin, count, key_code, query_code = plan
    _, length, width = qkv.shape
    pairs = width // PAIR
    blocks = length // ROWS
    w_qkv = weights[0]

    def whole(shape):
        return pl.BlockSpec(shape, lambda *_: (0,) * len(shape))

    row = pltpu.VMEM((length, width), BF)
    return pl.pallas_call(
        partial(mixed_backward_kernel, layer),
        name="mixed_backward",
        grid_spec=pltpu.PrefetchScalarGridSpec(
            num_scalar_prefetch=3,
            grid=(1,),
            in_specs=[ANY, whole(key_code.shape), whole(query_code.shape), ANY, whole(logsum.shape)]
            + [ANY] * 4,
            out_specs=[ANY, ANY, whole((2, width))],
            scratch_shapes=[
                *held_shapes(w_qkv),
                pltpu.VMEM((3, length, width), BF),
                row, row, row,
                pltpu.VMEM((pairs, PAIR, length), BF),
                pltpu.VMEM((pairs, 2 * QB, PAIR), BF),
                pltpu.VMEM((pairs, 2 * QB, PAIR), BF),
                pltpu.VMEM((pairs, PAIR, 2 * QB), F32),
                pltpu.VMEM((length, width), F32),
                pltpu.VMEM((length, width), F32),
                pltpu.SemaphoreType.DMA((1,)),
                pltpu.SemaphoreType.DMA((4,)),
                pltpu.SemaphoreType.DMA((1,)),
                pltpu.SemaphoreType.DMA((blocks,)),
            ],
        ),
        out_shape=[
            jax.ShapeDtypeStruct((3, length, width), BF),
            jax.ShapeDtypeStruct((length, width), BF),
            jax.ShapeDtypeStruct((2, width), F32),
        ],
        compiler_params=PARAMS,
        cost_estimate=COST,
    )(begin, count, sel, qkv, key_code, query_code, context, logsum, grad_context, skip, *w_qkv)


def layer_backward(sel, grad, kept, weights, layer, plan):
    grad_context, grads, sums = feed_backward(sel, grad, kept, weights, layer)
    grad_mixed, grad_x, mix_sums = mixed_backward(
        sel, grad_context, grads[2], kept, weights, layer, plan
    )
    return (grad_x, grads + (grad_mixed,), sums + (mix_sums,))


def swap_cores(value):
    return send(value, ((0, 1), (1, 0), (2, 3), (3, 2)))


def send(value, routes):
    return lax.ppermute(value, "section", routes)


def pick_row(value, at, axis=0):
    return lax.dynamic_index_in_dim(value, at, axis, keepdims=False)


def plus(*values):
    return sum(value.astype(F32) for value in values).astype(BF)


class RowSum:
    def __init__(self, value, x_first):
        at = lax.axis_index("dp")
        self.z, self.x, self.x_first = at // 2, at % 2, x_first
        self.value = value.reshape(4, 2, *value.shape[1:])
        self.travelling = None
        self.steps = [self.cross, self.line, self.line, self.line]
        if not x_first:
            self.steps = self.steps[1:] + self.steps[:1]
        self.line_at = 0

    def cross(self):
        axis = 1 if self.x_first else 0
        other = pick_row(self.value, 1 - self.x, axis)
        arrived = lax.ppermute(other, "dp", [(n, n ^ 1) for n in range(8)])
        self.value = plus(pick_row(self.value, self.x, axis), arrived)

    def line(self):
        self.line_at += 1
        far = 4 - self.line_at
        right = pick_row(self.value, jnp.minimum(self.z + far, 3))
        left = pick_row(self.value, jnp.maximum(self.z - far, 0))
        if self.travelling is not None:
            right, left = plus(right, self.travelling[0]), plus(left, self.travelling[1])
        self.travelling = (
            lax.ppermute(right, "dp", [(n, n + 2) for n in range(6)]),
            lax.ppermute(left, "dp", [(n + 2, n) for n in range(6)]),
        )
        if self.line_at == 3:
            self.value = plus(pick_row(self.value, self.z), *self.travelling)

    def step(self):
        if self.steps:
            self.steps.pop(0)()

    def result(self):
        while self.steps:
            self.step()
        return self.value


class PlainSum:
    def __init__(self, value, blocks):
        shards = lax.axis_size("dp")
        parts, at = [], 0
        for rows in blocks:
            part = value[:, at : at + rows].reshape(shards, -1, value.shape[2])
            parts, at = parts + [part], at + rows
        whole = jnp.concatenate(parts, axis=1)
        self.value = lax.psum_scatter(whole, "dp", scatter_dimension=0, tiled=True)[0]
        self.travelling = None

    def step(self):
        pass

    def result(self):
        return self.value


def body(
    tokens_in, seg_starts, pad_mask, w_qkv, b_qv, w_attn_out, b_attn_out, ln_gain, ln_bias,
    w_up, b_up, w_down, b_down, w_proj, cotangent,
):
    section_at = lax.axis_index("section")
    core = section_at % 2
    is_late = section_at >= 2
    flip = core == 1
    quarter = tokens_in.shape[1]
    length, width = 4 * quarter, tokens_in.shape[2]
    ff_width = w_up.shape[2]
    proj_cols = w_proj.shape[1]
    shards = lax.axis_size("dp")
    share = width // shards

    def sel_for(half):
        return jnp.stack([core, section_at // 2, half]).astype(jnp.int32)

    sel_mine, sel_theirs = sel_for(core), sel_for(1 - core)

    own = pick_row(tokens_in, core)
    other = pick_row(tokens_in, 1 - core)
    straight = send(own, [(2, 0), (3, 1)])
    crossed = send(other, [(2, 1), (3, 0)])
    near = swap_cores(other)
    small = pack_small(b_qv[0], b_attn_out[0], ln_gain[0], ln_bias[0], b_up[0], b_down[0])[None]
    small_other = swap_cores(small)
    small = jnp.stack([jnp.where(flip, small_other, small), jnp.where(flip, small, small_other)])
    weights = tuple((w[0], swap_cores(w[0])) for w in (w_qkv, w_attn_out, w_up, w_down)) + (small,)
    x = jnp.concatenate(
        [
            jnp.where(flip, near, own),
            jnp.where(flip, own, near),
            jnp.where(flip, crossed, straight),
            jnp.where(flip, straight, crossed),
        ],
        axis=0,
    )

    head_own = jnp.concatenate([w_proj.T, pick_row(cotangent, core).T], axis=1)
    head_other = jnp.concatenate([w_proj.T, pick_row(cotangent, 1 - core).T], axis=1)
    head_late = send(head_other, [(2, 3), (3, 2)])
    head_straight = send(head_own, [(0, 2), (1, 3)])
    head_crossed = send(head_other, [(0, 3), (1, 2)])
    head_cols = jnp.concatenate(
        [
            jnp.where(flip, head_crossed, head_straight),
            jnp.where(flip, head_straight, head_crossed),
            jnp.where(flip, head_late, head_own),
            jnp.where(flip, head_own, head_late),
        ],
        axis=0,
    )
    proj_rows, given_rows = head_cols[:, :width], head_cols[:, width:]
    plan = attention_plan(pick_row(seg_starts, core), pick_row(pad_mask, core))

    def both_forward(rows):
        middle, kept_even = layer_forward(sel_mine, rows, weights, 0, plan)
        last, kept_odd = layer_forward(sel_mine, middle, weights, 1, plan)
        return (last, kept_even, kept_odd)

    early, kept_even, kept_odd = both_forward(x)
    hopped = send(early, [(0, 2), (1, 3)])
    hopped, proj_rows, given_rows = lax.optimization_barrier((hopped, proj_rows, given_rows))

    def late_turn(rows, *_):
        last, kept_even, kept_odd = both_forward(rows)
        embedded, grad_proj, grad = head(last, proj_rows, given_rows)
        grad, grads_odd, sums_odd = layer_backward(sel_mine, grad, kept_odd, weights, 1, plan)
        grad, grads_even, sums_even = layer_backward(sel_mine, grad, kept_even, weights, 0, plan)
        return (
            kept_even, kept_odd, embedded, grad_proj, grad,
            grads_odd, sums_odd, grads_even, sums_even,
        )

    def early_turn(rows, kept_even, kept_odd):
        row, ff = jnp.zeros((length, width), BF), jnp.zeros((length, ff_width), BF)
        grads = (row, ff, row, jnp.zeros((3, length, width), BF))
        sums = (
            jnp.zeros((6, width), F32),
            jnp.zeros((1, ff_width), F32),
            jnp.zeros((2, width), F32),
        )
        return (
            kept_even, kept_odd, jnp.zeros((4 * proj_cols, length), BF),
            jnp.zeros((width, 4 * proj_cols), BF), row, grads, sums, grads, sums,
        )

    (
        kept_even, kept_odd, embedded, grad_proj, grad_mid,
        late_odd, late_sums_odd, late_even, late_sums_even,
    ) = lax.cond(is_late, late_turn, early_turn, hopped, kept_even, kept_odd)

    grad = send(grad_mid, [(2, 0), (3, 1)])
    embedded_cols = embedded.reshape(4, proj_cols, length)

    rows_of_one = width // SHARDS
    attend_blocks = (rows_of_one,) * 4
    feed_blocks = (rows_of_one,) * (ff_width // (2 * HALF)) + (ff_width // SHARDS,)

    def row_sum(value, blocks):
        return RowSum(value, True) if shards == SHARDS else PlainSum(value, blocks)

    def feed_sum(kept, late, now):
        args = (kept[4], late[1], now[1], kept[9], late[0], now[0])
        arrived = swap_cores(feed_grads(sel_theirs, *args))
        return row_sum(plus(feed_grads(sel_mine, *args), arrived), feed_blocks)

    def attend_parts(kept, late, now, mixed):
        args = (kept[2], kept[0], late[2], now[2], late[3], mixed)
        return (attend_grads(sel_theirs, *args), attend_grads(sel_mine, *args))

    def merged(late_sums, sums):
        return tuple(jnp.where(is_late, a, b) for a, b in zip(late_sums, sums))

    def tie(*values):
        return lax.optimization_barrier(values)

    grad_context, grads_odd, sums_odd = feed_backward(sel_mine, grad, kept_odd, weights, 1)
    feed_odd = feed_sum(kept_odd, late_odd, grads_odd)
    grad_context, feed_odd.value = tie(grad_context, feed_odd.value)
    feed_odd.step()
    mixed_odd, grad, mix_sums = mixed_backward(
        sel_mine, grad_context, grads_odd[2], kept_odd, weights, 1, plan
    )
    sums_odd = merged(late_sums_odd, sums_odd + (mix_sums,))
    theirs, mine = attend_parts(kept_odd, late_odd, grads_odd, mixed_odd)
    attend_odd = row_sum(plus(mine, swap_cores(theirs)), attend_blocks)
    grad, attend_odd.value, feed_odd.value = tie(grad, attend_odd.value, feed_odd.value)
    feed_odd.step()
    attend_odd.step()

    grad_context, grads_even, sums_even = feed_backward(sel_mine, grad, kept_even, weights, 0)
    args = (kept_even[4], late_even[1], grads_even[1], kept_even[9], late_even[0], grads_even[0])
    args, feed_odd.travelling, attend_odd.value = tie(
        args, feed_odd.travelling, attend_odd.value
    )
    feed_odd.step()
    attend_odd.step()
    theirs = feed_grads(sel_theirs, *args)
    arrived = swap_cores(theirs)
    args, theirs, feed_odd.travelling = tie(args, theirs, feed_odd.travelling)
    feed_odd.step()
    feed_even = row_sum(plus(feed_grads(sel_mine, *args), arrived), feed_blocks)
    grad_context, feed_even.value, feed_odd.value, attend_odd.travelling = tie(
        grad_context, feed_even.value, feed_odd.value, attend_odd.travelling
    )
    feed_even.step()
    attend_odd.step()
    mixed_even, grad, mix_sums = mixed_backward(
        sel_mine, grad_context, grads_even[2], kept_even, weights, 0, plan
    )
    sums_even = merged(late_sums_even, sums_even + (mix_sums,))
    args = (kept_even[2], kept_even[0], late_even[2], grads_even[2], late_even[3], mixed_even)
    args, attend_odd.travelling, feed_even.value = tie(
        args, attend_odd.travelling, feed_even.value
    )
    feed_even.step()
    attend_odd.step()
    theirs = attend_grads(sel_theirs, *args)
    arrived = swap_cores(theirs)
    args, theirs, feed_even.travelling = tie(args, theirs, feed_even.travelling)
    feed_even.step()
    mine = attend_grads(sel_mine, *args)

    def small_rows(sums):
        sums, up_sums, mix_sums = sums
        rows = [up_sums[0], mix_sums.reshape(-1)]
        rows += [sums[n] for n in range(6)]
        return jnp.concatenate([row.reshape(shards, -1) for row in rows], axis=1)

    extras = jnp.concatenate(
        [small_rows(sums_even), small_rows(sums_odd), grad_proj.reshape(shards, -1).astype(F32)],
        axis=1,
    )
    small_width = 12 * share
    lines = -(-extras.shape[1] // HALF)
    lines = -(-lines // 16) * 16
    extras = jnp.pad(extras, ((0, 0), (0, lines * HALF - extras.shape[1])))
    extras = extras.reshape(shards, lines, HALF).astype(BF)
    extras = plus(extras, swap_cores(extras))
    attend_even = plus(mine, arrived)
    if shards == SHARDS:
        tail = jnp.concatenate([attend_even, extras], axis=1)
        cut = tail.shape[1] // 32 * 16
        tails = [RowSum(tail[:, :cut], True), RowSum(tail[:, cut:], False)]
        for n in range(4):
            for part in tails:
                part.step()
            feed_even.step()
        feed_odd, attend_odd, feed_even = [
            part.result() for part in (feed_odd, attend_odd, feed_even)
        ]
        tail = jnp.concatenate([part.result() for part in tails], axis=0)
        attend_even, extras = tail[: 4 * share], tail[4 * share :]
    else:
        feed_odd, attend_odd, feed_even = [
            part.result() for part in (feed_odd, attend_odd, feed_even)
        ]
        attend_even = PlainSum(attend_even, attend_blocks).result()
        extras = lax.psum_scatter(extras, "dp", scatter_dimension=0, tiled=True)[0]

    routes_odd, routes_even = ((0, 1), (2, 3)), ((1, 0), (3, 2))

    def halves(even, odd):
        arrived = jnp.where(flip, send(odd, routes_odd), send(even, routes_even))
        mine = jnp.where(flip, odd, even)
        return (jnp.where(flip, arrived, mine), jnp.where(flip, mine, arrived))

    blocks = ff_width // (2 * HALF)
    feed_halves = halves(feed_even, feed_odd)
    attend_halves = halves(attend_even, attend_odd)

    def columns(pair, first, count):
        parts = [part[n * share : (n + 1) * share] for part in pair for n in range(first, first + count)]
        return jnp.concatenate(parts, axis=1).astype(F32)

    grad_w_up = columns(feed_halves, 0, blocks)[None]
    grad_w_down = jnp.concatenate([part[blocks * share :] for part in feed_halves], axis=1)
    grad_w_down = grad_w_down.astype(F32)[None]
    grad_w_out = columns(attend_halves, 0, 1)[None]
    grad_w_qkv = jnp.concatenate([columns(attend_halves, 1 + c, 1) for c in range(3)], axis=1)[None]

    extras = extras.reshape(-1).astype(F32)
    small_mine = jnp.where(flip, extras[small_width : 2 * small_width], extras[:small_width])
    at = ff_width // shards
    grad_b_up = small_mine[None, :at]
    grad_b_qv = small_mine[None, at : at + 2 * share]
    rows = small_mine[at + 2 * share :].reshape(6, share)
    grad_proj = extras[2 * small_width : 2 * small_width + share * 4 * proj_cols]
    grad_proj = grad_proj.reshape(share, 4 * proj_cols).astype(BF)
    grad_proj = jnp.where(is_late, grad_proj, send(grad_proj, [(2, 0), (3, 1)])).astype(F32)
    grad_w_proj = lax.dynamic_slice_in_dim(grad_proj, section_at * proj_cols, proj_cols, 1)

    straight_cols = send(pick_row(embedded_cols, core), [(2, 0), (3, 1)])
    crossed_cols = send(pick_row(embedded_cols, 1 - core), [(2, 1), (3, 0)])
    near_cols = swap_cores(pick_row(embedded_cols, 3 - core))
    own_cols = jnp.where(is_late, pick_row(embedded_cols, section_at), straight_cols)
    other_cols = jnp.where(is_late, near_cols, crossed_cols)
    embedded_out = jnp.stack(
        [jnp.where(flip, other_cols, own_cols).T, jnp.where(flip, own_cols, other_cols).T]
    )

    quarters = grad.reshape(4, quarter, width)
    straight_grad = send(pick_row(quarters, 2 + core), [(0, 2), (1, 3)])
    crossed_grad = send(pick_row(quarters, 3 - core), [(0, 3), (1, 2)])
    near_grad = swap_cores(pick_row(quarters, 1 - core))
    mine = jnp.where(is_late, straight_grad, pick_row(quarters, core))
    others = jnp.where(is_late, crossed_grad, near_grad)
    grad_in = jnp.stack(
        [jnp.where(flip, others, mine), jnp.where(flip, mine, others)]
    ).astype(F32)

    return (
        embedded_out,
        grad_in,
        grad_w_qkv,
        grad_b_qv,
        grad_w_out,
        rows[0][None],
        rows[1:3][None],
        rows[3:5][None],
        grad_w_up,
        grad_b_up,
        grad_w_down,
        rows[5][None],
        grad_w_proj,
    )


def solution(mesh):
    in_specs = (
        P("dp", "section", None),
        P("dp", None),
        P("dp", None),
        P("section", None, None),
        P("section", None),
        P("section", None, None),
        P("section", None),
        P("section", None, None),
        P("section", None, None),
        P("section", None, None),
        P("section", None),
        P("section", None, None),
        P("section", None),
        P(None, "section"),
        P("dp", None, "section"),
    )
    out_specs = (
        P("dp", None, "section"),
        P("dp", "section", None),
        P("section", "dp", None),
        P("section", "dp"),
        P("section", "dp", None),
        P("section", "dp"),
        P("section", None, "dp"),
        P("section", None, "dp"),
        P("section", "dp", None),
        P("section", "dp"),
        P("section", "dp", None),
        P("section", "dp"),
        P("dp", "section"),
    )
    return jax.shard_map(body, mesh=mesh, in_specs=in_specs, out_specs=out_specs, check_vma=False)
```

time: 1090 us -> 952 us (0.87)
  Pallas kernels: 657 us -> 590 us
  local copies, waits for them, and re-layouts: 68.5 us -> 34.1 us
  waiting for transfers between devices: 127 us -> 104 us
  starting transfers between devices: 156 us -> 135 us
  other arithmetic: 58.3 us -> 79.1 us
    pallas_call x20 -> x9, Pallas kernels: 454 us -> 395 us  [the longest x4 214 us: layer_forward(): pl.pallas_call(partial(forward_kernel, layer), name='layer_forward', grid...]
    ppermute x29, waiting for transfers between devices: 73.4 us -> 54.4 us  [send(): return lax.ppermute(value, 'section', routes)]
    ppermute x4 -> x5, starting transfers between devices: 24.6 us -> 7.22 us  [cross(): arrived = lax.ppermute(other, 'dp', [(n, n ^ 1) for n in range(8)])]
    convert_element_type x24 -> x28, other arithmetic: 33.3 us -> 49.4 us  [plus(): return sum((value.astype(F32) for value in values)).astype(BF)]
    select_n x8 -> x0, local copies, waits for them, and re-layouts: 15.1 us -> none  [the longest x2 3.83 us: head(): jnp.where(flip, straight, crossed)]
    another operation x16, local copies, waits for them, and re-layouts: 15.9 us -> 1.24 us  [small_rows(): return jnp.concatenate([row.reshape(shards, -1) for row in rows], axis=1)]
    ppermute x12 -> x15, waiting for transfers between devices: 32 us -> 18.4 us  [line(): lax.ppermute(left, 'dp', [(n + 2, n) for n in range(6)])]
    ppermute x4 -> x5, waiting for transfers between devices: 0.01 us -> 12.2 us  [cross(): arrived = lax.ppermute(other, 'dp', [(n, n ^ 1) for n in range(8)])]
  transfers between devices with their start and end apart: 57 -> 64, of which waited for: 15 -> 18; matrix products, arithmetic and copies ran while one was open for 8% -> 9% of each run, Pallas kernels for 18% -> 19%
where the time goes in v3:
time: 952 us; the launch traced here: 945 us
  Pallas kernels  590 us (62%)
  starting transfers between devices  135 us (14%)
  waiting for transfers between devices  104 us (11%)
  other arithmetic  79.1 us (8%)
  local copies, waits for them, and re-layouts  34.1 us (4%)
    pallas_call x4, Pallas kernels, layer_forward(): pl.pallas_call(partial(forward_kernel, layer), name='layer_forward', grid...  214 us
    pallas_call x4, Pallas kernels, mixed_backward(): pl.pallas_call(partial(mixed_backward_kernel, layer), name='mixed_backwar...  177 us
    pallas_call x4, Pallas kernels, refine_back(): pl.pallas_call(partial(refine_back_kernel, layer), name='refine_back', gr...  97.8 us
    pallas_call x4, Pallas kernels, feed_grads(): pl.pallas_call(feed_grads_kernel, name='feed_grads', grid_spec=pltpu.Pref...  62.2 us
    ppermute x29, waiting for transfers between devices, send(): return lax.ppermute(value, 'section', routes)  54.4 us
    convert_element_type x28, other arithmetic, plus(): return sum((value.astype(F32) for value in values)).astype(BF)  49.4 us
    ppermute x29, starting transfers between devices, send(): return lax.ppermute(value, 'section', routes)  43 us
    ppermute x15, starting transfers between devices, line(): lax.ppermute(left, 'dp', [(n + 2, n) for n in range(6)])  42.7 us
  transfers between devices with their start and end apart: 64, of which 18 were waited for; matrix products, arithmetic and copies ran while one was open for 9% of the time, Pallas kernels for 19%

profile of v3, /device:TPU:13, one launch (start us, length us, event | category | flops | bytes accessed | tf_op | source)
XLA Modules:
  0.0 944.8 jit_solution(13761296465568188215)
XLA Ops:
  18.0 7.6 collective-permute-done.2
  31.6 54.2 %layer_forward.8 = (bf16[3,1024,768]{2,1,0:T(8,128)(2,1)}, bf16[1024,768]{1,0:T(8,128)(2,1)}, f32[48,256]{1,0:T(8,128)}, bf16[1024,768]{1,0:T(8,128)(2,1)}, bf16...) custom-call(s32[8]{0:T(128)S(1)} %get-tuple-element.536.begin_ref, ...), custom_call_target="tpu_custom_call" | custom-call | flops 1 | bytes 1 | tf_op jit(solution)/shard_map/layer_forward/pallas_call | solution.py:659
  85.8 52.6 %layer_forward.9 = (bf16[3,1024,768]{2,1,0:T(8,128)(2,1)}, bf16[1024,768]{1,0:T(8,128)(2,1)}, f32[48,256]{1,0:T(8,128)}, bf16[1024,768]{1,0:T(8,128)(2,1)}, bf16...) custom-call(s32[8]{0:T(128)S(1)} %get-tuple-element.536.begin_ref, ...), custom_call_target="tpu_custom_call" | custom-call | flops 1 | bytes 1 | tf_op jit(solution)/shard_map/layer_forward/pallas_call | solution.py:659
  147.5 11.4 %collective-permute-done.9 = bf16[32,1792]{1,0:T(8,128)(2,1)} collective-permute-done((bf16[32,1792]{1,0:T(8,128)(2,1)}, bf16[32,1792]{1,0:T(8,128)(2,1)}, u32[]{:S(2)}, u32[]{:S(2)}) %collective-permute-start.9) | collective-permute-done | bytes 114720 | tf_op jit(solution)/shard_map/ppermute | solution.py:816
  158.9 12.6 %collective-permute-done.10 = bf16[32,1792]{1,0:T(8,128)(2,1)} collective-permute-done((bf16[32,1792]{1,0:T(8,128)(2,1)}, bf16[32,1792]{1,0:T(8,128)(2,1)}, u32[]{:S(2)}, u32[]{:S(2)}) %collective-permute-start.10) | collective-permute-done | bytes 114720 | tf_op jit(solution)/shard_map/ppermute | solution.py:816
  175.6 253.2 %conditional.1 = (bf16[1024,768]{1,0:T(8,128)(2,1)}, bf16[3,1024,768]{2,1,0:T(8,128)(2,1)}, bf16[1024,768]{1,0:T(8,128)(2,1)}, f32[48,256]{1,0:T(8,128)}, bf16[1...) conditional(s32[]{:T(128)} %convert_element_type.504, ...), branch_computations={%region_3.4_spmd, %region_4.5_spmd} | conditional | flops 7 | bytes 30417230 | solution.py:977
  175.6 54.6 %layer_forward.6 = (bf16[3,1024,768]{2,1,0:T(8,128)(2,1)}, bf16[1024,768]{1,0:T(8,128)(2,1)}, f32[48,256]{1,0:T(8,128)}, bf16[1024,768]{1,0:T(8,128)(2,1)}, bf16...) custom-call(s32[8]{0:T(128)S(1)} %get-tuple-element.185.begin_ref, ...), custom_call_target="tpu_custom_call" | custom-call | flops 1 | bytes 1 | tf_op jit(solution)/shard_map/cond/branch_1_fun/layer_forward/pallas_call | solution.py:659
  230.3 52.6 %layer_forward.7 = (bf16[3,1024,768]{2,1,0:T(8,128)(2,1)}, bf16[1024,768]{1,0:T(8,128)(2,1)}, f32[48,256]{1,0:T(8,128)S(1)}, bf16[1024,768]{1,0:T(8,128)(2,1)}, ...) custom-call(s32[8]{0:T(128)S(1)} %get-tuple-element.185.begin_ref, ...), custom_call_target="tpu_custom_call" | custom-call | flops 1 | bytes 1 | tf_op jit(solution)/shard_map/cond/branch_1_fun/layer_forward/pallas_call | solution.py:659
  287.1 24.6 %refine_back.6 = (bf16[1024,768]{1,0:T(8,128)(2,1)}, bf16[1024,3072]{1,0:T(8,128)(2,1)}, bf16[1024,768]{1,0:T(8,128)(2,1)}, bf16[1024,768]{1,0:T(8,128)(2,1)}, f32[6,768]{1,0:T(8,128)}, /*index=5*/f32[1,3072]{1,0:T(1,128)}) custom-call(s32[3]{0:T(128)S(1)} %get-tuple-element.187.sel_ref, bf16[1024,768]{1,0:T(8,128)(2,1)} %get-tuple-element.219.grad_ref, ...), custom_call_target="tpu_custom_call" | custom-call | flops 1 | bytes 1 | tf_op jit(solution)/shard_map/cond/branch_1_fun/refine_back/pallas_call | solution.py:348
  311.7 43.9 %mixed_backward.6 = (bf16[3,1024,768]{2,1,0:T(8,128)(2,1)}, bf16[1024,768]{1,0:T(8,128)(2,1)}, f32[2,768]{1,0:T(2,128)}) custom-call(s32[8]{0:T(128)S(1)} %get-tuple-element.185.begin_ref, s32[8]{0:T(128)S(1)} %get-tuple-element.186.count_ref, s32[3]{0:T(128)S(1)} %get-tuple-element.187.sel_ref, bf16[3,1024,768]{2,1,0:T(8,128)(2,1)} %get-tuple-element.648.qkv_hbm, ...), custom_call_target="tpu_custom_call" | custom-call | flops 1 | bytes 1 | tf_op jit(solution)/shard_map/cond/branch_1_fun/mixed_backward/pallas_call | solution.py:768
  355.6 24.5 %refine_back.7 = (bf16[1024,768]{1,0:T(8,128)(2,1)}, bf16[1024,3072]{1,0:T(8,128)(2,1)}, bf16[1024,768]{1,0:T(8,128)(2,1)}, bf16[1024,768]{1,0:T(8,128)(2,1)}, f32[6,768]{1,0:T(8,128)}, /*index=5*/f32[1,3072]{1,0:T(1,128)}) custom-call(s32[3]{0:T(128)S(1)} %get-tuple-element.187.sel_ref, bf16[1024,768]{1,0:T(8,128)(2,1)} %get-tuple-element.222.grad_ref, ...), custom_call_target="tpu_custom_call" | custom-call | flops 1 | bytes 1 | tf_op jit(solution)/shard_map/cond/branch_1_fun/refine_back/pallas_call | solution.py:348
  380.1 43.9 %mixed_backward.7 = (bf16[3,1024,768]{2,1,0:T(8,128)(2,1)}, bf16[1024,768]{1,0:T(8,128)(2,1)}, f32[2,768]{1,0:T(2,128)}) custom-call(s32[8]{0:T(128)S(1)} %get-tuple-element.185.begin_ref, s32[8]{0:T(128)S(1)} %get-tuple-element.186.count_ref, s32[3]{0:T(128)S(1)} %get-tuple-element.187.sel_ref, bf16[3,1024,768]{2,1,0:T(8,128)(2,1)} %get-tuple-element.639.qkv_hbm, ...), custom_call_target="tpu_custom_call" | custom-call | flops 1 | bytes 1 | tf_op jit(solution)/shard_map/cond/branch_1_fun/mixed_backward/pallas_call | solution.py:768
  432.0 15.8 %collective-permute-done.15.grad_ref = bf16[1024,768]{1,0:T(8,128)(2,1)} collective-permute-done((bf16[1024,768]{1,0:T(8,128)(2,1)}, bf16[1024,768]{1,0:T(8,128)(2,1)}, u32[]{:S(2)}, u32[]{:S(2)}) %collective-permute-start.15) | collective-permute-done | bytes 1572896 | tf_op jit(solution)/shard_map/ppermute | solution.py:816
  447.8 24.4 %refine_back.8 = (bf16[1024,768]{1,0:T(8,128)(2,1)}, bf16[1024,3072]{1,0:T(8,128)(2,1)}, bf16[1024,768]{1,0:T(8,128)(2,1)}, bf16[1024,768]{1,0:T(8,128)(2,1)}, f32[6,768]{1,0:T(8,128)}, /*index=5*/f32[1,3072]{1,0:T(1,128)}) custom-call(s32[3]{0:T(128)S(1)} %pad_add_fusion.sel_ref, bf16[1024,768]{1,0:T(8,128)(2,1)} %collective-permute-done.15.grad_ref, ...), custom_call_target="tpu_custom_call" | custom-call | flops 1 | bytes 1 | tf_op jit(solution)/shard_map/refine_back/pallas_call | solution.py:348
  472.2 15.8 %feed_grads.5 = bf16[8,768,384]{2,1,0:T(8,128)(2,1)} custom-call(s32[3]{0:T(128)} %pad_add_fusion.2.sel_ref, bf16[1024,768]{1,0:T(8,128)(2,1)} %get-tuple-element.401.hidden_ref, bf16[1024,3072]{1,0:T(8,128)(2,1)} %get-tuple-element.407.raised_late_ref, bf16[1024,3072]{1,0:T(8,128)(2,1)} %get-tuple-element.408.raised_ref, ...), custom_call_target="tpu_custom_call" | custom-call | flops 1 | bytes 1 | tf_op jit(solution)/shard_map/feed_grads/pallas_call | solution.py:453
  488.0 15.4 %feed_grads.4 = bf16[8,768,384]{2,1,0:T(8,128)(2,1)} custom-call(s32[3]{0:T(128)S(1)} %pad_add_fusion.sel_ref, bf16[1024,768]{1,0:T(8,128)(2,1)} %get-tuple-element.401.hidden_ref, bf16[1024,3072]{1,0:T(8,128)(2,1)} %get-tuple-element.407.raised_late_ref, bf16[1024,3072]{1,0:T(8,128)(2,1)} %get-tuple-element.408.raised_ref, ...), custom_call_target="tpu_custom_call" | custom-call | flops 1 | bytes 1 | tf_op jit(solution)/shard_map/feed_grads/pallas_call | solution.py:453
  511.3 43.9 %mixed_backward.8 = (bf16[3,1024,768]{2,1,0:T(8,128)(2,1)}, bf16[1024,768]{1,0:T(8,128)(2,1)}, f32[2,768]{1,0:T(2,128)}) custom-call(s32[8]{0:T(128)S(1)} %get-tuple-element.536.begin_ref, s32[8]{0:T(128)S(1)} %get-tuple-element.537.count_ref, s32[3]{0:T(128)S(1)} %pad_add_fusion.sel_ref, bf16[3,1024,768]{2,1,0:T(8,128)(2,1)} %get-tuple-element.397.qkv_hbm, ...), custom_call_target="tpu_custom_call" | custom-call | flops 1 | bytes 1 | tf_op jit(solution)/shard_map/mixed_backward/pallas_call | solution.py:768
  555.2 9.3 attend_grads.5
  564.5 9.1 attend_grads.4
  585.4 5.5 collective-permute-start.19
  593.0 24.4 %refine_back.9 = (bf16[1024,768]{1,0:T(8,128)(2,1)}, bf16[1024,3072]{1,0:T(8,128)(2,1)}, bf16[1024,768]{1,0:T(8,128)(2,1)}, bf16[1024,768]{1,0:T(8,128)(2,1)}, f32[6,768]{1,0:T(8,128)}, /*index=5*/f32[1,3072]{1,0:T(1,128)}) custom-call(s32[3]{0:T(128)S(1)} %pad_add_fusion.sel_ref, bf16[1024,768]{1,0:T(8,128)(2,1)} %get-tuple-element.420.grad_ref, ...), custom_call_target="tpu_custom_call" | custom-call | flops 1 | bytes 1 | tf_op jit(solution)/shard_map/refine_back/pallas_call | solution.py:348
  620.4 15.6 %feed_grads.6 = bf16[8,768,384]{2,1,0:T(8,128)(2,1)} custom-call(s32[3]{0:T(128)} %pad_add_fusion.2.sel_ref, bf16[1024,768]{1,0:T(8,128)(2,1)} %get-tuple-element.441.hidden_ref, bf16[1024,3072]{1,0:T(8,128)(2,1)} %get-tuple-element.442.raised_late_ref, bf16[1024,3072]{1,0:T(8,128)(2,1)} %get-tuple-element.443.raised_ref, ...), custom_call_target="tpu_custom_call" | custom-call | flops 1 | bytes 1 | tf_op jit(solution)/shard_map/feed_grads/pallas_call | solution.py:453
  645.6 11.0 %collective-permute-done.22 = bf16[768,384]{1,0:T(8,128)(2,1)} collective-permute-done((bf16[768,384]{1,0:T(8,128)(2,1)}, bf16[768,384]{1,0:T(8,128)(2,1)}, u32[]{:S(2)}, u32[]{:S(2)}) %collective-permute-start.22) | collective-permute-done | bytes 589856 | tf_op jit(solution)/shard_map/ppermute | solution.py:852
  676.8 15.5 %feed_grads.7 = bf16[8,768,384]{2,1,0:T(8,128)(2,1)} custom-call(s32[3]{0:T(128)S(1)} %pad_add_fusion.sel_ref, bf16[1024,768]{1,0:T(8,128)(2,1)} %get-tuple-element.441.hidden_ref, bf16[1024,3072]{1,0:T(8,128)(2,1)} %get-tuple-element.442.raised_late_ref, bf16[1024,3072]{1,0:T(8,128)(2,1)} %get-tuple-element.443.raised_ref, ...), custom_call_target="tpu_custom_call" | custom-call | flops 1 | bytes 1 | tf_op jit(solution)/shard_map/feed_grads/pallas_call | solution.py:453
  717.4 44.8 %mixed_backward.9 = (bf16[3,1024,768]{2,1,0:T(8,128)(2,1)}, bf16[1024,768]{1,0:T(8,128)(2,1)}, f32[2,768]{1,0:T(2,128)}) custom-call(s32[8]{0:T(128)S(1)} %get-tuple-element.536.begin_ref, s32[8]{0:T(128)S(1)} %get-tuple-element.537.count_ref, s32[3]{0:T(128)S(1)} %pad_add_fusion.sel_ref, bf16[3,1024,768]{2,1,0:T(8,128)(2,1)} %get-tuple-element.394.qkv_hbm, ...), custom_call_target="tpu_custom_call" | custom-call | flops 1 | bytes 1 | tf_op jit(solution)/shard_map/mixed_backward/pallas_call | solution.py:768
  780.9 8.4 attend_grads.6
  799.3 5.2 collective-permute-done.58
  814.9 8.7 collective-permute-done.60
  843.0 8.3 attend_grads.7
  873.2 6.1 collective-permute-start.41
  882.8 10.9 %collective-permute-done.41 = bf16[4,208,384]{2,1,0:T(8,128)(2,1)S(1)} collective-permute-done((bf16[4,208,384]{2,1,0:T(8,128)(2,1)S(1)}, bf16[4,208,384]{2,1,0:T(8,128)(2,1)S(1)}, u32[]{:S(2)}, u32[]{:S(2)}) %collective-permute-start.41) | collective-permute-done | bytes 639008 | tf_op jit(solution)/shard_map/ppermute | solution.py:841
  930.6 7.2 collective-permute-start.56
  (334 shorter events, 254.2 us)
Async XLA Ops:
  9.6 21.8 %collective-permute-start.5 = (bf16[768,3072]{1,0:T(8,128)(2,1)}, bf16[768,3072]{1,0:T(8,128)(2,1)}, u32[]{:S(2)}, u32[]{:S(2)}) collective-permute-start(bf16[768,3072]{1,0:T(8,128)(2,1)} %bitcast.250), channel_id=1, source_target_pairs={{0,8},{8,0},{16,24},{24,16},{1,9},{9,1},{17,25},{25,17},{2,10},{10... | collective-permute-start | bytes 14155784 | tf_op jit(solution)/shard_map/ppermute | solution.py:816
  9.7 21.7 %collective-permute-start.6 = (bf16[3072,768]{1,0:T(8,128)(2,1)}, bf16[3072,768]{1,0:T(8,128)(2,1)}, u32[]{:S(2)}, u32[]{:S(2)}) collective-permute-start(bf16[3072,768]{1,0:T(8,128)(2,1)} %bitcast.256), channel_id=1, source_target_pairs={{0,8},{8,0},{16,24},{24,16},{1,9},{9,1},{17,25},{25,17},{2,10},{10... | collective-permute-start | bytes 14155784 | tf_op jit(solution)/shard_map/ppermute | solution.py:816
  13.4 17.9 %collective-permute-start.3 = (bf16[768,2304]{1,0:T(8,128)(2,1)}, bf16[768,2304]{1,0:T(8,128)(2,1)}, u32[]{:S(2)}, u32[]{:S(2)}) collective-permute-start(bf16[768,2304]{1,0:T(8,128)(2,1)} %bitcast.262), channel_id=1, source_target_pairs={{0,8},{8,0},{16,24},{24,16},{1,9},{9,1},{17,25},{25,17},{2,10},{10... | collective-permute-start | bytes 10616840 | tf_op jit(solution)/shard_map/ppermute | solution.py:816
  138.4 37.2 %collective-permute-start.8 = (bf16[1024,768]{1,0:T(8,128)(2,1)}, bf16[1024,768]{1,0:T(8,128)(2,1)}, u32[]{:S(2)}, u32[]{:S(2)}) collective-permute-start(bf16[1024,768]{1,0:T(8,128)(2,1)} %get-tuple-element.385), channel_id=1, source_target_pairs={{0,16},{8,24},{1,17},{9,25},{2,18},{10,26},{3,19},{11,27},{4,20},{... | collective-permute-start | bytes 4718600 | tf_op jit(solution)/shard_map/ppermute | solution.py:816
  146.2 25.3 %collective-permute-start.10 = (bf16[32,1792]{1,0:T(8,128)(2,1)}, bf16[32,1792]{1,0:T(8,128)(2,1)}, u32[]{:S(2)}, u32[]{:S(2)}) collective-permute-start(bf16[32,1792]{1,0:T(8,128)(2,1)} %get-tuple-element.590), channel_id=1, source_target_pairs={{0,16},{8,24},{1,17},{9,25},{2,18},{10,26},{3,19},{11,27},{4,20},{... | collective-permute-start | bytes 344072 | tf_op jit(solution)/shard_map/ppermute | solution.py:816
  428.8 19.0 %collective-permute-start.15 = (bf16[1024,768]{1,0:T(8,128)(2,1)}, bf16[1024,768]{1,0:T(8,128)(2,1)}, u32[]{:S(2)}, u32[]{:S(2)}) collective-permute-start(bf16[1024,768]{1,0:T(8,128)(2,1)} %get-tuple-element.400), channel_id=1, source_target_pairs={{16,0},{24,8},{17,1},{25,9},{18,2},{26,10},{19,3},{27,11},{20,4},{... | collective-permute-start | bytes 4718600 | tf_op jit(solution)/shard_map/ppermute | solution.py:816
  511.3 62.3 %collective-permute-start.18 = (bf16[4,768,384]{2,1,0:T(8,128)(2,1)}, bf16[4,768,384]{2,1,0:T(8,128)(2,1)}, u32[]{:S(2)}, u32[]{:S(2)}) collective-permute-start(bf16[4,768,384]{2,1,0:T(8,128)(2,1)} %dynamic-slice_bitcast_fusion.1), channel_id=1, source_target_pairs={{0,1},{1,0},{2,3},{3,2},{4,5},{5,4},{6,7},{7,6},{8,9},{9,8},{10,11... | collective-permute-start | bytes 7077896 | tf_op jit(solution)/shard_map/ppermute | solution.py:841
  583.0 34.4 %collective-permute-start.21 = (bf16[4,384,384]{2,1,0:T(8,128)(2,1)}, bf16[4,384,384]{2,1,0:T(8,128)(2,1)}, u32[]{:S(2)}, u32[]{:S(2)}) collective-permute-start(bf16[4,384,384]{2,1,0:T(8,128)(2,1)} %dynamic-slice_bitcast_fusion.2), channel_id=1, source_target_pairs={{0,1},{1,0},{2,3},{3,2},{4,5},{5,4},{6,7},{7,6},{8,9},{9,8},{10,11... | collective-permute-start | bytes 3538952 | tf_op jit(solution)/shard_map/ppermute | solution.py:841
  585.4 35.0 %collective-permute-start.19 = (bf16[768,384]{1,0:T(8,128)(2,1)}, bf16[768,384]{1,0:T(8,128)(2,1)}, u32[]{:S(2)}, u32[]{:S(2)}) collective-permute-start(bf16[768,384]{1,0:T(8,128)(2,1)} %get-tuple-element.553), channel_id=1, source_target_pairs={{0,2},{1,3},{2,4},{3,5},{4,6},{5,7},{8,10},{9,11},{10,12},{11,13},... | collective-permute-start | bytes 1769480 | tf_op jit(solution)/shard_map/ppermute | solution.py:852
  590.9 29.5 %collective-permute-start.20 = (bf16[768,384]{1,0:T(8,128)(2,1)}, bf16[768,384]{1,0:T(8,128)(2,1)}, u32[]{:S(2)}, u32[]{:S(2)}) collective-permute-start(bf16[768,384]{1,0:T(8,128)(2,1)} %get-tuple-element.552), channel_id=1, source_target_pairs={{2,0},{3,1},{4,2},{5,3},{6,4},{7,5},{10,8},{11,9},{12,10},{13,11},... | collective-permute-start | bytes 1769480 | tf_op jit(solution)/shard_map/ppermute | solution.py:853
  635.9 58.8 %collective-permute-start.24 = (bf16[8,768,384]{2,1,0:T(8,128)(2,1)}, bf16[8,768,384]{2,1,0:T(8,128)(2,1)}, u32[]{:S(2)}, u32[]{:S(2)}) collective-permute-start(bf16[8,768,384]{2,1,0:T(8,128)(2,1)} %feed_grads.6), channel_id=1, source_target_pairs={{0,8},{8,0},{16,24},{24,16},{1,9},{9,1},{17,25},{25,17},{2,10},{10... | collective-permute-start | bytes 14155784 | tf_op jit(solution)/shard_map/ppermute | solution.py:816
  662.8 29.4 %collective-permute-start.25 = (bf16[768,384]{1,0:T(8,128)(2,1)}, bf16[768,384]{1,0:T(8,128)(2,1)}, u32[]{:S(2)}, u32[]{:S(2)}) collective-permute-start(bf16[768,384]{1,0:T(8,128)(2,1)} %get-tuple-element.548), channel_id=1, source_target_pairs={{0,2},{1,3},{2,4},{3,5},{4,6},{5,7},{8,10},{9,11},{10,12},{11,13},... | collective-permute-start | bytes 1769480 | tf_op jit(solution)/shard_map/ppermute | solution.py:852
  665.2 27.0 %collective-permute-start.26 = (bf16[768,384]{1,0:T(8,128)(2,1)}, bf16[768,384]{1,0:T(8,128)(2,1)}, u32[]{:S(2)}, u32[]{:S(2)}) collective-permute-start(bf16[768,384]{1,0:T(8,128)(2,1)} %get-tuple-element.549), channel_id=1, source_target_pairs={{2,0},{3,1},{4,2},{5,3},{6,4},{7,5},{10,8},{11,9},{12,10},{13,11},... | collective-permute-start | bytes 1769480 | tf_op jit(solution)/shard_map/ppermute | solution.py:853
  670.8 28.9 %collective-permute-start.27 = (bf16[384,384]{1,0:T(8,128)(2,1)}, bf16[384,384]{1,0:T(8,128)(2,1)}, u32[]{:S(2)}, u32[]{:S(2)}) collective-permute-start(bf16[384,384]{1,0:T(8,128)(2,1)} %get-tuple-element.568), channel_id=1, source_target_pairs={{0,2},{1,3},{2,4},{3,5},{4,6},{5,7},{8,10},{9,11},{10,12},{11,13},... | collective-permute-start | bytes 884744 | tf_op jit(solution)/shard_map/ppermute | solution.py:852
  672.7 27.0 %collective-permute-start.28 = (bf16[384,384]{1,0:T(8,128)(2,1)S(1)}, bf16[384,384]{1,0:T(8,128)(2,1)}, u32[]{:S(2)}, u32[]{:S(2)}) collective-permute-start(bf16[384,384]{1,0:T(8,128)(2,1)S(1)} %get-tuple-element.567), channel_id=1, source_target_pairs={{2,0},{3,1},{4,2},{5,3},{6,4},{7,5},{10,8},{11,9},{12,10},{13,11},... | collective-permute-start | bytes 884744 | tf_op jit(solution)/shard_map/ppermute | solution.py:853
  702.6 59.7 %collective-permute-start.34 = (bf16[4,768,384]{2,1,0:T(8,128)(2,1)}, bf16[4,768,384]{2,1,0:T(8,128)(2,1)}, u32[]{:S(2)}, u32[]{:S(2)}) collective-permute-start(bf16[4,768,384]{2,1,0:T(8,128)(2,1)} %dynamic-slice_bitcast_fusion), channel_id=1, source_target_pairs={{0,1},{1,0},{2,3},{3,2},{4,5},{5,4},{6,7},{7,6},{8,9},{9,8},{10,11... | collective-permute-start | bytes 7077896 | tf_op jit(solution)/shard_map/ppermute | solution.py:841
  704.2 103.0 %collective-permute-start.12 = (bf16[32,1024]{1,0:T(8,128)(2,1)}, bf16[32,1024]{1,0:T(8,128)(2,1)}, u32[]{:S(2)}, u32[]{:S(2)}) collective-permute-start(bf16[32,1024]{1,0:T(8,128)(2,1)} %get-tuple-element.583), channel_id=1, source_target_pairs={{0,8},{8,0},{16,24},{24,16},{1,9},{9,1},{17,25},{25,17},{2,10},{10... | collective-permute-start | bytes 196616 | tf_op jit(solution)/shard_map/ppermute | solution.py:816
  706.4 102.8 %collective-permute-start.13 = (bf16[32,1024]{1,0:T(8,128)(2,1)}, bf16[32,1024]{1,0:T(8,128)(2,1)}, u32[]{:S(2)}, u32[]{:S(2)}) collective-permute-start(bf16[32,1024]{1,0:T(8,128)(2,1)} %get-tuple-element.582), channel_id=1, source_target_pairs={{16,8},{24,0},{17,9},{25,1},{18,10},{26,2},{19,11},{27,3},{20,12},... | collective-permute-start | bytes 196616 | tf_op jit(solution)/shard_map/ppermute | solution.py:816
  711.0 98.3 %collective-permute-start.14 = (bf16[32,1024]{1,0:T(8,128)(2,1)}, bf16[32,1024]{1,0:T(8,128)(2,1)}, u32[]{:S(2)}, u32[]{:S(2)}) collective-permute-start(bf16[32,1024]{1,0:T(8,128)(2,1)} %get-tuple-element.581), channel_id=1, source_target_pairs={{16,0},{24,8},{17,1},{25,9},{18,2},{26,10},{19,3},{27,11},{20,4},{... | collective-permute-start | bytes 196616 | tf_op jit(solution)/shard_map/ppermute | solution.py:816
  715.5 53.9 %collective-permute-start.32 = (bf16[384,384]{1,0:T(8,128)(2,1)}, bf16[384,384]{1,0:T(8,128)(2,1)}, u32[]{:S(2)}, u32[]{:S(2)}) collective-permute-start(bf16[384,384]{1,0:T(8,128)(2,1)} %get-tuple-element.566), channel_id=1, source_target_pairs={{0,2},{1,3},{2,4},{3,5},{4,6},{5,7},{8,10},{9,11},{10,12},{11,13},... | collective-permute-start | bytes 884744 | tf_op jit(solution)/shard_map/ppermute | solution.py:852
  795.7 63.4 %collective-permute-start.40 = (bf16[8,384,384]{2,1,0:T(8,128)(2,1)}, bf16[8,384,384]{2,1,0:T(8,128)(2,1)}, u32[]{:S(2)}, u32[]{:S(2)}) collective-permute-start(bf16[8,384,384]{2,1,0:T(8,128)(2,1)} %attend_grads.6), channel_id=1, source_target_pairs={{0,8},{8,0},{16,24},{24,16},{1,9},{9,1},{17,25},{25,17},{2,10},{10... | collective-permute-start | bytes 7077896 | tf_op jit(solution)/shard_map/ppermute | solution.py:816
  812.3 19.5 %collective-permute-start.30 = (bf16[256,768]{1,0:T(8,128)(2,1)S(1)}, bf16[256,768]{1,0:T(8,128)(2,1)S(1)}, u32[]{:S(2)}, u32[]{:S(2)}) collective-permute-start(bf16[256,768]{1,0:T(8,128)(2,1)S(1)} %get-tuple-element.555), channel_id=1, source_target_pairs={{0,8},{8,0},{16,24},{24,16},{1,9},{9,1},{17,25},{25,17},{2,10},{10... | collective-permute-start | bytes 1179656 | tf_op jit(solution)/shard_map/ppermute | solution.py:816
  812.8 23.7 %collective-permute-start.31 = (bf16[256,768]{1,0:T(8,128)(2,1)S(1)}, bf16[256,768]{1,0:T(8,128)(2,1)S(1)}, u32[]{:S(2)}, u32[]{:S(2)}) collective-permute-start(bf16[256,768]{1,0:T(8,128)(2,1)S(1)} %get-tuple-element.554), channel_id=1, source_target_pairs={{0,16},{8,24},{1,17},{9,25},{2,18},{10,26},{3,19},{11,27},{4,20},{... | collective-permute-start | bytes 1179656 | tf_op jit(solution)/shard_map/ppermute | solution.py:816
  823.6 55.7 %collective-permute-start.57 = (bf16[768,384]{1,0:T(8,128)(2,1)S(1)}, bf16[768,384]{1,0:T(8,128)(2,1)}, u32[]{:S(2)}, u32[]{:S(2)}) collective-permute-start(bf16[768,384]{1,0:T(8,128)(2,1)S(1)} %copy-done.17), channel_id=1, source_target_pairs={{0,8},{16,24},{1,9},{17,25},{2,10},{18,26},{3,11},{19,27},{4,12},{... | collective-permute-start | bytes 1769480 | tf_op jit(solution)/shard_map/ppermute | solution.py:816
  828.0 23.3 %collective-permute-start.59 = (bf16[768,384]{1,0:T(8,128)(2,1)}, bf16[768,384]{1,0:T(8,128)(2,1)}, u32[]{:S(2)}, u32[]{:S(2)}) collective-permute-start(bf16[768,384]{1,0:T(8,128)(2,1)} %get-tuple-element.544), channel_id=1, source_target_pairs={{0,2},{1,3},{2,4},{3,5},{4,6},{5,7},{8,10},{9,11},{10,12},{11,13},... | collective-permute-start | bytes 1769480 | tf_op jit(solution)/shard_map/ppermute | solution.py:852
  831.7 22.5 %collective-permute-start.61 = (bf16[768,384]{1,0:T(8,128)(2,1)}, bf16[768,384]{1,0:T(8,128)(2,1)}, u32[]{:S(2)}, u32[]{:S(2)}) collective-permute-start(bf16[768,384]{1,0:T(8,128)(2,1)} %fusion.5), channel_id=1, source_target_pairs={{2,0},{3,1},{4,2},{5,3},{6,4},{7,5},{10,8},{11,9},{12,10},{13,11},... | collective-permute-start | bytes 1769480 | tf_op jit(solution)/shard_map/ppermute | solution.py:853
  839.7 24.6 %collective-permute-start.35 = (bf16[384,384]{1,0:T(8,128)(2,1)}, bf16[384,384]{1,0:T(8,128)(2,1)}, u32[]{:S(2)}, u32[]{:S(2)}) collective-permute-start(bf16[384,384]{1,0:T(8,128)(2,1)} %get-tuple-element.563), channel_id=1, source_target_pairs={{0,2},{1,3},{2,4},{3,5},{4,6},{5,7},{8,10},{9,11},{10,12},{11,13},... | collective-permute-start | bytes 884744 | tf_op jit(solution)/shard_map/ppermute | solution.py:852
  855.9 25.4 %collective-permute-start.62 = (bf16[768,384]{1,0:T(8,128)(2,1)S(1)}, bf16[768,384]{1,0:T(8,128)(2,1)S(1)}, u32[]{:S(2)}, u32[]{:S(2)}) collective-permute-start(bf16[768,384]{1,0:T(8,128)(2,1)S(1)} %fusion.9), channel_id=1, source_target_pairs={{8,0},{24,16},{9,1},{25,17},{10,2},{26,18},{11,3},{27,19},{12,4},{... | collective-permute-start | bytes 1769480 | tf_op jit(solution)/shard_map/ppermute | solution.py:816
  866.1 75.5 %collective-permute-start.37 = (bf16[384,384]{1,0:T(8,128)(2,1)}, bf16[384,384]{1,0:T(8,128)(2,1)}, u32[]{:S(2)}, u32[]{:S(2)}) collective-permute-start(bf16[384,384]{1,0:T(8,128)(2,1)} %fusion.27), channel_id=1, source_target_pairs={{0,8},{16,24},{1,9},{17,25},{2,10},{18,26},{3,11},{19,27},{4,12},{... | collective-permute-start | bytes 884744 | tf_op jit(solution)/shard_map/ppermute | solution.py:816
  867.6 31.7 %collective-permute-start.52 = (bf16[2,224,384]{2,1,0:T(8,128)(2,1)S(1)}, bf16[2,224,384]{2,1,0:T(8,128)(2,1)S(1)}, u32[]{:S(2)}, u32[]{:S(2)}) collective-permute-start(bf16[2,224,384]{2,1,0:T(8,128)(2,1)S(1)} %get-tuple-element.560), channel_id=1, source_target_pairs={{2,0},{3,1},{4,2},{5,3},{6,4},{7,5},{10,8},{11,9},{12,10},{13,11},... | collective-permute-start | bytes 1032200 | tf_op jit(solution)/shard_map/ppermute | solution.py:853
  873.2 20.5 %collective-permute-start.41 = (bf16[4,208,384]{2,1,0:T(8,128)(2,1)S(1)}, bf16[4,208,384]{2,1,0:T(8,128)(2,1)S(1)}, u32[]{:S(2)}, u32[]{:S(2)}) collective-permute-start(bf16[4,208,384]{2,1,0:T(8,128)(2,1)S(1)} %dynamic-slice_bitcast_fusion.3), channel_id=1, source_target_pairs={{0,1},{1,0},{2,3},{3,2},{4,5},{5,4},{6,7},{7,6},{8,9},{9,8},{10,11... | collective-permute-start | bytes 1916936 | tf_op jit(solution)/shard_map/ppermute | solution.py:841
  879.4 19.9 %collective-permute-start.50 = (bf16[2,224,384]{2,1,0:T(8,128)(2,1)S(1)}, bf16[2,224,384]{2,1,0:T(8,128)(2,1)S(1)}, u32[]{:S(2)}, u32[]{:S(2)}) collective-permute-start(bf16[2,224,384]{2,1,0:T(8,128)(2,1)S(1)} %fusion.18), channel_id=1, source_target_pairs={{0,2},{1,3},{2,4},{3,5},{4,6},{5,7},{8,10},{9,11},{10,12},{11,13},... | collective-permute-start | bytes 1032200 | tf_op jit(solution)/shard_map/ppermute | solution.py:852
  (67 other events, 1564.0 us)

commit v4 on v3

--- a/solution.py
+++ b/solution.py
@@ -16,7 +16,12 @@
 EPS_PROJ = 1e-06
 NEG_FILL = -1e30
 PARAMS = pltpu.CompilerParams(vmem_limit_bytes=60 * 1024 * 1024)
-COST = pl.CostEstimate(flops=1, bytes_accessed=1, transcendentals=0)
+
+
+def cost(micros):
+    return pl.CostEstimate(flops=int(micros * 1e9), bytes_accessed=1024, transcendentals=0)
+
+
 BF = jnp.bfloat16
 F32 = jnp.float32
 
@@ -373,7 +378,7 @@
             jax.ShapeDtypeStruct((1, ff_width), F32),
         ],
         compiler_params=PARAMS,
-        cost_estimate=COST,
+        cost_estimate=cost(24),
     )(sel, grad, hidden, out, scale1, scale2, slope, *w_out, *w_up, *w_down, small)
 
 
@@ -401,7 +406,7 @@
             jax.ShapeDtypeStruct((length, width), BF),
         ],
         compiler_params=PARAMS,
-        cost_estimate=COST,
+        cost_estimate=cost(6),
     )(rows, proj, given)
 
 
@@ -410,36 +415,38 @@
 
 
 def feed_grads_kernel(
-    sel_ref, hidden_ref, raised_late_ref, raised_ref, active_ref, low_late_ref, low_ref, out_ref,
-    hidden_scr, low_scr, raised_scr,
+    sel_ref, hidden_ref, raised_late_ref, raised_ref, active_ref, low_late_ref, low_ref, out_ref
 ):
     step = pl.program_id(0)
+    shards, rows, _ = out_ref.shape
     blocks = raised_ref.shape[1] // HALF
-    share = hidden_ref.shape[1] // SHARDS
+    share = rows // blocks
     late = sel_ref[1] == 1
 
-    @pl.when(step == 0)
-    def _():
-        hidden_scr[...] = hidden_ref[...].T
-        low_scr[...] = jnp.where(late, low_late_ref[...], low_ref[...]).T
-        raised_scr[...] = jnp.where(late, raised_late_ref[...], raised_ref[...])
-
-    @pl.when(step < 4)
-    def _():
-        at = pl.multiple_of(step * (2 * share), 2 * share)
-        part = dot(hidden_scr[pl.ds(at, 2 * share), :], raised_scr[...]).astype(BF)
-        for m in range(2):
+    def up(raised):
+        part = dot_tn(hidden_ref[...], raised).astype(BF)
+        for m in range(shards):
             for n in range(blocks):
                 out_ref[m, n * share : (n + 1) * share, :] = part[
                     m * share : (m + 1) * share, n * HALF : (n + 1) * HALF
                 ]
 
-    @pl.when(step >= 4)
-    def _():
-        rows = out_ref.shape[1]
-        for m in range(2):
-            part = dot(low_scr[...], active_ref[:, m * rows : (m + 1) * rows])
-            out_ref[m] = part.T.astype(BF)
+    def down(low):
+        for m in range(shards):
+            out_ref[m] = dot_tn(active_ref[:, m * rows : (m + 1) * rows], low).astype(BF)
+
+    for wanted, raised_now, low_now in (
+        (late, raised_late_ref, low_late_ref),
+        (jnp.logical_not(late), raised_ref, low_ref),
+    ):
+
+        @pl.when(wanted & (step < 2))
+        def _():
+            up(raised_now[...])
+
+        @pl.when(wanted & (step >= 2))
+        def _():
+            down(low_now[...])
 
 
 def feed_grads(sel, hidden, raised_late, raised, active, low_late, low):
@@ -455,51 +462,45 @@
         name="feed_grads",
         grid_spec=pltpu.PrefetchScalarGridSpec(
             num_scalar_prefetch=1,
-            grid=(8,),
+            grid=(4,),
             in_specs=[
-                pl.BlockSpec((length, width), lambda n, _: (0, 0)),
+                pl.BlockSpec((length, width // 2), lambda n, _: (0, jnp.minimum(n, 1))),
                 late_spec((length, half_ff), 1),
                 late_spec((length, half_ff), 0),
-                pl.BlockSpec((length, ff_width // 4), lambda n, _: (0, jnp.maximum(n - 4, 0))),
+                pl.BlockSpec((length, ff_width // 2), lambda n, _: (0, jnp.maximum(n - 2, 0))),
                 late_spec((length, width // 2), 1),
                 late_spec((length, width // 2), 0),
             ],
             out_specs=pl.BlockSpec(
-                (2, ff_width // SHARDS, HALF), lambda n, _: (lax.rem(n, 4), n // 4, 0)
+                (SHARDS // 2, ff_width // SHARDS, HALF), lambda n, _: (lax.rem(n, 2), n // 2, 0)
             ),
-            scratch_shapes=[
-                pltpu.VMEM((width, length), BF),
-                pltpu.VMEM((width // 2, length), BF),
-                pltpu.VMEM((length, half_ff), BF),
-            ],
         ),
         out_shape=jax.ShapeDtypeStruct((SHARDS, 2 * (ff_width // SHARDS), HALF), BF),
         compiler_params=PARAMS,
-        cost_estimate=COST,
+        cost_estimate=cost(12),
     )(sel, hidden, raised_late, raised, active, low_late, low)
 
 
 def attend_grads_kernel(
-    sel_ref, context_ref, x_ref, attn_late_ref, attn_ref, mixed_late_ref, mixed_ref, out_ref, turned
+    sel_ref, context_ref, x_ref, attn_late_ref, attn_ref, mixed_late_ref, mixed_ref, out_ref
 ):
     step = pl.program_id(0)
     late = sel_ref[1] == 1
 
-    def store(cols):
-        out_ref[...] = dot(turned[...], cols).astype(BF).reshape(out_ref.shape)
-
-    @pl.when(step == 0)
-    def _():
-        turned[...] = context_ref[...].T
-        store(jnp.where(late, attn_late_ref[...], attn_ref[...]))
-
-    @pl.when(step == 1)
-    def _():
-        turned[...] = x_ref[...].T
-
-    @pl.when(step > 0)
-    def _():
-        store(jnp.where(late, mixed_late_ref[0], mixed_ref[0]))
+    for wanted, attn_now, mixed_now in (
+        (late, attn_late_ref, mixed_late_ref),
+        (jnp.logical_not(late), attn_ref, mixed_ref),
+    ):
+
+        @pl.when(wanted & (step == 0))
+        def _():
+            part = dot_tn(context_ref[...], attn_now[...]).astype(BF)
+            out_ref[...] = part.reshape(out_ref.shape)
+
+        @pl.when(wanted & (step > 0))
+        def _():
+            part = dot_tn(x_ref[...], mixed_now[0]).astype(BF)
+            out_ref[...] = part.reshape(out_ref.shape)
 
 
 def attend_grads(sel, context, x, attn_late, attn, mixed_late, mixed):
@@ -530,11 +531,10 @@
             grid=(4,),
             in_specs=[whole, whole, late_spec(1), late_spec(0), mixed_spec(1), mixed_spec(0)],
             out_specs=pl.BlockSpec((SHARDS, share, HALF), lambda n, _: (0, n, 0)),
-            scratch_shapes=[pltpu.VMEM((width, length), BF)],
         ),
         out_shape=jax.ShapeDtypeStruct((SHARDS, 4 * share, HALF), BF),
         compiler_params=PARAMS,
-        cost_estimate=COST,
+        cost_estimate=cost(8),
     )(sel, context, x, attn_late, attn, mixed_late, mixed)
 
 
@@ -693,7 +693,7 @@
             jax.ShapeDtypeStruct(logsum_shape, F32), row, row, lanes, lanes, wide, wide,
         ],
         compiler_params=PARAMS,
-        cost_estimate=COST,
+        cost_estimate=cost(48),
     )(begin, count, sel, x, key_code, query_code, *w_qkv, *w_out, *w_up, *w_down, small)
     return (out, (x, qkv, context, logsum, hidden, out, scale1, scale2, slope, active))
 
@@ -796,7 +796,7 @@
             jax.ShapeDtypeStruct((2, width), F32),
         ],
         compiler_params=PARAMS,
-        cost_estimate=COST,
+        cost_estimate=cost(38),
     )(begin, count, sel, qkv, key_code, query_code, context, logsum, grad_context, skip, *w_qkv)
 
 
@@ -825,23 +825,30 @@
 
 
 class RowSum:
-    def __init__(self, value, x_first):
-        at = lax.axis_index("dp")
-        self.z, self.x, self.x_first = at // 2, at % 2, x_first
-        self.value = value.reshape(4, 2, *value.shape[1:])
-        self.travelling = None
-        self.steps = [self.cross, self.line, self.line, self.line]
-        if not x_first:
-            self.steps = self.steps[1:] + self.steps[:1]
-        self.line_at = 0
+    def __init__(self, value, blocks):
+        self.value, self.blocks, self.travelling = value, blocks, None
+        self.plain = lax.axis_size("dp") != SHARDS
+        if not self.plain:
+            at = lax.axis_index("dp")
+            self.z, self.x, self.line_at = at // 2, at % 2, 0
+
+    def state(self):
+        return (self.value, self.travelling)
+
+    def set(self, state):
+        self.value, self.travelling = state
 
     def cross(self):
-        axis = 1 if self.x_first else 0
-        other = pick_row(self.value, 1 - self.x, axis)
+        if self.plain:
+            return
+        value = self.value.reshape(4, 2, *self.value.shape[1:])
+        other = pick_row(value, 1 - self.x, 1)
         arrived = lax.ppermute(other, "dp", [(n, n ^ 1) for n in range(8)])
-        self.value = plus(pick_row(self.value, self.x, axis), arrived)
+        self.value = plus(pick_row(value, self.x, 1), arrived)
 
     def line(self):
+        if self.plain:
+            return
         self.line_at += 1
         far = 4 - self.line_at
         right = pick_row(self.value, jnp.minimum(self.z + far, 3))
@@ -852,35 +859,28 @@
             lax.ppermute(right, "dp", [(n, n + 2) for n in range(6)]),
             lax.ppermute(left, "dp", [(n + 2, n) for n in range(6)]),
         )
-        if self.line_at == 3:
-            self.value = plus(pick_row(self.value, self.z), *self.travelling)
-
-    def step(self):
-        if self.steps:
-            self.steps.pop(0)()
+
+    def direct(self):
+        if self.plain:
+            return
+        arrived = []
+        for far in (3, 2, 1):
+            for way in (far, -far):
+                part = pick_row(self.value, jnp.clip(self.z + way, 0, 3))
+                routes = [(n, n + 2 * way) for n in range(8) if 0 <= n + 2 * way < 8]
+                arrived.append(lax.ppermute(part, "dp", routes))
+        self.travelling = tuple(arrived)
 
     def result(self):
-        while self.steps:
-            self.step()
-        return self.value
-
-
-class PlainSum:
-    def __init__(self, value, blocks):
+        if not self.plain:
+            return plus(pick_row(self.value, self.z), *self.travelling)
         shards = lax.axis_size("dp")
         parts, at = [], 0
-        for rows in blocks:
-            part = value[:, at : at + rows].reshape(shards, -1, value.shape[2])
+        for rows in self.blocks:
+            part = self.value[:, at : at + rows].reshape(shards, -1, self.value.shape[2])
             parts, at = parts + [part], at + rows
         whole = jnp.concatenate(parts, axis=1)
-        self.value = lax.psum_scatter(whole, "dp", scatter_dimension=0, tiled=True)[0]
-        self.travelling = None
-
-    def step(self):
-        pass
-
-    def result(self):
-        return self.value
+        return lax.psum_scatter(whole, "dp", scatter_dimension=0, tiled=True)[0]
 
 
 def body(
@@ -983,70 +983,66 @@
     attend_blocks = (rows_of_one,) * 4
     feed_blocks = (rows_of_one,) * (ff_width // (2 * HALF)) + (ff_width // SHARDS,)
 
-    def row_sum(value, blocks):
-        return RowSum(value, True) if shards == SHARDS else PlainSum(value, blocks)
-
-    def feed_sum(kept, late, now):
-        args = (kept[4], late[1], now[1], kept[9], late[0], now[0])
-        arrived = swap_cores(feed_grads(sel_theirs, *args))
-        return row_sum(plus(feed_grads(sel_mine, *args), arrived), feed_blocks)
-
-    def attend_parts(kept, late, now, mixed):
-        args = (kept[2], kept[0], late[2], now[2], late[3], mixed)
-        return (attend_grads(sel_theirs, *args), attend_grads(sel_mine, *args))
-
     def merged(late_sums, sums):
         return tuple(jnp.where(is_late, a, b) for a, b in zip(late_sums, sums))
 
     def tie(*values):
         return lax.optimization_barrier(values)
 
+    def feed_args(kept, late, now):
+        return (kept[4], late[1], now[1], kept[9], late[0], now[0])
+
+    def attend_args(kept, late, now, mixed):
+        return (kept[2], kept[0], late[2], now[2], late[3], mixed)
+
+    def tie_sums(values, *sums):
+        values, states = tie(values, [part.state() for part in sums])
+        for part, state in zip(sums, states):
+            part.set(state)
+        return values
+
     grad_context, grads_odd, sums_odd = feed_backward(sel_mine, grad, kept_odd, weights, 1)
-    feed_odd = feed_sum(kept_odd, late_odd, grads_odd)
-    grad_context, feed_odd.value = tie(grad_context, feed_odd.value)
-    feed_odd.step()
+    args = feed_args(kept_odd, late_odd, grads_odd)
+    arrived = swap_cores(feed_grads(sel_theirs, *args))
+    feed_odd = RowSum(plus(feed_grads(sel_mine, *args), arrived), feed_blocks)
+    grad_context = tie_sums(grad_context, feed_odd)
+    feed_odd.cross()
     mixed_odd, grad, mix_sums = mixed_backward(
         sel_mine, grad_context, grads_odd[2], kept_odd, weights, 1, plan
     )
     sums_odd = merged(late_sums_odd, sums_odd + (mix_sums,))
-    theirs, mine = attend_parts(kept_odd, late_odd, grads_odd, mixed_odd)
-    attend_odd = row_sum(plus(mine, swap_cores(theirs)), attend_blocks)
-    grad, attend_odd.value, feed_odd.value = tie(grad, attend_odd.value, feed_odd.value)
-    feed_odd.step()
-    attend_odd.step()
+    args = tie_sums(attend_args(kept_odd, late_odd, grads_odd, mixed_odd), feed_odd)
+    feed_odd.line()
+    theirs = attend_grads(sel_theirs, *args)
+    args, theirs = tie_sums((args, theirs), feed_odd)
+    arrived = swap_cores(theirs)
+    attend_odd = RowSum(plus(attend_grads(sel_mine, *args), arrived), attend_blocks)
+    grad = tie_sums(grad, feed_odd, attend_odd)
+    feed_odd.line()
+    attend_odd.cross()
 
     grad_context, grads_even, sums_even = feed_backward(sel_mine, grad, kept_even, weights, 0)
-    args = (kept_even[4], late_even[1], grads_even[1], kept_even[9], late_even[0], grads_even[0])
-    args, feed_odd.travelling, attend_odd.value = tie(
-        args, feed_odd.travelling, attend_odd.value
-    )
-    feed_odd.step()
-    attend_odd.step()
+    args = tie_sums(feed_args(kept_even, late_even, grads_even), feed_odd, attend_odd)
+    feed_odd.line()
     theirs = feed_grads(sel_theirs, *args)
+    args, theirs = tie_sums((args, theirs), feed_odd)
     arrived = swap_cores(theirs)
-    args, theirs, feed_odd.travelling = tie(args, theirs, feed_odd.travelling)
-    feed_odd.step()
-    feed_even = row_sum(plus(feed_grads(sel_mine, *args), arrived), feed_blocks)
-    grad_context, feed_even.value, feed_odd.value, attend_odd.travelling = tie(
-        grad_context, feed_even.value, feed_odd.value, attend_odd.travelling
-    )
-    feed_even.step()
-    attend_odd.step()
+    feed_even = RowSum(plus(feed_grads(sel_mine, *args), arrived), feed_blocks)
+    grad_context = tie_sums(grad_context, feed_even, attend_odd)
+    feed_even.cross()
+    attend_odd.direct()
     mixed_even, grad, mix_sums = mixed_backward(
         sel_mine, grad_context, grads_even[2], kept_even, weights, 0, plan
     )
     sums_even = merged(late_sums_even, sums_even + (mix_sums,))
-    args = (kept_even[2], kept_even[0], late_even[2], grads_even[2], late_even[3], mixed_even)
-    args, attend_odd.travelling, feed_even.value = tie(
-        args, attend_odd.travelling, feed_even.value
-    )
-    feed_even.step()
-    attend_odd.step()
+    args = attend_args(kept_even, late_even, grads_even, mixed_even)
+    args = tie_sums(args, feed_even, attend_odd)
+    feed_even.line()
     theirs = attend_grads(sel_theirs, *args)
+    args, theirs = tie_sums((args, theirs), feed_even)
     arrived = swap_cores(theirs)
-    args, theirs, feed_even.travelling = tie(args, theirs, feed_even.travelling)
-    feed_even.step()
-    mine = attend_grads(sel_mine, *args)
+    feed_even.line()
+    attend_even = plus(attend_grads(sel_mine, *args), arrived)
 
     def small_rows(sums):
         sums, up_sums, mix_sums = sums
@@ -1064,26 +1060,20 @@
     extras = jnp.pad(extras, ((0, 0), (0, lines * HALF - extras.shape[1])))
     extras = extras.reshape(shards, lines, HALF).astype(BF)
     extras = plus(extras, swap_cores(extras))
-    attend_even = plus(mine, arrived)
+    attend_even = tie_sums(attend_even, feed_even)
+    feed_even.line()
     if shards == SHARDS:
-        tail = jnp.concatenate([attend_even, extras], axis=1)
-        cut = tail.shape[1] // 32 * 16
-        tails = [RowSum(tail[:, :cut], True), RowSum(tail[:, cut:], False)]
-        for n in range(4):
-            for part in tails:
-                part.step()
-            feed_even.step()
-        feed_odd, attend_odd, feed_even = [
-            part.result() for part in (feed_odd, attend_odd, feed_even)
-        ]
-        tail = jnp.concatenate([part.result() for part in tails], axis=0)
+        tail = RowSum(jnp.concatenate([attend_even, extras], axis=1), None)
+        tail.cross()
+        tail.direct()
+        tail = tail.result()
         attend_even, extras = tail[: 4 * share], tail[4 * share :]
     else:
-        feed_odd, attend_odd, feed_even = [
-            part.result() for part in (feed_odd, attend_odd, feed_even)
-        ]
-        attend_even = PlainSum(attend_even, attend_blocks).result()
+        attend_even = RowSum(attend_even, attend_blocks).result()
         extras = lax.psum_scatter(extras, "dp", scatter_dimension=0, tiled=True)[0]
+    feed_odd, attend_odd, feed_even = [
+        part.result() for part in (feed_odd, attend_odd, feed_even)
+    ]
 
     routes_odd, routes_even = ((0, 1), (2, 3)), ((1, 0), (3, 2))
 

time: 952 us -> 980 us (1.029)
  waiting for transfers between devices: 104 us -> 146 us
  other arithmetic: 79.1 us -> 57.3 us
  starting transfers between devices: 135 us -> 122 us
    ppermute x0 -> x12, starting transfers between devices: none -> 34.2 us  [direct(): arrived.append(lax.ppermute(part, 'dp', routes))]
    ppermute x15 -> x6, starting transfers between devices: 41.8 us -> 13.5 us  [line(): lax.ppermute(right, 'dp', [(n, n + 2) for n in range(6)])]
    ppermute x5 -> x4, waiting for transfers between devices: 12.2 us -> 34.8 us  [cross(): arrived = lax.ppermute(other, 'dp', [(n, n ^ 1) for n in range(8)])]
    ppermute x0 -> x12, waiting for transfers between devices: none -> 20.5 us  [direct(): arrived.append(lax.ppermute(part, 'dp', routes))]
    ppermute x15 -> x6, starting transfers between devices: 42.7 us -> 22.8 us  [line(): lax.ppermute(left, 'dp', [(n + 2, n) for n in range(6)])]
    ppermute x15 -> x6, waiting for transfers between devices: 19.1 us -> 3.61 us  [line(): lax.ppermute(right, 'dp', [(n, n + 2) for n in range(6)])]
    another operation x16, local copies, waits for them, and re-layouts: 1.24 us -> 12.5 us  [small_rows(): return jnp.concatenate([row.reshape(shards, -1) for row in rows], axis=1)]
    convert_element_type x28 -> x17, other arithmetic: 49.4 us -> 38.9 us  [plus(): return sum((value.astype(F32) for value in values)).astype(BF)]
  transfers between devices with their start and end apart: 64 -> 57, of which waited for: 18 -> 19; matrix products, arithmetic and copies ran while one was open for 9% -> 7% of each run, Pallas kernels for 19% -> 20%
where the time goes in v4:
time: 980 us; the launch traced here: 965 us
  Pallas kernels  593 us (61%)
  waiting for transfers between devices  146 us (15%)
  starting transfers between devices  122 us (12%)
  other arithmetic  57.3 us (6%)
  local copies, waits for them, and re-layouts  43.8 us (4%)
    pallas_call x4, Pallas kernels, layer_forward(): pl.pallas_call(partial(forward_kernel, layer), name='layer_forward', grid...  220 us
    pallas_call x4, Pallas kernels, mixed_backward(): pl.pallas_call(partial(mixed_backward_kernel, layer), name='mixed_backwar...  186 us
    pallas_call x4, Pallas kernels, refine_back(): pl.pallas_call(partial(refine_back_kernel, layer), name='refine_back', gr...  97.2 us
    ppermute x29, waiting for transfers between devices, send(): return lax.ppermute(value, 'section', routes)  61.6 us
    pallas_call x4, Pallas kernels, feed_grads(): pl.pallas_call(feed_grads_kernel, name='feed_grads', grid_spec=pltpu.Pref...  52.8 us
    ppermute x29, starting transfers between devices, send(): return lax.ppermute(value, 'section', routes)  46.7 us
    convert_element_type x17, other arithmetic, plus(): return sum((value.astype(F32) for value in values)).astype(BF)  38.9 us
    pallas_call x4, Pallas kernels, attend_grads(): pl.pallas_call(attend_grads_kernel, name='attend_grads', grid_spec=pltpu....  35.7 us
  transfers between devices with their start and end apart: 57, of which 19 were waited for; matrix products, arithmetic and copies ran while one was open for 7% of the time, Pallas kernels for 20%

profile of v4, /device:TPU:13, one launch (start us, length us, event | category | flops | bytes accessed | tf_op | source)
XLA Modules:
  0.0 964.5 jit_solution(16979587062856829617)
XLA Ops:
  17.4 8.3 collective-permute-done.2
  33.4 54.6 %layer_forward.8 = (bf16[3,1024,768]{2,1,0:T(8,128)(2,1)}, bf16[1024,768]{1,0:T(8,128)(2,1)}, f32[48,256]{1,0:T(8,128)}, bf16[1024,768]{1,0:T(8,128)(2,1)}, bf16...) custom-call(s32[8]{0:T(128)S(1)} %get-tuple-element.598.begin_ref, ...), custom_call_target="tpu_custom_call" | custom-call | flops 48000000000 | bytes 1024 | tf_op jit(solution)/shard_map/layer_forward/pallas_call | solution.py:659
  88.0 54.9 %layer_forward.9 = (bf16[3,1024,768]{2,1,0:T(8,128)(2,1)}, bf16[1024,768]{1,0:T(8,128)(2,1)}, f32[48,256]{1,0:T(8,128)}, bf16[1024,768]{1,0:T(8,128)(2,1)}, bf16...) custom-call(s32[8]{0:T(128)S(1)} %get-tuple-element.598.begin_ref, ...), custom_call_target="tpu_custom_call" | custom-call | flops 48000000000 | bytes 1024 | tf_op jit(solution)/shard_map/layer_forward/pallas_call | solution.py:659
  148.9 12.7 %collective-permute-done.9 = bf16[32,1792]{1,0:T(8,128)(2,1)S(1)} collective-permute-done((bf16[32,1792]{1,0:T(8,128)(2,1)S(1)}, bf16[32,1792]{1,0:T(8,128)(2,1)S(1)}, u32[]{:S(2)}, u32[]{:S(2)}) %collective-permute-start.9) | collective-permute-done | bytes 114720 | tf_op jit(solution)/shard_map/ppermute | solution.py:816
  161.5 13.5 %collective-permute-done.10 = bf16[32,1792]{1,0:T(8,128)(2,1)S(1)} collective-permute-done((bf16[32,1792]{1,0:T(8,128)(2,1)S(1)}, bf16[32,1792]{1,0:T(8,128)(2,1)S(1)}, u32[]{:S(2)}, u32[]{:S(2)}) %collective-permute-start.10) | collective-permute-done | bytes 114720 | tf_op jit(solution)/shard_map/ppermute | solution.py:816
  175.2 255.7 %conditional.1 = (bf16[1024,768]{1,0:T(8,128)(2,1)}, bf16[3,1024,768]{2,1,0:T(8,128)(2,1)}, bf16[1024,768]{1,0:T(8,128)(2,1)}, f32[48,256]{1,0:T(8,128)}, bf16[1...) conditional(s32[]{:T(128)} %convert_element_type.357, ...), branch_computations={%region_3.4_spmd, %region_4.5_spmd} | conditional | flops 226000011264 | bytes 45096532 | solution.py:977
  175.2 54.8 %layer_forward.6 = (bf16[3,1024,768]{2,1,0:T(8,128)(2,1)}, bf16[1024,768]{1,0:T(8,128)(2,1)}, f32[48,256]{1,0:T(8,128)}, bf16[1024,768]{1,0:T(8,128)(2,1)}, bf16...) custom-call(s32[8]{0:T(128)S(1)} %get-tuple-element.185.begin_ref, ...), custom_call_target="tpu_custom_call" | custom-call | flops 48000000000 | bytes 1024 | tf_op jit(solution)/shard_map/cond/branch_1_fun/layer_forward/pallas_call | solution.py:659
  230.0 55.3 %layer_forward.7 = (bf16[3,1024,768]{2,1,0:T(8,128)(2,1)}, bf16[1024,768]{1,0:T(8,128)(2,1)}, f32[48,256]{1,0:T(8,128)S(1)}, bf16[1024,768]{1,0:T(8,128)(2,1)S(1...) custom-call(s32[8]{0:T(128)S(1)} %get-tuple-element.185.begin_ref, ...), custom_call_target="tpu_custom_call" | custom-call | flops 48000000000 | bytes 1024 | tf_op jit(solution)/shard_map/cond/branch_1_fun/layer_forward/pallas_call | solution.py:659
  288.0 24.1 %refine_back.6 = (bf16[1024,768]{1,0:T(8,128)(2,1)}, bf16[1024,3072]{1,0:T(8,128)(2,1)}, bf16[1024,768]{1,0:T(8,128)(2,1)S(1)}, bf16[1024,768]{1,0:T(8,128)(2,1)}, f32[6,768]{1,0:T(8,128)}, /*index=5*/f32[1,3072]{1,0:T(1,128)}) custom-call(s32[3]{0:T(128)S(1)} %get-tuple-element.187.sel_ref, bf16[1024,768]{1,0:T(8,128)(2,1)} %get-tuple-element.219.grad_ref, ...), custom_call_target="tpu_custom_call" | custom-call | flops 24000000000 | bytes 1024 | tf_op jit(solution)/shard_map/cond/branch_1_fun/refine_back/pallas_call | solution.py:353
  312.1 46.5 %mixed_backward.6 = (bf16[3,1024,768]{2,1,0:T(8,128)(2,1)}, bf16[1024,768]{1,0:T(8,128)(2,1)}, f32[2,768]{1,0:T(2,128)}) custom-call(s32[8]{0:T(128)S(1)} %get-tuple-element.185.begin_ref, s32[8]{0:T(128)S(1)} %get-tuple-element.186.count_ref, s32[3]{0:T(128)S(1)} %get-tuple-element.187.sel_ref, bf16[3,1024,768]{2,1,0:T(8,128)(2,1)} %get-tuple-element.712.qkv_hbm, ...), custom_call_target="tpu_custom_call" | custom-call | flops 38000001024 | bytes 1024 | tf_op jit(solution)/shard_map/cond/branch_1_fun/mixed_backward/pallas_call | solution.py:768
  358.6 24.3 %refine_back.7 = (bf16[1024,768]{1,0:T(8,128)(2,1)}, bf16[1024,3072]{1,0:T(8,128)(2,1)}, bf16[1024,768]{1,0:T(8,128)(2,1)}, bf16[1024,768]{1,0:T(8,128)(2,1)}, f32[6,768]{1,0:T(8,128)}, /*index=5*/f32[1,3072]{1,0:T(1,128)}) custom-call(s32[3]{0:T(128)S(1)} %get-tuple-element.187.sel_ref, bf16[1024,768]{1,0:T(8,128)(2,1)} %get-tuple-element.222.grad_ref, ...), custom_call_target="tpu_custom_call" | custom-call | flops 24000000000 | bytes 1024 | tf_op jit(solution)/shard_map/cond/branch_1_fun/refine_back/pallas_call | solution.py:353
  383.0 45.8 %mixed_backward.7 = (bf16[3,1024,768]{2,1,0:T(8,128)(2,1)}, bf16[1024,768]{1,0:T(8,128)(2,1)}, f32[2,768]{1,0:T(2,128)}) custom-call(s32[8]{0:T(128)S(1)} %get-tuple-element.185.begin_ref, s32[8]{0:T(128)S(1)} %get-tuple-element.186.count_ref, s32[3]{0:T(128)S(1)} %get-tuple-element.187.sel_ref, bf16[3,1024,768]{2,1,0:T(8,128)(2,1)} %get-tuple-element.703.qkv_hbm, ...), custom_call_target="tpu_custom_call" | custom-call | flops 38000001024 | bytes 1024 | tf_op jit(solution)/shard_map/cond/branch_1_fun/mixed_backward/pallas_call | solution.py:768
  432.9 17.0 %collective-permute-done.15.grad_ref = bf16[1024,768]{1,0:T(8,128)(2,1)S(1)} collective-permute-done((bf16[1024,768]{1,0:T(8,128)(2,1)}, bf16[1024,768]{1,0:T(8,128)(2,1)S(1)}, u32[]{:S(2)}, u32[]{:S(2)}) %collective-permute-start.15) | collective-permute-done | bytes 1572896 | tf_op jit(solution)/shard_map/ppermute | solution.py:816
  451.0 24.3 %refine_back.8 = (bf16[1024,768]{1,0:T(8,128)(2,1)}, bf16[1024,3072]{1,0:T(8,128)(2,1)}, bf16[1024,768]{1,0:T(8,128)(2,1)}, bf16[1024,768]{1,0:T(8,128)(2,1)}, f32[6,768]{1,0:T(8,128)}, /*index=5*/f32[1,3072]{1,0:T(1,128)}) custom-call(s32[3]{0:T(128)S(1)} %pad_add_fusion.sel_ref, bf16[1024,768]{1,0:T(8,128)(2,1)} %copy-done.30, ...), custom_call_target="tpu_custom_call" | custom-call | flops 24000000000 | bytes 1024 | tf_op jit(solution)/shard_map/refine_back/pallas_call | solution.py:353
  475.3 13.2 %feed_grads.5 = bf16[8,768,384]{2,1,0:T(8,128)(2,1)} custom-call(s32[3]{0:T(128)} %pad_add_fusion.2.sel_ref, bf16[1024,768]{1,0:T(8,128)(2,1)S(1)} %copy-done.33, bf16[1024,3072]{1,0:T(8,128)(2,1)} %get-tuple-element.438.raised_late_ref, bf16[1024,3072]{1,0:T(8,128)(2,1)} %get-tuple-element.439.raised_ref, bf16[1024,3072]{1,0:T(8,128)(2,1)} %get-tuple-element.440.active_ref, ...), custom_call_target="tpu_custom_call" | custom-call | flops 12000000000 | bytes 1024 | tf_op jit(solution)/shard_map/feed_grads/pallas_call | solution.py:460
  488.5 13.2 %feed_grads.4 = bf16[8,768,384]{2,1,0:T(8,128)(2,1)} custom-call(s32[3]{0:T(128)S(1)} %pad_add_fusion.sel_ref, bf16[1024,768]{1,0:T(8,128)(2,1)S(1)} %copy-done.33, bf16[1024,3072]{1,0:T(8,128)(2,1)} %get-tuple-element.438.raised_late_ref, bf16[1024,3072]{1,0:T(8,128)(2,1)} %get-tuple-element.439.raised_ref, ...), custom_call_target="tpu_custom_call" | custom-call | flops 12000000000 | bytes 1024 | tf_op jit(solution)/shard_map/feed_grads/pallas_call | solution.py:460
  508.9 46.2 %mixed_backward.8 = (bf16[3,1024,768]{2,1,0:T(8,128)(2,1)}, bf16[1024,768]{1,0:T(8,128)(2,1)}, f32[2,768]{1,0:T(2,128)}) custom-call(s32[8]{0:T(128)S(1)} %get-tuple-element.598.begin_ref, s32[8]{0:T(128)S(1)} %get-tuple-element.599.count_ref, s32[3]{0:T(128)S(1)} %pad_add_fusion.sel_ref, bf16[3,1024,768]{2,1,0:T(8,128)(2,1)} %get-tuple-element.428.qkv_hbm, ...), custom_call_target="tpu_custom_call" | custom-call | flops 38000001024 | bytes 1024 | tf_op jit(solution)/shard_map/mixed_backward/pallas_call | solution.py:768
  555.1 6.1 collective-permute-done.17
  571.5 9.1 attend_grads.4
  580.9 22.8 %collective-permute-done.19 = bf16[768,384]{1,0:T(8,128)(2,1)} collective-permute-done((bf16[768,384]{1,0:T(8,128)(2,1)}, bf16[768,384]{1,0:T(8,128)(2,1)}, u32[]{:S(2)}, u32[]{:S(2)}) %collective-permute-start.19) | collective-permute-done | bytes 589856 | tf_op jit(solution)/shard_map/ppermute | solution.py:860
  605.2 8.8 attend_grads.5
  627.2 24.4 %refine_back.9 = (bf16[1024,768]{1,0:T(8,128)(2,1)}, bf16[1024,3072]{1,0:T(8,128)(2,1)}, bf16[1024,768]{1,0:T(8,128)(2,1)}, bf16[1024,768]{1,0:T(8,128)(2,1)}, f32[6,768]{1,0:T(8,128)}, /*index=5*/f32[1,3072]{1,0:T(1,128)}) custom-call(s32[3]{0:T(128)S(1)} %copy-done.39, bf16[1024,768]{1,0:T(8,128)(2,1)} %get-tuple-element.468.grad_ref, ...), custom_call_target="tpu_custom_call" | custom-call | flops 24000000000 | bytes 1024 | tf_op jit(solution)/shard_map/refine_back/pallas_call | solution.py:353
  662.3 13.4 %feed_grads.6 = bf16[8,768,384]{2,1,0:T(8,128)(2,1)} custom-call(s32[3]{0:T(128)} %pad_add_fusion.2.sel_ref, bf16[1024,768]{1,0:T(8,128)(2,1)} %get-tuple-element.492.hidden_ref, bf16[1024,3072]{1,0:T(8,128)(2,1)} %get-tuple-element.493.raised_late_ref, bf16[1024,3072]{1,0:T(8,128)(2,1)} %get-tuple-element.494.raised_ref, ...), custom_call_target="tpu_custom_call" | custom-call | flops 12000000000 | bytes 1024 | tf_op jit(solution)/shard_map/feed_grads/pallas_call | solution.py:460
  690.0 13.0 %feed_grads.7 = bf16[8,768,384]{2,1,0:T(8,128)(2,1)} custom-call(s32[3]{0:T(128)S(1)} %copy-done.39, bf16[1024,768]{1,0:T(8,128)(2,1)} %get-tuple-element.492.hidden_ref, bf16[1024,3072]{1,0:T(8,128)(2,1)} %get-tuple-element.493.raised_late_ref, bf16[1024,3072]{1,0:T(8,128)(2,1)} %get-tuple-element.494.raised_ref, ...), custom_call_target="tpu_custom_call" | custom-call | flops 12000000000 | bytes 1024 | tf_op jit(solution)/shard_map/feed_grads/pallas_call | solution.py:460
  715.2 9.3 collective-permute-start.33
  726.0 47.1 %mixed_backward.9 = (bf16[3,1024,768]{2,1,0:T(8,128)(2,1)}, bf16[1024,768]{1,0:T(8,128)(2,1)}, f32[2,768]{1,0:T(2,128)}) custom-call(s32[8]{0:T(128)S(1)} %get-tuple-element.598.begin_ref, s32[8]{0:T(128)S(1)} %get-tuple-element.599.count_ref, s32[3]{0:T(128)S(1)} %copy-done.39, bf16[3,1024,768]{2,1,0:T(8,128)(2,1)} %get-tuple-element.425.qkv_hbm, ...), custom_call_target="tpu_custom_call" | custom-call | flops 38000001024 | bytes 1024 | tf_op jit(solution)/shard_map/mixed_backward/pallas_call | solution.py:768
  790.6 8.9 attend_grads.6
  840.6 8.9 attend_grads.7
  883.3 28.6 %collective-permute-done.44 = bf16[4,432,384]{2,1,0:T(8,128)(2,1)S(1)} collective-permute-done((bf16[4,432,384]{2,1,0:T(8,128)(2,1)S(1)}, bf16[4,432,384]{2,1,0:T(8,128)(2,1)S(1)}, u32[]{:S(2)}, u32[]{:S(2)}) %collective-permute-start.44) | collective-permute-done | bytes 1327136 | tf_op jit(solution)/shard_map/ppermute | solution.py:846
  915.1 7.4 collective-permute-start.47
  936.8 7.1 collective-permute-done.49
  943.9 6.2 collective-permute-done.50
  (317 shorter events, 232.0 us)
Async XLA Ops:
  9.6 21.6 %collective-permute-start.5 = (bf16[768,3072]{1,0:T(8,128)(2,1)}, bf16[768,3072]{1,0:T(8,128)(2,1)}, u32[]{:S(2)}, u32[]{:S(2)}) collective-permute-start(bf16[768,3072]{1,0:T(8,128)(2,1)} %bitcast.241), channel_id=1, source_target_pairs={{0,8},{8,0},{16,24},{24,16},{1,9},{9,1},{17,25},{25,17},{2,10},{10... | collective-permute-start | bytes 14155784 | tf_op jit(solution)/shard_map/ppermute | solution.py:816
  9.7 21.7 %collective-permute-start.6 = (bf16[3072,768]{1,0:T(8,128)(2,1)}, bf16[3072,768]{1,0:T(8,128)(2,1)}, u32[]{:S(2)}, u32[]{:S(2)}) collective-permute-start(bf16[3072,768]{1,0:T(8,128)(2,1)} %bitcast.247), channel_id=1, source_target_pairs={{0,8},{8,0},{16,24},{24,16},{1,9},{9,1},{17,25},{25,17},{2,10},{10... | collective-permute-start | bytes 14155784 | tf_op jit(solution)/shard_map/ppermute | solution.py:816
  12.2 19.0 %collective-permute-start.3 = (bf16[768,2304]{1,0:T(8,128)(2,1)}, bf16[768,2304]{1,0:T(8,128)(2,1)S(1)}, u32[]{:S(2)}, u32[]{:S(2)}) collective-permute-start(bf16[768,2304]{1,0:T(8,128)(2,1)} %bitcast.253), channel_id=1, source_target_pairs={{0,8},{8,0},{16,24},{24,16},{1,9},{9,1},{17,25},{25,17},{2,10},{10... | collective-permute-start | bytes 10616840 | tf_op jit(solution)/shard_map/ppermute | solution.py:816
  12.4 18.8 %collective-permute-start.4 = (bf16[768,768]{1,0:T(8,128)(2,1)}, bf16[768,768]{1,0:T(8,128)(2,1)S(1)}, u32[]{:S(2)}, u32[]{:S(2)}) collective-permute-start(bf16[768,768]{1,0:T(8,128)(2,1)} %bitcast.259), channel_id=1, source_target_pairs={{0,8},{8,0},{16,24},{24,16},{1,9},{9,1},{17,25},{25,17},{2,10},{10... | collective-permute-start | bytes 3538952 | tf_op jit(solution)/shard_map/ppermute | solution.py:816
  142.9 32.2 %collective-permute-start.8 = (bf16[1024,768]{1,0:T(8,128)(2,1)}, bf16[1024,768]{1,0:T(8,128)(2,1)S(1)}, u32[]{:S(2)}, u32[]{:S(2)}) collective-permute-start(bf16[1024,768]{1,0:T(8,128)(2,1)} %get-tuple-element.416), channel_id=1, source_target_pairs={{0,16},{8,24},{1,17},{9,25},{2,18},{10,26},{3,19},{11,27},{4,20},{... | collective-permute-start | bytes 4718600 | tf_op jit(solution)/shard_map/ppermute | solution.py:816
  147.6 27.5 %collective-permute-start.10 = (bf16[32,1792]{1,0:T(8,128)(2,1)S(1)}, bf16[32,1792]{1,0:T(8,128)(2,1)S(1)}, u32[]{:S(2)}, u32[]{:S(2)}) collective-permute-start(bf16[32,1792]{1,0:T(8,128)(2,1)S(1)} %get-tuple-element.652), channel_id=1, source_target_pairs={{0,16},{8,24},{1,17},{9,25},{2,18},{10,26},{3,19},{11,27},{4,20},{... | collective-permute-start | bytes 344072 | tf_op jit(solution)/shard_map/ppermute | solution.py:816
  430.9 19.0 %collective-permute-start.15 = (bf16[1024,768]{1,0:T(8,128)(2,1)}, bf16[1024,768]{1,0:T(8,128)(2,1)S(1)}, u32[]{:S(2)}, u32[]{:S(2)}) collective-permute-start(bf16[1024,768]{1,0:T(8,128)(2,1)} %get-tuple-element.431), channel_id=1, source_target_pairs={{16,0},{24,8},{17,1},{25,9},{18,2},{26,10},{19,3},{27,11},{20,4},{... | collective-permute-start | bytes 4718600 | tf_op jit(solution)/shard_map/ppermute | solution.py:816
  508.8 52.3 %collective-permute-start.17 = (bf16[4,768,384]{2,1,0:T(8,128)(2,1)S(1)}, bf16[4,768,384]{2,1,0:T(8,128)(2,1)}, u32[]{:S(2)}, u32[]{:S(2)}) collective-permute-start(bf16[4,768,384]{2,1,0:T(8,128)(2,1)S(1)} %dynamic-slice_bitcast_fusion.1), channel_id=1, source_target_pairs={{0,1},{1,0},{2,3},{3,2},{4,5},{5,4},{6,7},{7,6},{8,9},{9,8},{10,11... | collective-permute-start | bytes 7077896 | tf_op jit(solution)/shard_map/ppermute | solution.py:846
  567.2 36.5 %collective-permute-start.19 = (bf16[768,384]{1,0:T(8,128)(2,1)}, bf16[768,384]{1,0:T(8,128)(2,1)}, u32[]{:S(2)}, u32[]{:S(2)}) collective-permute-start(bf16[768,384]{1,0:T(8,128)(2,1)} %get-tuple-element.616), channel_id=1, source_target_pairs={{2,0},{3,1},{4,2},{5,3},{6,4},{7,5},{10,8},{11,9},{12,10},{13,11},... | collective-permute-start | bytes 1769480 | tf_op jit(solution)/shard_map/ppermute | solution.py:860
  617.1 34.5 %collective-permute-start.23 = (bf16[4,384,384]{2,1,0:T(8,128)(2,1)S(1)}, bf16[4,384,384]{2,1,0:T(8,128)(2,1)}, u32[]{:S(2)}, u32[]{:S(2)}) collective-permute-start(bf16[4,384,384]{2,1,0:T(8,128)(2,1)S(1)} %dynamic-slice_bitcast_fusion.3), channel_id=1, source_target_pairs={{0,1},{1,0},{2,3},{3,2},{4,5},{5,4},{6,7},{7,6},{8,9},{9,8},{10,11... | collective-permute-start | bytes 3538952 | tf_op jit(solution)/shard_map/ppermute | solution.py:846
  621.1 32.5 %collective-permute-start.21 = (bf16[768,384]{1,0:T(8,128)(2,1)}, bf16[768,384]{1,0:T(8,128)(2,1)}, u32[]{:S(2)}, u32[]{:S(2)}) collective-permute-start(bf16[768,384]{1,0:T(8,128)(2,1)} %get-tuple-element.615), channel_id=1, source_target_pairs={{0,2},{1,3},{2,4},{3,5},{4,6},{5,7},{8,10},{9,11},{10,12},{11,13},... | collective-permute-start | bytes 1769480 | tf_op jit(solution)/shard_map/ppermute | solution.py:859
  624.4 29.2 %collective-permute-start.22 = (bf16[768,384]{1,0:T(8,128)(2,1)}, bf16[768,384]{1,0:T(8,128)(2,1)}, u32[]{:S(2)}, u32[]{:S(2)}) collective-permute-start(bf16[768,384]{1,0:T(8,128)(2,1)} %get-tuple-element.614), channel_id=1, source_target_pairs={{2,0},{3,1},{4,2},{5,3},{6,4},{7,5},{10,8},{11,9},{12,10},{13,11},... | collective-permute-start | bytes 1769480 | tf_op jit(solution)/shard_map/ppermute | solution.py:860
  656.2 19.5 %collective-permute-start.24 = (bf16[768,384]{1,0:T(8,128)(2,1)}, bf16[768,384]{1,0:T(8,128)(2,1)}, u32[]{:S(2)}, u32[]{:S(2)}) collective-permute-start(bf16[768,384]{1,0:T(8,128)(2,1)} %get-tuple-element.613), channel_id=1, source_target_pairs={{0,2},{1,3},{2,4},{3,5},{4,6},{5,7},{8,10},{9,11},{10,12},{11,13},... | collective-permute-start | bytes 1769480 | tf_op jit(solution)/shard_map/ppermute | solution.py:859
  658.7 17.0 %collective-permute-start.25 = (bf16[768,384]{1,0:T(8,128)(2,1)}, bf16[768,384]{1,0:T(8,128)(2,1)}, u32[]{:S(2)}, u32[]{:S(2)}) collective-permute-start(bf16[768,384]{1,0:T(8,128)(2,1)} %get-tuple-element.612), channel_id=1, source_target_pairs={{2,0},{3,1},{4,2},{5,3},{6,4},{7,5},{10,8},{11,9},{12,10},{13,11},... | collective-permute-start | bytes 1769480 | tf_op jit(solution)/shard_map/ppermute | solution.py:860
  675.7 27.3 %collective-permute-start.26 = (bf16[8,768,384]{2,1,0:T(8,128)(2,1)}, bf16[8,768,384]{2,1,0:T(8,128)(2,1)}, u32[]{:S(2)}, u32[]{:S(2)}) collective-permute-start(bf16[8,768,384]{2,1,0:T(8,128)(2,1)} %feed_grads.6), channel_id=1, source_target_pairs={{0,8},{8,0},{16,24},{24,16},{1,9},{9,1},{17,25},{25,17},{2,10},{10... | collective-permute-start | bytes 14155784 | tf_op jit(solution)/shard_map/ppermute | solution.py:816
  710.9 64.2 %collective-permute-start.30 = (bf16[4,768,384]{2,1,0:T(8,128)(2,1)}, bf16[4,768,384]{2,1,0:T(8,128)(2,1)}, u32[]{:S(2)}, u32[]{:S(2)}) collective-permute-start(bf16[4,768,384]{2,1,0:T(8,128)(2,1)} %dynamic-slice_bitcast_fusion), channel_id=1, source_target_pairs={{0,1},{1,0},{2,3},{3,2},{4,5},{5,4},{6,7},{7,6},{8,9},{9,8},{10,11... | collective-permute-start | bytes 7077896 | tf_op jit(solution)/shard_map/ppermute | solution.py:846
  712.5 60.7 %collective-permute-start.31 = (bf16[384,384]{1,0:T(8,128)(2,1)}, bf16[384,384]{1,0:T(8,128)(2,1)}, u32[]{:S(2)}, u32[]{:S(2)}) collective-permute-start(bf16[384,384]{1,0:T(8,128)(2,1)} %get-tuple-element.634), channel_id=1, source_target_pairs={{0,6},{1,7},{8,14},{9,15},{16,22},{17,23},{24,30},{25,31}} | collective-permute-start | bytes 884744 | tf_op jit(solution)/shard_map/ppermute | solution.py:871
  713.8 67.6 %collective-permute-start.32 = (bf16[384,384]{1,0:T(8,128)(2,1)}, bf16[384,384]{1,0:T(8,128)(2,1)}, u32[]{:S(2)}, u32[]{:S(2)}) collective-permute-start(bf16[384,384]{1,0:T(8,128)(2,1)} %get-tuple-element.633), channel_id=1, source_target_pairs={{6,0},{7,1},{14,8},{15,9},{22,16},{23,17},{30,24},{31,25}} | collective-permute-start | bytes 884744 | tf_op jit(solution)/shard_map/ppermute | solution.py:871
  715.2 66.3 %collective-permute-start.33 = (bf16[384,384]{1,0:T(8,128)(2,1)}, bf16[384,384]{1,0:T(8,128)(2,1)}, u32[]{:S(2)}, u32[]{:S(2)}) collective-permute-start(bf16[384,384]{1,0:T(8,128)(2,1)} %get-tuple-element.632), channel_id=1, source_target_pairs={{0,4},{1,5},{2,6},{3,7},{8,12},{9,13},{10,14},{11,15},{16,20},{17,... | collective-permute-start | bytes 884744 | tf_op jit(solution)/shard_map/ppermute | solution.py:871
  724.5 56.9 %collective-permute-start.34 = (bf16[384,384]{1,0:T(8,128)(2,1)}, bf16[384,384]{1,0:T(8,128)(2,1)}, u32[]{:S(2)}, u32[]{:S(2)}) collective-permute-start(bf16[384,384]{1,0:T(8,128)(2,1)} %get-tuple-element.631), channel_id=1, source_target_pairs={{4,0},{5,1},{6,2},{7,3},{12,8},{13,9},{14,10},{15,11},{20,16},{21,... | collective-permute-start | bytes 884744 | tf_op jit(solution)/shard_map/ppermute | solution.py:871
  800.0 49.5 %collective-permute-start.40 = (bf16[8,384,384]{2,1,0:T(8,128)(2,1)}, bf16[8,384,384]{2,1,0:T(8,128)(2,1)}, u32[]{:S(2)}, u32[]{:S(2)}) collective-permute-start(bf16[8,384,384]{2,1,0:T(8,128)(2,1)} %attend_grads.6), channel_id=1, source_target_pairs={{0,8},{8,0},{16,24},{24,16},{1,9},{9,1},{17,25},{25,17},{2,10},{10... | collective-permute-start | bytes 7077896 | tf_op jit(solution)/shard_map/ppermute | solution.py:816
  827.8 30.6 %collective-permute-start.43 = (bf16[8,48,384]{2,1,0:T(8,128)(2,1)}, bf16[8,48,384]{2,1,0:T(8,128)(2,1)}, u32[]{:S(2)}, u32[]{:S(2)}) collective-permute-start(bf16[8,48,384]{2,1,0:T(8,128)(2,1)} %bitcast.222), channel_id=1, source_target_pairs={{0,8},{8,0},{16,24},{24,16},{1,9},{9,1},{17,25},{25,17},{2,10},{10... | collective-permute-start | bytes 884744 | tf_op jit(solution)/shard_map/ppermute | solution.py:816
  830.1 32.8 %collective-permute-start.27 = (bf16[256,768]{1,0:T(8,128)(2,1)}, bf16[256,768]{1,0:T(8,128)(2,1)}, u32[]{:S(2)}, u32[]{:S(2)}) collective-permute-start(bf16[256,768]{1,0:T(8,128)(2,1)} %get-tuple-element.620), channel_id=1, source_target_pairs={{0,24},{8,16},{1,25},{9,17},{2,26},{10,18},{3,27},{11,19},{4,28},{... | collective-permute-start | bytes 1179656 | tf_op jit(solution)/shard_map/ppermute | solution.py:816
  834.1 19.3 %collective-permute-start.41 = (bf16[768,384]{1,0:T(8,128)(2,1)}, bf16[768,384]{1,0:T(8,128)(2,1)}, u32[]{:S(2)}, u32[]{:S(2)}) collective-permute-start(bf16[768,384]{1,0:T(8,128)(2,1)} %get-tuple-element.609), channel_id=1, source_target_pairs={{0,2},{1,3},{2,4},{3,5},{4,6},{5,7},{8,10},{9,11},{10,12},{11,13},... | collective-permute-start | bytes 1769480 | tf_op jit(solution)/shard_map/ppermute | solution.py:859
  836.0 18.8 %collective-permute-start.42 = (bf16[768,384]{1,0:T(8,128)(2,1)}, bf16[768,384]{1,0:T(8,128)(2,1)}, u32[]{:S(2)}, u32[]{:S(2)}) collective-permute-start(bf16[768,384]{1,0:T(8,128)(2,1)} %get-tuple-element.608), channel_id=1, source_target_pairs={{2,0},{3,1},{4,2},{5,3},{6,4},{7,5},{10,8},{11,9},{12,10},{13,11},... | collective-permute-start | bytes 1769480 | tf_op jit(solution)/shard_map/ppermute | solution.py:860
  856.5 16.8 %collective-permute-start.53 = (bf16[768,384]{1,0:T(8,128)(2,1)S(1)}, bf16[768,384]{1,0:T(8,128)(2,1)S(1)}, u32[]{:S(2)}, u32[]{:S(2)}) collective-permute-start(bf16[768,384]{1,0:T(8,128)(2,1)S(1)} %get-tuple-element.606), channel_id=1, source_target_pairs={{0,2},{1,3},{2,4},{3,5},{4,6},{5,7},{8,10},{9,11},{10,12},{11,13},... | collective-permute-start | bytes 1769480 | tf_op jit(solution)/shard_map/ppermute | solution.py:859
  862.9 20.1 %collective-permute-start.52 = (bf16[768,384]{1,0:T(8,128)(2,1)S(1)}, bf16[768,384]{1,0:T(8,128)(2,1)S(1)}, u32[]{:S(2)}, u32[]{:S(2)}) collective-permute-start(bf16[768,384]{1,0:T(8,128)(2,1)S(1)} %copy-done.7), channel_id=1, source_target_pairs={{0,8},{16,24},{1,9},{17,25},{2,10},{18,26},{3,11},{19,27},{4,12},{... | collective-permute-start | bytes 1769480 | tf_op jit(solution)/shard_map/ppermute | solution.py:816
  880.3 31.7 %collective-permute-start.44 = (bf16[4,432,384]{2,1,0:T(8,128)(2,1)S(1)}, bf16[4,432,384]{2,1,0:T(8,128)(2,1)S(1)}, u32[]{:S(2)}, u32[]{:S(2)}) collective-permute-start(bf16[4,432,384]{2,1,0:T(8,128)(2,1)S(1)} %dynamic-slice_bitcast_fusion.2), channel_id=1, source_target_pairs={{0,1},{1,0},{2,3},{3,2},{4,5},{5,4},{6,7},{7,6},{8,9},{9,8},{10,11... | collective-permute-start | bytes 3981320 | tf_op jit(solution)/shard_map/ppermute | solution.py:846
  915.1 21.8 %collective-permute-start.47 = (bf16[432,384]{1,0:T(8,128)(2,1)S(1)}, bf16[432,384]{1,0:T(8,128)(2,1)S(1)}, u32[]{:S(2)}, u32[]{:S(2)}) collective-permute-start(bf16[432,384]{1,0:T(8,128)(2,1)S(1)} %get-tuple-element.625), channel_id=1, source_target_pairs={{0,4},{1,5},{2,6},{3,7},{8,12},{9,13},{10,14},{11,15},{16,20},{17,... | collective-permute-start | bytes 995336 | tf_op jit(solution)/shard_map/ppermute | solution.py:871
  923.8 20.2 %collective-permute-start.49 = (bf16[432,384]{1,0:T(8,128)(2,1)S(1)}, bf16[432,384]{1,0:T(8,128)(2,1)S(1)}, u32[]{:S(2)}, u32[]{:S(2)}) collective-permute-start(bf16[432,384]{1,0:T(8,128)(2,1)S(1)} %get-tuple-element.623), channel_id=1, source_target_pairs={{0,2},{1,3},{2,4},{3,5},{4,6},{5,7},{8,10},{9,11},{10,12},{11,13},... | collective-permute-start | bytes 995336 | tf_op jit(solution)/shard_map/ppermute | solution.py:871
  925.7 24.4 %collective-permute-start.50 = (bf16[432,384]{1,0:T(8,128)(2,1)S(1)}, bf16[432,384]{1,0:T(8,128)(2,1)S(1)}, u32[]{:S(2)}, u32[]{:S(2)}) collective-permute-start(bf16[432,384]{1,0:T(8,128)(2,1)S(1)} %get-tuple-element.622), channel_id=1, source_target_pairs={{2,0},{3,1},{4,2},{5,3},{6,4},{7,5},{10,8},{11,9},{12,10},{13,11},... | collective-permute-start | bytes 995336 | tf_op jit(solution)/shard_map/ppermute | solution.py:871
  930.2 31.9 %collective-permute-start.37 = (bf16[384,384]{1,0:T(8,128)(2,1)S(1)}, bf16[384,384]{1,0:T(8,128)(2,1)S(1)}, u32[]{:S(2)}, u32[]{:S(2)}) collective-permute-start(bf16[384,384]{1,0:T(8,128)(2,1)S(1)} %fusion.27), channel_id=1, source_target_pairs={{0,8},{16,24},{1,9},{17,25},{2,10},{18,26},{3,11},{19,27},{4,12},{... | collective-permute-start | bytes 884744 | tf_op jit(solution)/shard_map/ppermute | solution.py:816
  (66 other events, 2047.9 us)
